TPU v7x, 32 devices: a whole 2x2x4 slice. The times are simulated.
32 devices in a mesh: row: 4 (over x, core), col: 8 (over z, y).
Axes of the slice: x: 2, y: 2, z: 4, core: 2. Of those that a mesh axis runs over, the one named last changes fastest.
Arguments:
- tokens: bfloat16 [512, 6144], P('row', 'col'), may hold values from -6 to 6
- weight_in: bfloat16 [6144, 24576], P('row', 'col'), may hold values from -0.109375 to 0.109375
- weight_out: bfloat16 [24576, 6144], P('col', 'row'), may hold values from -0.0546875 to 0.0546875
- out_grad: bfloat16 [512, 6144], P('row', 'col'), may hold values from -1.5 to 1.5
Outputs:
- block_out: bfloat16 [512, 6144], P('row', 'col')
- grad_tokens: bfloat16 [512, 6144], P('row', 'col')
- grad_in: bfloat16 [6144, 24576], P('row', 'col')
- grad_out: bfloat16 [24576, 6144], P('col', 'row')
All inputs are finite; a program needn't handle non-finite values.
Results may differ from a plain program's by a relative error of at most 0.0051.
Values may be sent and summed in bfloat16 or wider, within the bound.
No kernel may reach another device: no remote copies, remote signals or barrier semaphores. Data moves between devices by JAX's collectives and lax.ppermute only.
A program may use at most 256 MiB of HBM per device.

v0:
```python
import jax
import jax.numpy as jnp
from jax import lax
from jax.sharding import PartitionSpec as P


def cdf_of(value):
    return 0.5 * (1.0 + lax.erf(value * 0.7071067811865476))


def contract(left, right, left_dim, right_dim):
    return lax.dot_general(
        left, right, (((left_dim,), (right_dim,)), ((), ())), preferred_element_type=jnp.float32
    )


def body(tokens, weight_in, weight_out, out_grad):
    tok_panel, grad_panel = (
        lax.all_gather(tokens, "col", axis=1, tiled=True),
        lax.all_gather(out_grad, "col", axis=1, tiled=True),
    )
    in_panel, out_panel = (
        lax.all_gather(weight_in, "row", axis=0, tiled=True),
        lax.all_gather(weight_out, "row", axis=1, tiled=True),
    )
    hidden_pre = jnp.dot(tok_panel, in_panel, preferred_element_type=jnp.float32)
    cumul = cdf_of(hidden_pre)
    act = (hidden_pre * cumul).astype(jnp.bfloat16)
    out_terms = jnp.dot(act, out_panel, preferred_element_type=jnp.float32)
    grad_act = contract(grad_panel, out_panel, 1, 1)
    density = jnp.exp(-0.5 * hidden_pre * hidden_pre) * 0.3989422804014327
    grad_pre = (grad_act * (cumul + hidden_pre * density)).astype(jnp.bfloat16)
    back_terms = contract(grad_pre, in_panel, 1, 1)
    block_out, grad_tokens = (
        lax.psum_scatter(out_terms, "col", scatter_dimension=1, tiled=True),
        lax.psum_scatter(back_terms, "col", scatter_dimension=1, tiled=True),
    )
    all_tok, all_grad = (
        lax.all_to_all(tok_panel, "row", split_axis=1, concat_axis=0, tiled=True),
        lax.all_to_all(grad_panel, "row", split_axis=1, concat_axis=0, tiled=True),
    )
    all_act, all_pre = (
        lax.all_gather(act, "row", axis=0, tiled=True),
        lax.all_gather(grad_pre, "row", axis=0, tiled=True),
    )
    grad_in = contract(all_tok, all_pre, 0, 0)
    grad_out = contract(all_act, all_grad, 0, 0)
    return (
        block_out.astype(jnp.bfloat16),
        grad_tokens.astype(jnp.bfloat16),
        grad_in.astype(jnp.bfloat16),
        grad_out.astype(jnp.bfloat16),
    )


def solution(mesh):
    return jax.shard_map(
        body,
        mesh=mesh,
        in_specs=(P("row", "col"), P("row", "col"), P("col", "row"), P("row", "col")),
        out_specs=(P("row", "col"), P("row", "col"), P("row", "col"), P("col", "row")),
        check_vma=False,
    )
```

profile of v0, /device:TPU:2, one launch (start us, length us, event | category | flops | bytes accessed | tf_op | source)
XLA Modules:
  0.0 810.7 jit_solution(18078944411229849737)
XLA Ops:
  7.2 0.0 all-gather.7.cloned.1.call-start
  7.2 1.7 copy.10
  9.0 0.0 all-gather.7.cloned.1.call-update
  9.0 0.0 copy-start.3
  9.0 0.0 all-gather.9.cloned.1.call-start
  9.0 0.7 all-gather.9.cloned.1.call-update
  9.7 0.0 all-gather.13.cloned.1.call-start
  9.8 0.1 copy-done.3
  9.9 0.8 copy.11
  10.7 0.0 all-gather.13.cloned.1.call-update
  10.7 0.0 all-gather.11.cloned.1.call-start
  10.8 0.5 all-gather.11.cloned.1.call-update
  11.3 0.0 all-gather.15.cloned.1.call-start
  11.4 44.8 %all-gather.7.cloned.1.call-done = bf16[128,6144]{0,1:T(8,128)(2,1)} async-done(((bf16[128,768]{0,1:T(8,128)(2,1)}), bf16[128,6144]{0,1:T(8,128)(2,1)}) %all-gather.7.cloned.1.call-update) | async-done | bytes 1572880 | tf_op jit(solution)/shard_map/all_gather | solution.py:19
  56.2 226.5 %all-gather.9.cloned.1.call-done = bf16[6144,3072]{1,0:T(8,128)(2,1)} async-done(((bf16[1536,3072]{1,0:T(8,128)(2,1)}), bf16[6144,3072]{1,0:T(8,128)(2,1)}) %all-gather.9.cloned.1.call-update) | async-done | bytes 37748752 | tf_op jit(solution)/shard_map/all_gather | solution.py:23
  282.7 15.9 %multiply_convert_fusion = (bf16[128,3072]{1,0:T(8,128)(2,1)}, f32[128,3072]{1,0:T(8,128)S(1)}) fusion(bf16[128,6144]{0,1:T(8,128)(2,1)} %all-gather.7.cloned.1.call-done, bf16[6144,3072]{1,0:T(8,128)(2,1)} %all-gather.9.cloned.1.call-done), kind=kOutput, calls=%fused_computation.10 | convolution fusion | flops 4833804288 | bytes 41680896 | tf_op jit(solution)/shard_map/dot_general | solution.py:26
  298.6 32.2 %all-gather.13.cloned.1.call-done = bf16[128,6144]{0,1:T(8,128)(2,1)} async-done(((bf16[128,768]{0,1:T(8,128)(2,1)}), bf16[128,6144]{0,1:T(8,128)(2,1)}) %all-gather.13.cloned.1.call-update) | async-done | bytes 1572880 | tf_op jit(solution)/shard_map/all_gather | solution.py:20
  330.8 226.3 %all-gather.11.cloned.1.call-done = bf16[3072,6144]{1,0:T(8,128)(2,1)} async-done(((bf16[3072,1536]{1,0:T(8,128)(2,1)}), bf16[3072,6144]{1,0:T(8,128)(2,1)}) %all-gather.11.cloned.1.call-update) | async-done | bytes 37748752 | tf_op jit(solution)/shard_map/all_gather | solution.py:24
  557.1 18.9 %fusion.1 = bf16[128,3072]{1,0:T(8,128)(2,1)} fusion(bf16[128,6144]{0,1:T(8,128)(2,1)} %all-gather.13.cloned.1.call-done, bf16[3072,6144]{1,0:T(8,128)(2,1)} %all-gather.11.cloned.1.call-done, f32[128,3072]{1,0:T(8,128)S(1)} %get-tuple-element.17), kind=kOutput, calls=%fused_computation.4 | convolution fusion | flops 4835770368 | bytes 41680896 | tf_op jit(solution)/shard_map/dot_general | solution.py:12
  576.0 0.0 copy-start.1
  576.0 0.0 all-gather.15.cloned.1.call-update
  576.0 0.0 all-gather.17.cloned.1.call-start
  576.1 0.5 all-gather.17.cloned.1.call-update
  576.6 0.0 reduce-scatter.3.cloned.1.call-start
  576.6 0.5 copy-done.1
  577.1 17.3 %fusion.6 = f32[128,6144]{1,0:T(8,128)} fusion(bf16[128,3072]{1,0:T(8,128)(2,1)S(1)} %copy-done.1, bf16[3072,6144]{1,0:T(8,128)(2,1)} %all-gather.11.cloned.1.call-done), kind=kOutput, calls=%fused_computation.12 | convolution fusion | flops 4831838208 | bytes 41680896 | tf_op jit(solution)/shard_map/dot_general | solution.py:29
  594.4 0.0 copy-start
  594.4 0.0 reduce-scatter.3.cloned.1.call-update
  594.4 0.2 reduce-scatter.5.cloned.1.call-start
  594.7 0.9 copy-done
  595.5 19.5 %fusion.7 = f32[128,6144]{1,0:T(8,128)} fusion(bf16[128,3072]{1,0:T(8,128)(2,1)S(1)} %copy-done, bf16[6144,3072]{1,0:T(8,128)(2,1)} %all-gather.9.cloned.1.call-done), kind=kOutput, calls=%fused_computation.13 | convolution fusion | flops 4831838208 | bytes 41680896 | tf_op jit(solution)/shard_map/dot_general | solution.py:12
  615.1 0.0 copy-start.2
  615.1 0.0 reduce-scatter.5.cloned.1.call-update
  615.1 1.6 copy-done.2
  616.7 33.3 %all_to_all.38 = bf16[128,4,1536]{0,2,1:T(8,128)(2,1)S(1)} all-to-all(bf16[128,4,1536]{0,2,1:T(8,128)(2,1)S(1)} %bitcast.20), channel_id=1, replica_groups=mesh['row'=4,'col'=8] {'row'}, dimensions={1} | all-to-all | bytes 3145728 | tf_op jit(solution)/shard_map/all_to_all | solution.py:39
  650.0 5.2 all-to-all-start.1
  655.2 1.6 copy.12
  656.8 16.9 %all-to-all-done.1 = bf16[128,4,1536]{0,2,1:T(8,128)(2,1)S(1)} async-done(((bf16[128,4,1536]{0,2,1:T(8,128)(2,1)}), bf16[128,4,1536]{0,2,1:T(8,128)(2,1)S(1)}, u32[]{:S(2)}, u32[]{:S(2)}) %all-to-all-start.1) | async-done | bytes 1572896 | tf_op jit(solution)/shard_map/all_to_all | solution.py:40
  673.6 0.7 copy.13
  674.3 0.0 all-gather.15.cloned.1.call-done
  674.4 9.5 %fusion = bf16[1536,3072]{0,1:T(8,128)(2,1)} fusion(bf16[512,3072]{1,0:T(8,128)(2,1)} %all-gather.15.cloned.1.call-done, bf16[512,1536]{1,0:T(8,128)(2,1)} %bitcast.24), kind=kOutput, calls=%fused_computation.2 | convolution fusion | flops 4836556800 | bytes 14155776 | tf_op jit(solution)/shard_map/dot_general | solution.py:12
  683.9 12.7 %copy.14 = bf16[1536,3072]{1,0:T(8,128)(2,1)} copy(bf16[1536,3072]{0,1:T(8,128)(2,1)} %fusion) | data formatting | bytes 18874368
  696.5 0.0 all-gather.17.cloned.1.call-done
  696.5 9.4 %convolution_convert_fusion = bf16[3072,1536]{1,0:T(8,128)(2,1)} fusion(bf16[512,3072]{1,0:T(8,128)(2,1)} %all-gather.17.cloned.1.call-done, bf16[512,1536]{1,0:T(8,128)(2,1)S(1)} %bitcast.23), kind=kOutput, calls=%fused_computation | convolution fusion | flops 4836556800 | bytes 14155776 | tf_op jit(solution)/shard_map/dot_general | solution.py:12
  706.0 19.3 %reduce-scatter.3.cloned.1.call-done = f32[128,768]{1,0:T(8,128)} async-done(((f32[128,6144]{1,0:T(8,128)}), f32[128,768]{1,0:T(8,128)}) %reduce-scatter.3.cloned.1.call-update) | async-done | bytes 393232 | tf_op jit(solution)/shard_map/reduce_scatter | solution.py:35
  725.2 1.7 convert_element_type.22
  726.9 75.2 %reduce-scatter.5.cloned.1.call-done = f32[128,768]{1,0:T(8,128)} async-done(((f32[128,6144]{1,0:T(8,128)}), f32[128,768]{1,0:T(8,128)}) %reduce-scatter.5.cloned.1.call-update) | async-done | bytes 393232 | tf_op jit(solution)/shard_map/reduce_scatter | solution.py:36
  802.1 1.7 convert_element_type.24
Async XLA Ops:
  7.2 49.0 %all-gather.7.cloned.1.call-start = ((), (), s32[]{:S(2)}) async-start(), calls=%async_computation.4 | async-start | bytes 1769472 | tf_op jit(solution)/shard_map/all_gather | solution.py:19
  9.0 0.9 copy-start.3
  9.0 273.7 %all-gather.9.cloned.1.call-start = ((), (), s32[]{:S(2)}) async-start(), calls=%async_computation.5 | async-start | bytes 47185920 | tf_op jit(solution)/shard_map/all_gather | solution.py:23
  9.7 321.1 %all-gather.13.cloned.1.call-start = ((), (), s32[]{:S(2)}) async-start(), calls=%async_computation.8 | async-start | bytes 1769472 | tf_op jit(solution)/shard_map/all_gather | solution.py:20
  10.7 546.4 %all-gather.11.cloned.1.call-start = ((), (), s32[]{:S(2)}) async-start(), calls=%async_computation.6 | async-start | bytes 47185920 | tf_op jit(solution)/shard_map/all_gather | solution.py:24
  11.3 663.0 %all-gather.15.cloned.1.call-start = ((), (), s32[]{:S(2)}) async-start(), calls=%async_computation.10 | async-start | bytes 3932160 | tf_op jit(solution)/shard_map/all_gather | solution.py:44
  576.0 1.1 copy-start.1
  576.0 120.5 %all-gather.17.cloned.1.call-start = ((), (), s32[]{:S(2)}) async-start(), calls=%async_computation.11 | async-start | bytes 3932160 | tf_op jit(solution)/shard_map/all_gather | solution.py:43
  576.6 148.6 %reduce-scatter.3.cloned.1.call-start = ((), (), s32[]{:S(2)}) async-start(), calls=%async_computation.7 | async-start | bytes 3538944 | tf_op jit(solution)/shard_map/reduce_scatter | solution.py:35
  594.4 1.1 copy-start
  594.4 207.7 %reduce-scatter.5.cloned.1.call-start = ((), (), s32[]{:S(2)}) async-start(), calls=%async_computation.9 | async-start | bytes 3538944 | tf_op jit(solution)/shard_map/reduce_scatter | solution.py:36
  615.1 1.6 copy-start.2
  650.0 23.7 %all-to-all-start.1 = ((bf16[128,4,1536]{0,2,1:T(8,128)(2,1)}), bf16[128,4,1536]{0,2,1:T(8,128)(2,1)S(1)}, u32[]{:S(2)}, u32[]{:S(2)}) async-start(bf16[128,4,1536]{0,2,1:T(8,128)(2,1)} %bitcast.4), calls=%async_computation.3 | async-start | bytes 3145728 | tf_op jit(solution)/shard_map/all_to_all | solution.py:40
Sparse Core Ops, SparseCore 0:
  10.8 45.4 all-gather.6
  57.8 224.8 all-gather.8
  285.4 45.3 all-gather.12
  332.2 224.8 all-gather.10
  576.1 28.5 all-gather.14
  606.1 39.5 all-gather.16
  649.3 75.9 reduce-scatter.2
  728.8 73.2 reduce-scatter.4
where the time goes:
time: 813 us; the launch traced here: 811 us
  waiting for transfers between devices  643 us (79%)
  matrix products  90.5 us (11%)
  blocking collectives  33.3 us (4%)
  local copies, waits for them, and re-layouts  20.6 us (3%)
  between operations  14.2 us (2%)
    all_gather x1, waiting for transfers between devices, body(): lax.all_gather(weight_in, 'row', axis=0, tiled=True)  226 us
    all_gather x1, waiting for transfers between devices, body(): lax.all_gather(weight_out, 'row', axis=1, tiled=True)  226 us
    reduce_scatter x1, waiting for transfers between devices, body(): lax.psum_scatter(back_terms, 'col', scatter_dimension=1, tiled=True)  75.2 us
    dot_general x4, matrix products, contract(): lax.dot_general(left, right, (((left_dim,), (right_dim,)), ((), ())), pre...  57.3 us
    all_gather x1, waiting for transfers between devices, body(): lax.all_gather(tokens, 'col', axis=1, tiled=True)  44.8 us
    all_to_all x1, blocking collectives, body(): lax.all_to_all(tok_panel, 'row', split_axis=1, concat_axis=0, tiled=True)  33.3 us
    all_gather x1, waiting for transfers between devices, body(): lax.all_gather(out_grad, 'col', axis=1, tiled=True)  32.2 us
    reduce_scatter x1, waiting for transfers between devices, body(): lax.psum_scatter(out_terms, 'col', scatter_dimension=1, tiled=True)  19.3 us
  transfers between devices with their start and end apart: 9, of which 7 were waited for; matrix products, arithmetic and copies ran while one was open for 11% of the time, Pallas kernels for 0%

commit v1 on v0

v1 whole, which is shorter than its diff:
```python
import functools

import jax
import jax.numpy as jnp
from jax import lax
from jax.sharding import PartitionSpec as P

CHUNKS = 2


def cdf_of(value):
    return 0.5 * (1.0 + lax.erf(value * 0.7071067811865476))


def contract(left, right, left_dim, right_dim):
    return lax.dot_general(
        left, right, (((left_dim,), (right_dim,)), ((), ())), preferred_element_type=jnp.float32
    )


def swap(value, axis, size, mask):
    return lax.ppermute(value, axis, [(i, i ^ mask) for i in range(size)])


def transposed(value, rows, cols):
    per = cols // rows
    pairs = [
        (r * cols + c, (c // per) * cols + r * per + c % per) for r in range(rows) for c in range(cols)
    ]
    return lax.ppermute(value, ("row", "col"), pairs)


def is_small(rows, cols):
    return rows == 4 and cols == 8


def gather_panel(block, rows, cols):
    core = lax.axis_index("row") % 2
    if is_small(rows, cols):
        parts = [block] + [swap(block, "col", cols, 2 * d) for d in (1, 2, 3)]
        mine = jnp.where(
            core == 0,
            jnp.concatenate(parts, axis=1),
            jnp.concatenate(parts[2:] + parts[:2], axis=1),
        )
        other = swap(mine, "col", cols, 1)
        return jnp.where(
            lax.axis_index("col") % 2 == 0,
            jnp.concatenate([mine, other], axis=2),
            jnp.concatenate([other, mine], axis=2),
        )
    per = cols // rows
    two, n, f = block.shape
    whole = lax.all_gather(block, "col", axis=0)
    whole = whole.reshape(rows, per, two, n, f).transpose(2, 0, 3, 1, 4).reshape(two, rows * n, per * f)
    return jnp.where(core == 0, whole, jnp.roll(whole, rows * n // 2, axis=1))


def scatter_sum(terms, rows, cols):
    core = lax.axis_index("row") % 2
    two, all_n, all_f = terms.shape
    n, per = all_n // rows, cols // rows
    f = all_f // per
    if is_small(rows, cols):
        side = lax.axis_index("col") % 2
        away = lax.dynamic_slice_in_dim(terms, (1 - side) * f, f, axis=2).astype(jnp.bfloat16)
        total = lax.dynamic_slice_in_dim(terms, side * f, f, axis=2) + swap(away, "col", cols, 1)

        def block_of(d):
            return lax.dynamic_slice_in_dim(total, (d ^ (2 * core)) * n, n, axis=1)

        out = block_of(0)
        for d in (1, 2, 3):
            out = out + swap(block_of(d).astype(jnp.bfloat16), "col", cols, 2 * d)
        return out
    terms = jnp.where(core == 0, terms, jnp.roll(terms, all_n // 2, axis=1))
    terms = terms.reshape(two, rows, n, per, f).transpose(1, 3, 0, 2, 4).reshape(cols, two, n, f)
    return lax.psum_scatter(terms, "col", scatter_dimension=0)


def body(rows, cols, tokens, weight_in, weight_out, out_grad):
    both = jnp.stack([tokens, out_grad])
    n = tokens.shape[0] // CHUNKS
    panels, acts, pres, outs = [], [], [], []
    for step in range(CHUNKS):
        block = transposed(both[:, step * n : (step + 1) * n], rows, cols)
        panel = gather_panel(block, rows, cols)
        panels.append(panel)
        half = panel.shape[1] // 2
        terms = jnp.stack([contract(panel[0], weight_in, 1, 0), contract(panel[1], weight_out, 1, 1)])
        sums = terms[:, :half] + swap(terms[:, half:].astype(jnp.bfloat16), "row", rows, 1)
        sums = sums + swap(sums.astype(jnp.bfloat16), "row", rows, 2)
        hidden_pre, grad_act = sums[0], sums[1]
        cumul = cdf_of(hidden_pre)
        density = jnp.exp(-0.5 * hidden_pre * hidden_pre) * 0.3989422804014327
        act = (hidden_pre * cumul).astype(jnp.bfloat16)
        grad_pre = (grad_act * (cumul + hidden_pre * density)).astype(jnp.bfloat16)
        own = jnp.stack([act, grad_pre])
        full = jnp.concatenate([own, swap(own, "row", rows, 1)], axis=1)
        acts.append(full[0])
        pres.append(full[1])
        terms = jnp.stack([contract(full[0], weight_out, 1, 0), contract(full[1], weight_in, 1, 1)])
        outs.append(transposed(scatter_sum(terms, rows, cols).astype(jnp.bfloat16), rows, cols))
    panel = jnp.concatenate(panels, axis=1)
    grad_in = contract(panel[0], jnp.concatenate(pres), 0, 0)
    grad_out = contract(jnp.concatenate(acts), panel[1], 0, 0)
    out = jnp.concatenate(outs, axis=1)
    return out[0], out[1], grad_in.astype(jnp.bfloat16), grad_out.astype(jnp.bfloat16)


def solution(mesh):
    return jax.shard_map(
        functools.partial(body, mesh.shape["row"], mesh.shape["col"]),
        mesh=mesh,
        in_specs=(P("row", "col"), P("row", "col"), P("col", "row"), P("row", "col")),
        out_specs=(P("row", "col"), P("row", "col"), P("row", "col"), P("col", "row")),
        check_vma=False,
    )
```

time: 813 us -> 270 us (0.33)
  waiting for transfers between devices: 643 us -> 159 us
  matrix products: 90.5 us -> 53.5 us
  blocking collectives: 33.3 us -> 0 us
  starting transfers between devices: 5.74 us -> 37.6 us
  local copies, waits for them, and re-layouts: 20.6 us -> 3.53 us
  between operations: 14.2 us -> 1.13 us
  other arithmetic: 3.39 us -> 15.7 us
    all_gather x6 -> x0, waiting for transfers between devices: 530 us -> none  [the longest x1 226 us: body(): lax.all_gather(weight_in, 'row', axis=0, tiled=True)]
    ppermute x0 -> x26, waiting for transfers between devices: none -> 159 us  [the longest x22 136 us: swap(): return lax.ppermute(value, axis, [(i, i ^ mask) for i in range(size)])]
    reduce_scatter x2 -> x0, waiting for transfers between devices: 94.5 us -> none  [the longest x1 75.2 us: body(): lax.psum_scatter(back_terms, 'col', scatter_dimension=1, tiled=True)]
    ppermute x0 -> x26, starting transfers between devices: none -> 37.6 us  [the longest x22 20.5 us: swap(): return lax.ppermute(value, axis, [(i, i ^ mask) for i in range(size)])]
    all_to_all x1 -> x0, blocking collectives: 33.3 us -> none  [body(): lax.all_to_all(tok_panel, 'row', split_axis=1, concat_axis=0, tiled=True)]
    dot_general x2 -> x0, matrix products: 33.2 us -> none  [the longest x1 17.3 us: body(): out_terms = jnp.dot(act, out_panel, preferred_element_type=jnp.float32)]
    all_to_all x1 -> x0, waiting for transfers between devices: 16.9 us -> none  [body(): lax.all_to_all(grad_panel, 'row', split_axis=1, concat_axis=0, tiled=True)]
    unnamed x11 -> x37, local copies, waits for them, and re-layouts: 18.3 us -> 2.19 us
  transfers between devices with their start and end apart: 9 -> 26, of which waited for: 7 -> 16; matrix products, arithmetic and copies ran while one was open for 11% -> 21% of each run, Pallas kernels for 0% -> 0%
where the time goes in v1:
time: 270 us
  waiting for transfers between devices  159 us (59%)
  matrix products  53.5 us (20%)
  starting transfers between devices  37.6 us (14%)
  other arithmetic  15.7 us (6%)
  local copies, waits for them, and re-layouts  3.53 us (1%)
    ppermute x22, waiting for transfers between devices, swap(): return lax.ppermute(value, axis, [(i, i ^ mask) for i in range(size)])  136 us
    dot_general x10, matrix products, contract(): lax.dot_general(left, right, (((left_dim,), (right_dim,)), ((), ())), pre...  53.5 us
    ppermute x4, waiting for transfers between devices, transposed(): return lax.ppermute(value, ('row', 'col'), pairs)  22.6 us
    ppermute x22, starting transfers between devices, swap(): return lax.ppermute(value, axis, [(i, i ^ mask) for i in range(size)])  20.5 us
    ppermute x4, starting transfers between devices, transposed(): return lax.ppermute(value, ('row', 'col'), pairs)  17.1 us
  transfers between devices with their start and end apart: 26, of which 16 were waited for; matrix products, arithmetic and copies ran while one was open for 21% of the time, Pallas kernels for 0%

profile of v1, /device:TPU:2, one launch (start us, length us, event | category | flops | bytes accessed | tf_op | source)
XLA Modules:
  0.0 270.0 jit_solution(18213530966500604182)
XLA Ops:
  0.6 1.1 pad_maximum_fusion.7
  1.7 4.5 %collective-permute-start.13 = (bf16[2,64,768]{2,1,0:T(8,128)(2,1)S(1)}, bf16[2,64,768]{2,1,0:T(8,128)(2,1)S(1)}, u32[]{:S(2)}, u32[]{:S(2)}) collective-permute-start(bf16[2,64,768]{2,1,0:T(8,128)(2,1)S(1)} %get-tuple-element.20), channel_id=1, source_target_pairs={{0,0},{1,1},{2,8},{3,9},{4,16},{5,17},{6,24},{7,25},{8,2},{9,3},{1... | collective-permute-start | bytes 589832 | tf_op jit(solution)/shard_map/ppermute | solution.py:30
  6.2 10.7 %collective-permute-done.13 = bf16[2,64,768]{2,1,0:T(8,128)(2,1)S(1)} collective-permute-done((bf16[2,64,768]{2,1,0:T(8,128)(2,1)S(1)}, bf16[2,64,768]{2,1,0:T(8,128)(2,1)S(1)}, u32[]{:S(2)}, u32[]{:S(2)}) %collective-permute-start.13) | collective-permute-done | bytes 196640 | tf_op jit(solution)/shard_map/ppermute | solution.py:30
  16.9 1.8 collective-permute-start.15
  18.7 2.6 collective-permute-start.14
  21.3 5.2 %collective-permute-done.16 = bf16[2,64,768]{2,1,0:T(8,128)(2,1)S(1)} collective-permute-done((bf16[2,64,768]{2,1,0:T(8,128)(2,1)S(1)}, bf16[2,64,768]{2,1,0:T(8,128)(2,1)S(1)}, u32[]{:S(2)}, u32[]{:S(2)}) %collective-permute-start.16) | collective-permute-done | bytes 196640 | tf_op jit(solution)/shard_map/ppermute | solution.py:22
  26.6 8.1 %collective-permute-done.15 = bf16[2,64,768]{2,1,0:T(8,128)(2,1)S(1)} collective-permute-done((bf16[2,64,768]{2,1,0:T(8,128)(2,1)S(1)}, bf16[2,64,768]{2,1,0:T(8,128)(2,1)S(1)}, u32[]{:S(2)}, u32[]{:S(2)}) %collective-permute-start.15) | collective-permute-done | bytes 196640 | tf_op jit(solution)/shard_map/ppermute | solution.py:22
  35.0 1.6 collective-permute-start.17
  36.6 1.9 collective-permute-start
  38.5 10.1 %collective-permute-done = bf16[2,64,768]{2,1,0:T(8,128)(2,1)S(1)} collective-permute-done((bf16[2,64,768]{2,1,0:T(8,128)(2,1)S(1)}, bf16[2,64,768]{2,1,0:T(8,128)(2,1)S(1)}, u32[]{:S(2)}, u32[]{:S(2)}) %collective-permute-start) | collective-permute-done | bytes 196640 | tf_op jit(solution)/shard_map/ppermute | solution.py:30
  48.6 4.3 %collective-permute-start.1 = (bf16[2,64,768]{2,1,0:T(8,128)(2,1)S(1)}, bf16[2,64,768]{2,1,0:T(8,128)(2,1)S(1)}, u32[]{:S(2)}, u32[]{:S(2)}) collective-permute-start(bf16[2,64,768]{2,1,0:T(8,128)(2,1)S(1)} %collective-permute-done), channel_id=1, source_target_pairs={{0,2},{1,3},{2,0},{3,1},{4,6},{5,7},{6,4},{7,5},{8,10},{9,11},{10,... | collective-permute-start | bytes 589832 | tf_op jit(solution)/shard_map/ppermute | solution.py:22
  53.0 5.3 %collective-permute-done.3 = bf16[2,64,768]{2,1,0:T(8,128)(2,1)S(1)} collective-permute-done((bf16[2,64,768]{2,1,0:T(8,128)(2,1)S(1)}, bf16[2,64,768]{2,1,0:T(8,128)(2,1)S(1)}, u32[]{:S(2)}, u32[]{:S(2)}) %collective-permute-start.3) | collective-permute-done | bytes 196640 | tf_op jit(solution)/shard_map/ppermute | solution.py:22
  58.2 8.5 %collective-permute-done.2 = bf16[2,64,768]{2,1,0:T(8,128)(2,1)S(1)} collective-permute-done((bf16[2,64,768]{2,1,0:T(8,128)(2,1)S(1)}, bf16[2,64,768]{2,1,0:T(8,128)(2,1)S(1)}, u32[]{:S(2)}, u32[]{:S(2)}) %collective-permute-start.2) | collective-permute-done | bytes 196640 | tf_op jit(solution)/shard_map/ppermute | solution.py:22
  68.0 6.0 %convolution_bitcast_fusion = f32[1,256,3072]{2,1,0:T(8,128)S(1)} fusion(bf16[3072,1536]{1,0:T(8,128)(2,1)} %param.6, bf16[2,256,1536]{2,1,0:T(8,128)(2,1)S(1)} %maximum_select_fusion.1), kind=kOutput, calls=%fused_computation.6 | convolution fusion | flops 2415919104 | bytes 13369344 | tf_op jit(solution)/shard_map/dot_general | solution.py:16
  74.6 2.6 convolution_bitcast_fusion.1
  77.5 8.8 %collective-permute-done.4 = bf16[2,256,768]{2,1,0:T(8,128)(2,1)S(1)} collective-permute-done((bf16[2,256,768]{2,1,0:T(8,128)(2,1)S(1)}, bf16[2,256,768]{2,1,0:T(8,128)(2,1)S(1)}, u32[]{:S(2)}, u32[]{:S(2)}) %collective-permute-start.4) | collective-permute-done | bytes 786464 | tf_op jit(solution)/shard_map/ppermute | solution.py:22
  86.7 5.8 %convolution_bitcast_fusion.2 = f32[1,256,3072]{2,1,0:T(8,128)S(1)} fusion(bf16[3072,1536]{1,0:T(8,128)(2,1)} %param.6, bf16[2,256,1536]{2,1,0:T(8,128)(2,1)S(1)} %maximum_select_fusion), kind=kOutput, calls=%fused_computation.8 | convolution fusion | flops 2415919104 | bytes 13369344 | tf_op jit(solution)/shard_map/dot_general | solution.py:16
  92.5 5.4 %convolution_bitcast_fusion.3 = f32[1,256,3072]{2,1,0:T(8,128)S(1)} fusion(bf16[1536,3072]{1,0:T(8,128)(2,1)} %param.5, bf16[2,256,1536]{2,1,0:T(8,128)(2,1)S(1)} %maximum_select_fusion), kind=kOutput, calls=%fused_computation.9 | convolution fusion | flops 2415919104 | bytes 13369344 | tf_op jit(solution)/shard_map/dot_general | solution.py:16
  97.9 1.6 fusion.5
  100.1 1.7 fusion.42
  101.9 2.0 collective-permute-done.5
  103.9 2.4 fusion.41
  106.4 33.0 %collective-permute-done.19 = bf16[2,128,3072]{2,1,0:T(8,128)(2,1)} collective-permute-done((bf16[2,128,3072]{2,1,0:T(8,128)(2,1)}, bf16[2,128,3072]{2,1,0:T(8,128)(2,1)}, u32[]{:S(2)}, u32[]{:S(2)}) %collective-permute-start.19) | collective-permute-done | bytes 1572896 | tf_op jit(solution)/shard_map/ppermute | solution.py:22
  139.4 2.1 convert_add_fusion
  141.5 0.7 multiply_convert_fusion
  142.5 30.1 %collective-permute-done.6 = bf16[2,128,3072]{2,1,0:T(8,128)(2,1)S(1)} collective-permute-done((bf16[2,128,3072]{2,1,0:T(8,128)(2,1)S(1)}, bf16[2,128,3072]{2,1,0:T(8,128)(2,1)S(1)}, u32[]{:S(2)}, u32[]{:S(2)}) %collective-permute-start.6) | collective-permute-done | bytes 1572896 | tf_op jit(solution)/shard_map/ppermute | solution.py:22
  172.6 2.2 convert_add_fusion.1
  174.8 0.7 multiply_convert_fusion.1
  177.0 2.6 convolution_bitcast_fusion.5
  179.8 5.4 %convolution_bitcast_fusion.4 = f32[1,256,1536]{2,1,0:T(8,128)S(1)} fusion(bf16[1536,3072]{1,0:T(8,128)(2,1)} %param.5, bf16[2,256,3072]{2,1,0:T(8,128)(2,1)S(1)} %pad_maximum_fusion.3), kind=kOutput, calls=%fused_computation.38 | convolution fusion | flops 2415919104 | bytes 12582912 | tf_op jit(solution)/shard_map/dot_general | solution.py:16
  185.5 5.2 %convolution_bitcast_fusion.7 = f32[1,256,1536]{2,1,0:T(8,128)S(1)} fusion(bf16[3072,1536]{1,0:T(8,128)(2,1)} %param.6, bf16[2,256,3072]{2,1,0:T(8,128)(2,1)S(1)} %pad_maximum_fusion.2), kind=kOutput, calls=%fused_computation.41 | convolution fusion | flops 2415919104 | bytes 12582912 | tf_op jit(solution)/shard_map/dot_general | solution.py:16
  190.7 5.4 %convolution_bitcast_fusion.6 = f32[1,256,1536]{2,1,0:T(8,128)S(1)} fusion(bf16[1536,3072]{1,0:T(8,128)(2,1)} %param.5, bf16[2,256,3072]{2,1,0:T(8,128)(2,1)S(1)} %pad_maximum_fusion.2), kind=kOutput, calls=%fused_computation.40 | convolution fusion | flops 2415919104 | bytes 12582912 | tf_op jit(solution)/shard_map/dot_general | solution.py:16
  196.4 0.6 collective-permute-start.21
  197.1 1.6 collective-permute-start.8
  198.7 7.5 %convolution_convert_fusion = bf16[3072,1536]{1,0:T(8,128)(2,1)} fusion(bf16[256,3072]{1,0:T(8,128)(2,1)S(1)} %get-tuple-element.6, bf16[256,3072]{1,0:T(8,128)(2,1)S(1)} %get-tuple-element.4, bf16[2,256,1536]{2,1,0:T(8,128)(2,1)S(1)} %copy-done.9, bf16[2,256,1536]{2,1,0:T(8,128)(2,1)S(1)} %copy-done.11), kind=kOutput, calls=%fused_computation | convolution fusion | flops 4845993984 | bytes 15728640 | tf_op jit(solution)/shard_map/dot_general | solution.py:16
  206.2 10.7 %collective-permute-done.21 = bf16[2,256,768]{2,1,0:T(8,128)(2,1)S(1)} collective-permute-done((bf16[2,256,768]{2,1,0:T(8,128)(2,1)S(1)}, bf16[2,256,768]{2,1,0:T(8,128)(2,1)S(1)}, u32[]{:S(2)}, u32[]{:S(2)}) %collective-permute-start.21) | collective-permute-done | bytes 786464 | tf_op jit(solution)/shard_map/ppermute | solution.py:22
  217.3 1.3 collective-permute-start.24
  218.6 2.2 collective-permute-start.23
  220.8 11.7 %collective-permute-done.8 = bf16[2,256,768]{2,1,0:T(8,128)(2,1)S(1)} collective-permute-done((bf16[2,256,768]{2,1,0:T(8,128)(2,1)S(1)}, bf16[2,256,768]{2,1,0:T(8,128)(2,1)S(1)}, u32[]{:S(2)}, u32[]{:S(2)}) %collective-permute-start.8) | collective-permute-done | bytes 786464 | tf_op jit(solution)/shard_map/ppermute | solution.py:22
  232.8 1.3 collective-permute-start.11
  234.2 2.2 collective-permute-start.10
  236.4 3.2 %collective-permute-start.25 = (bf16[2,64,768]{2,1,0:T(8,128)(2,1)S(1)}, bf16[2,64,768]{2,1,0:T(8,128)(2,1)S(1)}, u32[]{:S(2)}, u32[]{:S(2)}) collective-permute-start(bf16[2,64,768]{2,1,0:T(8,128)(2,1)S(1)} %add_convert_fusion), channel_id=1, source_target_pairs={{0,0},{1,1},{2,8},{3,9},{4,16},{5,17},{6,24},{7,25},{8,2},{9,3},{1... | collective-permute-start | bytes 589832 | tf_op jit(solution)/shard_map/ppermute | solution.py:30
  239.7 4.0 %collective-permute-done.9 = bf16[2,64,768]{2,1,0:T(8,128)(2,1)S(1)} collective-permute-done((bf16[2,64,768]{2,1,0:T(8,128)(2,1)S(1)}, bf16[2,64,768]{2,1,0:T(8,128)(2,1)S(1)}, u32[]{:S(2)}, u32[]{:S(2)}) %collective-permute-start.9) | collective-permute-done | bytes 196640 | tf_op jit(solution)/shard_map/ppermute | solution.py:22
  244.1 8.1 %collective-permute-done.10 = bf16[2,64,768]{2,1,0:T(8,128)(2,1)S(1)} collective-permute-done((bf16[2,64,768]{2,1,0:T(8,128)(2,1)S(1)}, bf16[2,64,768]{2,1,0:T(8,128)(2,1)S(1)}, u32[]{:S(2)}, u32[]{:S(2)}) %collective-permute-start.10) | collective-permute-done | bytes 196640 | tf_op jit(solution)/shard_map/ppermute | solution.py:22
  252.4 7.5 %collective-permute-start.12 = (bf16[2,64,768]{2,1,0:T(8,128)(2,1)S(1)}, bf16[2,64,768]{2,1,0:T(8,128)(2,1)S(1)}, u32[]{:S(2)}, u32[]{:S(2)}) collective-permute-start(bf16[2,64,768]{2,1,0:T(8,128)(2,1)S(1)} %add_convert_fusion.1), channel_id=1, source_target_pairs={{0,0},{1,1},{2,8},{3,9},{4,16},{5,17},{6,24},{7,25},{8,2},{9,3},{1... | collective-permute-start | bytes 589832 | tf_op jit(solution)/shard_map/ppermute | solution.py:30
  259.9 7.6 %convolution_convert_fusion.1 = bf16[1536,3072]{1,0:T(8,128)(2,1)} fusion(bf16[256,3072]{1,0:T(8,128)(2,1)S(1)} %get-tuple-element.7, bf16[256,3072]{1,0:T(8,128)(2,1)S(1)} %get-tuple-element.5, bf16[2,256,1536]{2,1,0:T(8,128)(2,1)S(1)} %copy-done.11, bf16[2,256,1536]{2,1,0:T(8,128)(2,1)S(1)} %copy-done.9), kind=kOutput, calls=%fused_computation.1 | convolution fusion | flops 4845993984 | bytes 15728640 | tf_op jit(solution)/shard_map/dot_general | solution.py:16
  267.4 1.8 collective-permute-done.12
  269.3 0.8 slice_bitcast_fusion.12
  (82 shorter events, 7.5 us)
Async XLA Ops:
  1.7 15.2 %collective-permute-start.13 = (bf16[2,64,768]{2,1,0:T(8,128)(2,1)S(1)}, bf16[2,64,768]{2,1,0:T(8,128)(2,1)S(1)}, u32[]{:S(2)}, u32[]{:S(2)}) collective-permute-start(bf16[2,64,768]{2,1,0:T(8,128)(2,1)S(1)} %get-tuple-element.20), channel_id=1, source_target_pairs={{0,0},{1,1},{2,8},{3,9},{4,16},{5,17},{6,24},{7,25},{8,2},{9,3},{1... | collective-permute-start | bytes 589832 | tf_op jit(solution)/shard_map/ppermute | solution.py:30
  16.9 9.6 %collective-permute-start.16 = (bf16[2,64,768]{2,1,0:T(8,128)(2,1)S(1)}, bf16[2,64,768]{2,1,0:T(8,128)(2,1)S(1)}, u32[]{:S(2)}, u32[]{:S(2)}) collective-permute-start(bf16[2,64,768]{2,1,0:T(8,128)(2,1)S(1)} %collective-permute-done.13), channel_id=1, source_target_pairs={{0,6},{1,7},{2,4},{3,5},{4,2},{5,3},{6,0},{7,1},{8,14},{9,15},{10,... | collective-permute-start | bytes 589832 | tf_op jit(solution)/shard_map/ppermute | solution.py:22
  16.9 17.7 %collective-permute-start.15 = (bf16[2,64,768]{2,1,0:T(8,128)(2,1)S(1)}, bf16[2,64,768]{2,1,0:T(8,128)(2,1)S(1)}, u32[]{:S(2)}, u32[]{:S(2)}) collective-permute-start(bf16[2,64,768]{2,1,0:T(8,128)(2,1)S(1)} %collective-permute-done.13), channel_id=1, source_target_pairs={{0,4},{1,5},{2,6},{3,7},{4,0},{5,1},{6,2},{7,3},{8,12},{9,13},{10,... | collective-permute-start | bytes 589832 | tf_op jit(solution)/shard_map/ppermute | solution.py:22
  18.7 15.9 %collective-permute-start.14 = (bf16[2,64,768]{2,1,0:T(8,128)(2,1)S(1)}, bf16[2,64,768]{2,1,0:T(8,128)(2,1)S(1)}, u32[]{:S(2)}, u32[]{:S(2)}) collective-permute-start(bf16[2,64,768]{2,1,0:T(8,128)(2,1)S(1)} %collective-permute-done.13), channel_id=1, source_target_pairs={{0,2},{1,3},{2,0},{3,1},{4,6},{5,7},{6,4},{7,5},{8,10},{9,11},{10,... | collective-permute-start | bytes 589832 | tf_op jit(solution)/shard_map/ppermute | solution.py:22
  35.0 32.6 %collective-permute-start.17 = (bf16[2,256,768]{2,1,0:T(8,128)(2,1)S(1)}, bf16[2,256,768]{2,1,0:T(8,128)(2,1)S(1)}, u32[]{:S(2)}, u32[]{:S(2)}) collective-permute-start(bf16[2,256,768]{2,1,0:T(8,128)(2,1)S(1)} %maximum_select_fusion.3), channel_id=1, source_target_pairs={{0,1},{1,0},{2,3},{3,2},{4,5},{5,4},{6,7},{7,6},{8,9},{9,8},{10,11... | collective-permute-start | bytes 2359304 | tf_op jit(solution)/shard_map/ppermute | solution.py:22
  36.6 12.0 %collective-permute-start = (bf16[2,64,768]{2,1,0:T(8,128)(2,1)S(1)}, bf16[2,64,768]{2,1,0:T(8,128)(2,1)S(1)}, u32[]{:S(2)}, u32[]{:S(2)}) collective-permute-start(bf16[2,64,768]{2,1,0:T(8,128)(2,1)S(1)} %get-tuple-element.21), channel_id=1, source_target_pairs={{0,0},{1,1},{2,8},{3,9},{4,16},{5,17},{6,24},{7,25},{8,2},{9,3},{1... | collective-permute-start | bytes 589832 | tf_op jit(solution)/shard_map/ppermute | solution.py:30
  48.6 9.6 %collective-permute-start.3 = (bf16[2,64,768]{2,1,0:T(8,128)(2,1)S(1)}, bf16[2,64,768]{2,1,0:T(8,128)(2,1)S(1)}, u32[]{:S(2)}, u32[]{:S(2)}) collective-permute-start(bf16[2,64,768]{2,1,0:T(8,128)(2,1)S(1)} %collective-permute-done), channel_id=1, source_target_pairs={{0,6},{1,7},{2,4},{3,5},{4,2},{5,3},{6,0},{7,1},{8,14},{9,15},{10,... | collective-permute-start | bytes 589832 | tf_op jit(solution)/shard_map/ppermute | solution.py:22
  48.6 18.1 %collective-permute-start.2 = (bf16[2,64,768]{2,1,0:T(8,128)(2,1)S(1)}, bf16[2,64,768]{2,1,0:T(8,128)(2,1)S(1)}, u32[]{:S(2)}, u32[]{:S(2)}) collective-permute-start(bf16[2,64,768]{2,1,0:T(8,128)(2,1)S(1)} %collective-permute-done), channel_id=1, source_target_pairs={{0,4},{1,5},{2,6},{3,7},{4,0},{5,1},{6,2},{7,3},{8,12},{9,13},{10,... | collective-permute-start | bytes 589832 | tf_op jit(solution)/shard_map/ppermute | solution.py:22
  48.6 18.1 %collective-permute-start.1 = (bf16[2,64,768]{2,1,0:T(8,128)(2,1)S(1)}, bf16[2,64,768]{2,1,0:T(8,128)(2,1)S(1)}, u32[]{:S(2)}, u32[]{:S(2)}) collective-permute-start(bf16[2,64,768]{2,1,0:T(8,128)(2,1)S(1)} %collective-permute-done), channel_id=1, source_target_pairs={{0,2},{1,3},{2,0},{3,1},{4,6},{5,7},{6,4},{7,5},{8,10},{9,11},{10,... | collective-permute-start | bytes 589832 | tf_op jit(solution)/shard_map/ppermute | solution.py:22
  67.0 19.3 %collective-permute-start.4 = (bf16[2,256,768]{2,1,0:T(8,128)(2,1)S(1)}, bf16[2,256,768]{2,1,0:T(8,128)(2,1)S(1)}, u32[]{:S(2)}, u32[]{:S(2)}) collective-permute-start(bf16[2,256,768]{2,1,0:T(8,128)(2,1)S(1)} %maximum_select_fusion.2), channel_id=1, source_target_pairs={{0,1},{1,0},{2,3},{3,2},{4,5},{5,4},{6,7},{7,6},{8,9},{9,8},{10,11... | collective-permute-start | bytes 2359304 | tf_op jit(solution)/shard_map/ppermute | solution.py:22
  67.6 6.4 %slice-start.3 = ((s8[9437184]{0:T(1024)(128)(4,1)}), s8[4194304]{0:T(1024)(128)(4,1)S(1)}, s32[]{:S(2)}) async-start(s8[9437184]{0:T(1024)(128)(4,1)} %bitcast.64), calls=%async_computation.3 | async-start | bytes 8388608
  67.9 6.0 %copy-start.8 = (bf16[2,256,1536]{2,1,0:T(8,128)(2,1)}, bf16[2,256,1536]{2,1,0:T(8,128)(2,1)S(1)}, u32[]{:S(2)}) copy-start(bf16[2,256,1536]{2,1,0:T(8,128)(2,1)S(1)} %maximum_select_fusion.1) | copy-start | bytes 4718596
  68.0 6.4 %slice-start.4 = ((s8[9437184]{0:T(1024)(128)(4,1)}), s8[4194304]{0:T(1024)(128)(4,1)S(1)}, s32[]{:S(2)}) async-start(s8[9437184]{0:T(1024)(128)(4,1)} %bitcast.64), calls=%async_computation.4 | async-start | bytes 8388608
  68.0 6.6 %slice-start.5 = ((s8[9437184]{0:T(1024)(128)(4,1)}), s8[1048576]{0:T(1024)(128)(4,1)S(1)}, s32[]{:S(2)}) async-start(s8[9437184]{0:T(1024)(128)(4,1)} %bitcast.64), calls=%async_computation.5 | async-start | bytes 2097152
  74.6 25.5 %copy-start.2 = (f32[1,256,3072]{2,1,0:T(8,128)}, f32[1,256,3072]{2,1,0:T(8,128)S(1)}, u32[]{:S(2)}) copy-start(f32[1,256,3072]{2,1,0:T(8,128)S(1)} %convolution_bitcast_fusion) | copy-start | bytes 9437188
  77.2 22.9 %copy-start.4 = (f32[1,256,3072]{2,1,0:T(8,128)}, f32[1,256,3072]{2,1,0:T(8,128)S(1)}, u32[]{:S(2)}) copy-start(f32[1,256,3072]{2,1,0:T(8,128)S(1)} %convolution_bitcast_fusion.1) | copy-start | bytes 9437188
  77.4 22.7 %collective-permute-start.18 = (bf16[2,128,3072]{2,1,0:T(8,128)(2,1)S(1)}, bf16[2,128,3072]{2,1,0:T(8,128)(2,1)S(1)}, u32[]{:S(2)}, u32[]{:S(2)}) collective-permute-start(bf16[2,128,3072]{2,1,0:T(8,128)(2,1)S(1)} %fusion.4), channel_id=1, source_target_pairs={{0,8},{8,0},{16,24},{24,16},{1,9},{9,1},{17,25},{25,17},{2,10},{10... | collective-permute-start | bytes 4718600 | tf_op jit(solution)/shard_map/ppermute | solution.py:22
  86.7 5.8 %copy-start.10 = (bf16[2,256,1536]{2,1,0:T(8,128)(2,1)}, bf16[2,256,1536]{2,1,0:T(8,128)(2,1)S(1)}, u32[]{:S(2)}) copy-start(bf16[2,256,1536]{2,1,0:T(8,128)(2,1)S(1)} %maximum_select_fusion) | copy-start | bytes 4718596
  97.9 2.2 copy-start
  100.1 3.8 %collective-permute-start.5 = (bf16[2,128,3072]{2,1,0:T(8,128)(2,1)}, bf16[2,128,3072]{2,1,0:T(8,128)(2,1)}, u32[]{:S(2)}, u32[]{:S(2)}) collective-permute-start(bf16[2,128,3072]{2,1,0:T(8,128)(2,1)} %fusion.5), channel_id=1, source_target_pairs={{0,8},{8,0},{16,24},{24,16},{1,9},{9,1},{17,25},{25,17},{2,10},{10... | collective-permute-start | bytes 4718600 | tf_op jit(solution)/shard_map/ppermute | solution.py:22
  100.1 1.7 copy-start.6
  101.9 37.5 %collective-permute-start.19 = (bf16[2,128,3072]{2,1,0:T(8,128)(2,1)}, bf16[2,128,3072]{2,1,0:T(8,128)(2,1)}, u32[]{:S(2)}, u32[]{:S(2)}) collective-permute-start(bf16[2,128,3072]{2,1,0:T(8,128)(2,1)} %fusion.42), channel_id=1, source_target_pairs={{0,16},{8,24},{16,0},{24,8},{1,17},{9,25},{17,1},{25,9},{2,18},{10... | collective-permute-start | bytes 4718600 | tf_op jit(solution)/shard_map/ppermute | solution.py:22
  101.9 37.5 %copy-start.7 = (bf16[2,128,3072]{2,1,0:T(8,128)(2,1)S(1)}, bf16[2,128,3072]{2,1,0:T(8,128)(2,1)}, u32[]{:S(2)}) copy-start(bf16[2,128,3072]{2,1,0:T(8,128)(2,1)} %copy-done.6) | copy-start | bytes 4718596
  103.8 35.5 %copy-start.3 = (f32[1,256,3072]{2,1,0:T(8,128)S(1)}, f32[1,256,3072]{2,1,0:T(8,128)}, u32[]{:S(2)}) copy-start(f32[1,256,3072]{2,1,0:T(8,128)} %copy-done.2) | copy-start | bytes 9437188
  103.9 35.5 %copy-start.5 = (f32[1,256,3072]{2,1,0:T(8,128)S(1)}, f32[1,256,3072]{2,1,0:T(8,128)}, u32[]{:S(2)}) copy-start(f32[1,256,3072]{2,1,0:T(8,128)} %copy-done.4) | copy-start | bytes 9437188
  106.3 66.3 %collective-permute-start.6 = (bf16[2,128,3072]{2,1,0:T(8,128)(2,1)S(1)}, bf16[2,128,3072]{2,1,0:T(8,128)(2,1)S(1)}, u32[]{:S(2)}, u32[]{:S(2)}) collective-permute-start(bf16[2,128,3072]{2,1,0:T(8,128)(2,1)S(1)} %fusion.41), channel_id=1, source_target_pairs={{0,16},{8,24},{16,0},{24,8},{1,17},{9,25},{17,1},{25,9},{2,18},{10... | collective-permute-start | bytes 4718600 | tf_op jit(solution)/shard_map/ppermute | solution.py:22
  142.2 30.4 %copy-start.1 = (f32[1,256,3072]{2,1,0:T(8,128)S(1)}, f32[1,256,3072]{2,1,0:T(8,128)}, u32[]{:S(2)}) copy-start(f32[1,256,3072]{2,1,0:T(8,128)} %copy-done) | copy-start | bytes 9437188
  142.4 33.4 %collective-permute-start.20 = (bf16[2,128,3072]{2,1,0:T(8,128)(2,1)S(1)}, bf16[2,128,3072]{2,1,0:T(8,128)(2,1)S(1)}, u32[]{:S(2)}, u32[]{:S(2)}) collective-permute-start(bf16[2,128,3072]{2,1,0:T(8,128)(2,1)S(1)} %pad_maximum_fusion.6), channel_id=1, source_target_pairs={{0,8},{8,0},{16,24},{24,16},{1,9},{9,1},{17,25},{25,17},{2,10},{10... | collective-permute-start | bytes 4718600 | tf_op jit(solution)/shard_map/ppermute | solution.py:22
  172.6 3.5 %slice-start = ((s8[9437184]{0:T(1024)(128)(4,1)}), s8[4194304]{0:T(1024)(128)(4,1)S(1)}, s32[]{:S(2)}) async-start(s8[9437184]{0:T(1024)(128)(4,1)} %bitcast.62), calls=%async_computation | async-start | bytes 8388608
  172.6 3.9 %slice-start.1 = ((s8[9437184]{0:T(1024)(128)(4,1)}), s8[4194304]{0:T(1024)(128)(4,1)S(1)}, s32[]{:S(2)}) async-start(s8[9437184]{0:T(1024)(128)(4,1)} %bitcast.62), calls=%async_computation.1 | async-start | bytes 8388608
  175.6 1.5 slice-start.2
  175.7 9.5 %collective-permute-start.7 = (bf16[2,128,3072]{2,1,0:T(8,128)(2,1)S(1)}, bf16[2,128,3072]{2,1,0:T(8,128)(2,1)S(1)}, u32[]{:S(2)}, u32[]{:S(2)}) collective-permute-start(bf16[2,128,3072]{2,1,0:T(8,128)(2,1)S(1)} %pad_maximum_fusion.5), channel_id=1, source_target_pairs={{0,8},{8,0},{16,24},{24,16},{1,9},{9,1},{17,25},{25,17},{2,10},{10... | collective-permute-start | bytes 4718600 | tf_op jit(solution)/shard_map/ppermute | solution.py:22
  196.4 2.3 copy-start.9
  196.4 2.3 copy-start.11
  196.4 20.5 %collective-permute-start.21 = (bf16[2,256,768]{2,1,0:T(8,128)(2,1)S(1)}, bf16[2,256,768]{2,1,0:T(8,128)(2,1)S(1)}, u32[]{:S(2)}, u32[]{:S(2)}) collective-permute-start(bf16[2,256,768]{2,1,0:T(8,128)(2,1)S(1)} %fusion.28), channel_id=1, source_target_pairs={{0,1},{1,0},{2,3},{3,2},{4,5},{5,4},{6,7},{7,6},{8,9},{9,8},{10,11... | collective-permute-start | bytes 2359304 | tf_op jit(solution)/shard_map/ppermute | solution.py:22
  197.1 35.4 %collective-permute-start.8 = (bf16[2,256,768]{2,1,0:T(8,128)(2,1)S(1)}, bf16[2,256,768]{2,1,0:T(8,128)(2,1)S(1)}, u32[]{:S(2)}, u32[]{:S(2)}) collective-permute-start(bf16[2,256,768]{2,1,0:T(8,128)(2,1)S(1)} %fusion.32), channel_id=1, source_target_pairs={{0,1},{1,0},{2,3},{3,2},{4,5},{5,4},{6,7},{7,6},{8,9},{9,8},{10,11... | collective-permute-start | bytes 2359304 | tf_op jit(solution)/shard_map/ppermute | solution.py:22
  217.2 17.0 %collective-permute-start.22 = (bf16[2,64,768]{2,1,0:T(8,128)(2,1)S(1)}, bf16[2,64,768]{2,1,0:T(8,128)(2,1)S(1)}, u32[]{:S(2)}, u32[]{:S(2)}) collective-permute-start(bf16[2,64,768]{2,1,0:T(8,128)(2,1)S(1)} %get-tuple-element.12), channel_id=1, source_target_pairs={{0,2},{1,3},{2,0},{3,1},{4,6},{5,7},{6,4},{7,5},{8,10},{9,11},{10,... | collective-permute-start | bytes 589832 | tf_op jit(solution)/shard_map/ppermute | solution.py:22
  217.3 19.0 %collective-permute-start.24 = (bf16[2,64,768]{2,1,0:T(8,128)(2,1)S(1)}, bf16[2,64,768]{2,1,0:T(8,128)(2,1)S(1)}, u32[]{:S(2)}, u32[]{:S(2)}) collective-permute-start(bf16[2,64,768]{2,1,0:T(8,128)(2,1)S(1)} %get-tuple-element.13), channel_id=1, source_target_pairs={{0,6},{1,7},{2,4},{3,5},{4,2},{5,3},{6,0},{7,1},{8,14},{9,15},{10,... | collective-permute-start | bytes 589832 | tf_op jit(solution)/shard_map/ppermute | solution.py:22
  218.6 17.8 %collective-permute-start.23 = (bf16[2,64,768]{2,1,0:T(8,128)(2,1)S(1)}, bf16[2,64,768]{2,1,0:T(8,128)(2,1)S(1)}, u32[]{:S(2)}, u32[]{:S(2)}) collective-permute-start(bf16[2,64,768]{2,1,0:T(8,128)(2,1)S(1)} %get-tuple-element.14), channel_id=1, source_target_pairs={{0,4},{1,5},{2,6},{3,7},{4,0},{5,1},{6,2},{7,3},{8,12},{9,13},{10,... | collective-permute-start | bytes 589832 | tf_op jit(solution)/shard_map/ppermute | solution.py:22
  232.8 10.9 %collective-permute-start.9 = (bf16[2,64,768]{2,1,0:T(8,128)(2,1)S(1)}, bf16[2,64,768]{2,1,0:T(8,128)(2,1)S(1)}, u32[]{:S(2)}, u32[]{:S(2)}) collective-permute-start(bf16[2,64,768]{2,1,0:T(8,128)(2,1)S(1)} %get-tuple-element.15), channel_id=1, source_target_pairs={{0,2},{1,3},{2,0},{3,1},{4,6},{5,7},{6,4},{7,5},{8,10},{9,11},{10,... | collective-permute-start | bytes 589832 | tf_op jit(solution)/shard_map/ppermute | solution.py:22
  232.8 11.3 %collective-permute-start.11 = (bf16[2,64,768]{2,1,0:T(8,128)(2,1)S(1)}, bf16[2,64,768]{2,1,0:T(8,128)(2,1)S(1)}, u32[]{:S(2)}, u32[]{:S(2)}) collective-permute-start(bf16[2,64,768]{2,1,0:T(8,128)(2,1)S(1)} %get-tuple-element.16), channel_id=1, source_target_pairs={{0,6},{1,7},{2,4},{3,5},{4,2},{5,3},{6,0},{7,1},{8,14},{9,15},{10,... | collective-permute-start | bytes 589832 | tf_op jit(solution)/shard_map/ppermute | solution.py:22
  234.2 18.1 %collective-permute-start.10 = (bf16[2,64,768]{2,1,0:T(8,128)(2,1)S(1)}, bf16[2,64,768]{2,1,0:T(8,128)(2,1)S(1)}, u32[]{:S(2)}, u32[]{:S(2)}) collective-permute-start(bf16[2,64,768]{2,1,0:T(8,128)(2,1)S(1)} %get-tuple-element.17), channel_id=1, source_target_pairs={{0,4},{1,5},{2,6},{3,7},{4,0},{5,1},{6,2},{7,3},{8,12},{9,13},{10,... | collective-permute-start | bytes 589832 | tf_op jit(solution)/shard_map/ppermute | solution.py:22
  236.4 32.8 %collective-permute-start.25 = (bf16[2,64,768]{2,1,0:T(8,128)(2,1)S(1)}, bf16[2,64,768]{2,1,0:T(8,128)(2,1)S(1)}, u32[]{:S(2)}, u32[]{:S(2)}) collective-permute-start(bf16[2,64,768]{2,1,0:T(8,128)(2,1)S(1)} %add_convert_fusion), channel_id=1, source_target_pairs={{0,0},{1,1},{2,8},{3,9},{4,16},{5,17},{6,24},{7,25},{8,2},{9,3},{1... | collective-permute-start | bytes 589832 | tf_op jit(solution)/shard_map/ppermute | solution.py:30
  252.4 16.8 %collective-permute-start.12 = (bf16[2,64,768]{2,1,0:T(8,128)(2,1)S(1)}, bf16[2,64,768]{2,1,0:T(8,128)(2,1)S(1)}, u32[]{:S(2)}, u32[]{:S(2)}) collective-permute-start(bf16[2,64,768]{2,1,0:T(8,128)(2,1)S(1)} %add_convert_fusion.1), channel_id=1, source_target_pairs={{0,0},{1,1},{2,8},{3,9},{4,16},{5,17},{6,24},{7,25},{8,2},{9,3},{1... | collective-permute-start | bytes 589832 | tf_op jit(solution)/shard_map/ppermute | solution.py:30

commit v2 on v0

v2 whole, which is shorter than its diff:
```python
import functools

import jax
import jax.numpy as jnp
from jax import lax
from jax.experimental import pallas as pl
from jax.experimental.pallas import tpu as pltpu
from jax.sharding import PartitionSpec as P

SHARES = (2, 2, 2, 2)
ORDER = (
    0, 1, 0, 1, 0, 2, 1, 0, 2, 3, 1, 2, 0, 2, 0, 3, 1, 3, 2, 1, 3, 0, 2, 0, 3, 1, 0, 3, 1, 0, 2, 0, 1, 2, 1, 3, 1, 3,
    2, -1, 3, 0, 2, 3, 2, 1, 3, -1, 3, 2,
)


def cdf_of(value):
    return 0.5 * (1.0 + lax.erf(value * 0.7071067811865476))


def contract(left, right, left_dim, right_dim):
    return lax.dot_general(
        left, right, (((left_dim,), (right_dim,)), ((), ())), preferred_element_type=jnp.float32
    )


def swap(value, axis, size, mask):
    return lax.ppermute(value, axis, [(i, i ^ mask) for i in range(size)])


def transposed(value, rows, cols):
    per = cols // rows
    pairs = [
        (r * cols + c, (c // per) * cols + r * per + c % per) for r in range(rows) for c in range(cols)
    ]
    return lax.ppermute(value, ("row", "col"), pairs)


def fetch_kernel(*refs):
    count = len(refs) // 2
    copies = [pltpu.make_async_copy(refs[i], refs[count + i], refs[-1].at[i]) for i in range(count)]
    for copy in copies:
        copy.start()
    for copy in copies:
        copy.wait()


def fetched(*arrays):
    size = sum(a.size * a.dtype.itemsize for a in arrays)
    return pl.pallas_call(
        fetch_kernel,
        out_shape=[jax.ShapeDtypeStruct(a.shape, a.dtype) for a in arrays],
        in_specs=[pl.BlockSpec(memory_space=pltpu.HBM)] * len(arrays),
        out_specs=[pl.BlockSpec(memory_space=pltpu.VMEM)] * len(arrays),
        scratch_shapes=[pltpu.SemaphoreType.DMA((len(arrays),))],
        compiler_params=pltpu.CompilerParams(vmem_limit_bytes=size + (2 << 20)),
        cost_estimate=pl.CostEstimate(flops=0, bytes_accessed=2 * size, transcendentals=0),
    )(*arrays)


class Clock:
    def __init__(self, on):
        self.on, self.last = on, None

    def start(self, value):
        if not self.on or self.last is None:
            return value
        return lax.optimization_barrier((value, self.last))[0]

    def end(self, value):
        self.last = value
        return value


class Grid:
    def __init__(self, rows, cols, clock):
        self.rows, self.cols, self.clock = rows, cols, clock
        self.core, self.y = lax.axis_index("row") % 2, lax.axis_index("col") % 2

    def gather(self, block):
        clock = self.clock
        block = clock.end(clock.start(block))
        block = transposed(block, self.rows, self.cols)
        yield
        block = clock.end(clock.start(block))
        far = swap(block, "col", self.cols, 4)
        yield
        near = clock.end(jnp.concatenate([block, clock.start(far)], axis=1))
        far = swap(near, "col", self.cols, 2)
        yield
        far = clock.start(far)
        mine = jnp.where(
            self.core == 0,
            jnp.concatenate([near, far], axis=1),
            jnp.concatenate([far, near], axis=1),
        )
        mine = clock.end(mine)
        other = swap(mine, "col", self.cols, 1)
        yield
        other = clock.start(other)
        return jnp.where(
            self.y == 0,
            jnp.concatenate([mine, other], axis=2),
            jnp.concatenate([other, mine], axis=2),
        )

    def scatter(self, terms):
        clock = self.clock
        f, n = terms.shape[2] // 2, terms.shape[1] // 4
        away = lax.dynamic_slice_in_dim(terms, (1 - self.y) * f, f, axis=2).astype(jnp.bfloat16)
        away = clock.end(away)
        keep = lax.dynamic_slice_in_dim(terms, self.y * f, f, axis=2)
        got = swap(away, "col", self.cols, 1)
        yield
        total = keep + clock.start(got)
        away = lax.dynamic_slice_in_dim(total, (1 - self.core) * 2 * n, 2 * n, axis=1)
        away = clock.end(away.astype(jnp.bfloat16))
        keep = lax.dynamic_slice_in_dim(total, self.core * 2 * n, 2 * n, axis=1)
        got = swap(away, "col", self.cols, 2)
        yield
        total = keep + clock.start(got)
        away = clock.end(total[:, n:].astype(jnp.bfloat16))
        got = swap(away, "col", self.cols, 4)
        yield
        out = clock.end((total[:, :n] + clock.start(got)).astype(jnp.bfloat16))
        out = transposed(out, self.rows, self.cols)
        yield
        return clock.end(clock.start(out))


class Plain:
    def __init__(self, rows, cols, clock):
        self.rows, self.cols, self.per = rows, cols, cols // rows
        self.core = lax.axis_index("row") % 2

    def gather(self, block):
        two, n, f = block.shape
        whole = lax.all_gather(transposed(block, self.rows, self.cols), "col", axis=0)
        yield
        whole = whole.reshape(self.rows, self.per, two, n, f).transpose(2, 0, 3, 1, 4)
        whole = whole.reshape(two, self.rows * n, self.per * f)
        return jnp.where(self.core == 0, whole, jnp.roll(whole, self.rows * n // 2, axis=1))

    def scatter(self, terms):
        two, all_n, all_f = terms.shape
        n, f = all_n // self.rows, all_f // self.per
        terms = jnp.where(self.core == 0, terms, jnp.roll(terms, all_n // 2, axis=1))
        terms = terms.reshape(two, self.rows, n, self.per, f).transpose(1, 3, 0, 2, 4)
        total = lax.psum_scatter(terms.reshape(self.cols, two, n, f), "col", scatter_dimension=0)
        yield
        return transposed(total.astype(jnp.bfloat16), self.rows, self.cols)


def part_steps(grid, clock, rows, weights, block, made):
    panel = yield from grid.gather(block)
    weight_in, weight_out = weights
    half = panel.shape[1] // 2
    terms = jnp.stack([contract(panel[0], weight_in, 1, 0), contract(panel[1], weight_out, 1, 1)])
    away = clock.end(terms[:, half:].astype(jnp.bfloat16))
    got = swap(away, "row", rows, 1)
    yield
    sums = terms[:, :half] + clock.start(got)
    got = swap(clock.end(sums.astype(jnp.bfloat16)), "row", rows, 2)
    yield
    sums = sums + clock.start(got)
    hidden_pre, grad_act = sums[0], sums[1]
    cumul = cdf_of(hidden_pre)
    density = jnp.exp(-0.5 * hidden_pre * hidden_pre) * 0.3989422804014327
    act = (hidden_pre * cumul).astype(jnp.bfloat16)
    grad_pre = (grad_act * (cumul + hidden_pre * density)).astype(jnp.bfloat16)
    own = clock.end(jnp.stack([act, grad_pre]))
    got = swap(own, "row", rows, 1)
    yield
    full = jnp.concatenate([own, clock.start(got)], axis=1)
    made["panel"], made["full"] = panel, full
    terms = jnp.stack([contract(full[0], weight_out, 1, 0), contract(full[1], weight_in, 1, 1)])
    made["out"] = yield from grid.scatter(terms)


def body(rows, cols, tokens, weight_in, weight_out, out_grad):
    special = (rows, cols) == (4, 8)
    clock = Clock(special)
    grid = (Grid if special else Plain)(rows, cols, clock)
    both = jnp.stack([tokens, out_grad])
    weights = [weight_in, weight_out]
    parts, made = [], []
    first = 0
    for share in SHARES:
        n = tokens.shape[0] * share // sum(SHARES)
        made.append({})
        parts.append(part_steps(grid, clock, rows, weights, both[:, first : first + n], made[-1]))
        first += n

    def weight_gradient(of_in):
        panel = jnp.concatenate([m["panel"] for m in made], axis=1)
        full = jnp.concatenate([m["full"] for m in made], axis=1)
        if of_in:
            out = contract(panel[0], clock.start(full[1]), 0, 0)
        else:
            out = contract(clock.start(full[0]), panel[1], 0, 0)
        return clock.end(out.astype(jnp.bfloat16))

    grads = []
    if special:
        for count, part in enumerate(ORDER):
            if count == 1:
                weights[:] = fetched(clock.start(weight_in), weight_out)
                clock.end(weights[1])
            if part < 0:
                grads.append(weight_gradient(not grads))
            else:
                next(parts[part], None)
    else:
        for part in parts:
            for _ in part:
                pass
        grads = [weight_gradient(True), weight_gradient(False)]
    out = jnp.concatenate([m["out"] for m in made], axis=1)
    return out[0], out[1], grads[0], grads[1]


def solution(mesh):
    return jax.shard_map(
        functools.partial(body, mesh.shape["row"], mesh.shape["col"]),
        mesh=mesh,
        in_specs=(P("row", "col"), P("row", "col"), P("col", "row"), P("row", "col")),
        out_specs=(P("row", "col"), P("row", "col"), P("row", "col"), P("col", "row")),
        check_vma=False,
    )
```

time: 813 us -> 251 us (0.31)
  the two profiles are of different devices: /device:TPU:2 before, /device:TPU:3 now
where the time goes in v2:
time: 251 us; the launch traced here: 246 us
  starting transfers between devices  71.1 us (28%)
  matrix products  60.5 us (24%)
  waiting for transfers between devices  40.4 us (16%)
  other arithmetic  36.1 us (14%)
  local copies, waits for them, and re-layouts  31.5 us (13%)
  Pallas kernels  4.32 us (2%)
    dot_general x18, matrix products, contract(): lax.dot_general(left, right, (((left_dim,), (right_dim,)), ((), ())), pre...  60.5 us
    ppermute x36, starting transfers between devices, swap(): return lax.ppermute(value, axis, [(i, i ^ mask) for i in range(size)])  36.4 us
    ppermute x8, starting transfers between devices, transposed(): return lax.ppermute(value, ('row', 'col'), pairs)  34.6 us
    ppermute x36, waiting for transfers between devices, swap(): return lax.ppermute(value, axis, [(i, i ^ mask) for i in range(size)])  29.4 us
    unnamed x114, local copies, waits for them, and re-layouts  23.9 us
    ppermute x8, waiting for transfers between devices, transposed(): return lax.ppermute(value, ('row', 'col'), pairs)  11 us
    convert_element_type x4, other arithmetic, part_steps(): got = swap(clock.end(sums.astype(jnp.bfloat16)), 'row', rows, 2)  7.05 us
    add x4, other arithmetic, part_steps(): sums = sums + clock.start(got)  6.01 us
  transfers between devices with their start and end apart: 44, of which 12 were waited for; matrix products, arithmetic and copies ran while one was open for 37% of the time, Pallas kernels for 2%

profile of v2, /device:TPU:3, one launch (start us, length us, event | category | flops | bytes accessed | tf_op | source)
XLA Modules:
  0.0 245.8 jit_solution(13738510342637424580)
XLA Ops:
  1.6 5.8 %collective-permute-start = (bf16[2,32,768]{2,1,0:T(8,128)(2,1)S(1)}, bf16[2,32,768]{2,1,0:T(8,128)(2,1)S(1)}, u32[]{:S(2)}, u32[]{:S(2)}) collective-permute-start(bf16[2,32,768]{2,1,0:T(8,128)(2,1)S(1)} %get-tuple-element.129), channel_id=1, source_target_pairs={{0,0},{1,1},{2,8},{3,9},{4,16},{5,17},{6,24},{7,25},{8,2},{9,3},{1... | collective-permute-start | bytes 294920 | tf_op jit(solution)/shard_map/ppermute | solution.py:36
  7.4 3.7 %copy-done.3 = bf16[1536,3072]{1,0:T(8,128)(2,1)S(1)} copy-done((bf16[1536,3072]{1,0:T(8,128)(2,1)S(1)}, bf16[1536,3072]{1,0:T(8,128)(2,1)}, u32[]{:S(2)}) %copy-start.3) | copy-done | bytes 9437208
  11.1 4.3 %shard_map.75 = (bf16[1536,3072]{1,0:T(8,128)(2,1)S(1)}, bf16[3072,1536]{1,0:T(8,128)(2,1)S(1)}) custom-call(bf16[1536,3072]{1,0:T(8,128)(2,1)S(1)} %copy-done.3, bf16[3072,1536]{1,0:T(8,128)(2,1)} %refs_1_.1), custom_call_target="tpu_custom_call" | custom-call | bytes 37748736 | tf_op jit(solution)/shard_map/pallas_call | solution.py:50
  15.4 3.7 %copy-done = bf16[3072,1536]{1,0:T(8,128)(2,1)} copy-done((bf16[3072,1536]{1,0:T(8,128)(2,1)}, bf16[3072,1536]{1,0:T(8,128)(2,1)S(1)}, u32[]{:S(2)}) %copy-start) | copy-done | bytes 9437208
  19.2 3.7 %copy-done.1 = bf16[1536,3072]{1,0:T(8,128)(2,1)} copy-done((bf16[1536,3072]{1,0:T(8,128)(2,1)}, bf16[1536,3072]{1,0:T(8,128)(2,1)S(1)}, u32[]{:S(2)}) %copy-start.1) | copy-done | bytes 9437208
  22.9 2.5 %collective-permute-start.2 = (bf16[2,32,768]{2,1,0:T(8,128)(2,1)S(1)}, bf16[2,32,768]{2,1,0:T(8,128)(2,1)S(1)}, u32[]{:S(2)}, u32[]{:S(2)}) collective-permute-start(bf16[2,32,768]{2,1,0:T(8,128)(2,1)S(1)} %get-tuple-element.58), channel_id=1, source_target_pairs={{0,0},{1,1},{2,8},{3,9},{4,16},{5,17},{6,24},{7,25},{8,2},{9,3},{1... | collective-permute-start | bytes 294920 | tf_op jit(solution)/shard_map/ppermute | solution.py:36
  25.5 6.2 %collective-permute-done.2 = bf16[2,32,768]{2,1,0:T(8,128)(2,1)S(1)} collective-permute-done((bf16[2,32,768]{2,1,0:T(8,128)(2,1)S(1)}, bf16[2,32,768]{2,1,0:T(8,128)(2,1)S(1)}, u32[]{:S(2)}, u32[]{:S(2)}) %collective-permute-start.2) | collective-permute-done | bytes 98336 | tf_op jit(solution)/shard_map/ppermute | solution.py:36
  32.9 2.2 collective-permute-start.3
  35.1 3.1 %collective-permute-done.4 = bf16[2,32,768]{2,1,0:T(8,128)(2,1)S(1)} collective-permute-done((bf16[2,32,768]{2,1,0:T(8,128)(2,1)S(1)}, bf16[2,32,768]{2,1,0:T(8,128)(2,1)S(1)}, u32[]{:S(2)}, u32[]{:S(2)}) %collective-permute-start.4) | collective-permute-done | bytes 98336 | tf_op jit(solution)/shard_map/ppermute | solution.py:28
  38.3 5.4 %collective-permute-start.6 = (bf16[2,32,768]{2,1,0:T(8,128)(2,1)S(1)}, bf16[2,32,768]{2,1,0:T(8,128)(2,1)S(1)}, u32[]{:S(2)}, u32[]{:S(2)}) collective-permute-start(bf16[2,32,768]{2,1,0:T(8,128)(2,1)S(1)} %get-tuple-element.62), channel_id=1, source_target_pairs={{0,0},{1,1},{2,8},{3,9},{4,16},{5,17},{6,24},{7,25},{8,2},{9,3},{1... | collective-permute-start | bytes 294920 | tf_op jit(solution)/shard_map/ppermute | solution.py:36
  45.1 4.3 %collective-permute-done.6 = bf16[2,32,768]{2,1,0:T(8,128)(2,1)S(1)} collective-permute-done((bf16[2,32,768]{2,1,0:T(8,128)(2,1)S(1)}, bf16[2,32,768]{2,1,0:T(8,128)(2,1)S(1)}, u32[]{:S(2)}, u32[]{:S(2)}) %collective-permute-start.6) | collective-permute-done | bytes 98336 | tf_op jit(solution)/shard_map/ppermute | solution.py:36
  50.7 4.1 %collective-permute-done.7 = bf16[2,32,768]{2,1,0:T(8,128)(2,1)S(1)} collective-permute-done((bf16[2,32,768]{2,1,0:T(8,128)(2,1)S(1)}, bf16[2,32,768]{2,1,0:T(8,128)(2,1)S(1)}, u32[]{:S(2)}, u32[]{:S(2)}) %collective-permute-start.7) | collective-permute-done | bytes 98336 | tf_op jit(solution)/shard_map/ppermute | solution.py:28
  55.1 6.9 %convolution_bitcast_fusion.6 = f32[1,128,3072]{2,1,0:T(8,128)S(1)} fusion(bf16[3072,1536]{1,0:T(8,128)(2,1)} %copy-done, bf16[2,128,1536]{2,1,0:T(8,128)(2,1)S(1)} %maximum_select_fusion), kind=kOutput, calls=%fused_computation.8 | convolution fusion | flops 1207959552 | bytes 11403264 | tf_op jit(solution)/shard_map/dot_general | solution.py:22
  63.6 3.7 %collective-permute-start.9 = (bf16[2,64,3072]{2,1,0:T(8,128)(2,1)S(1)}, bf16[2,64,3072]{2,1,0:T(8,128)(2,1)S(1)}, u32[]{:S(2)}, u32[]{:S(2)}) collective-permute-start(bf16[2,64,3072]{2,1,0:T(8,128)(2,1)S(1)} %fusion.11), channel_id=1, source_target_pairs={{0,8},{8,0},{16,24},{24,16},{1,9},{9,1},{17,25},{25,17},{2,10},{10... | collective-permute-start | bytes 2359304 | tf_op jit(solution)/shard_map/ppermute | solution.py:28
  67.3 3.2 %collective-permute-start.12 = (bf16[2,32,768]{2,1,0:T(8,128)(2,1)S(1)}, bf16[2,32,768]{2,1,0:T(8,128)(2,1)S(1)}, u32[]{:S(2)}, u32[]{:S(2)}) collective-permute-start(bf16[2,32,768]{2,1,0:T(8,128)(2,1)S(1)} %get-tuple-element.66), channel_id=1, source_target_pairs={{0,0},{1,1},{2,8},{3,9},{4,16},{5,17},{6,24},{7,25},{8,2},{9,3},{1... | collective-permute-start | bytes 294920 | tf_op jit(solution)/shard_map/ppermute | solution.py:36
  71.8 2.0 collective-permute-done.10
  76.8 3.8 %collective-permute-done.14 = bf16[2,128,768]{2,1,0:T(8,128)(2,1)S(1)} collective-permute-done((bf16[2,128,768]{2,1,0:T(8,128)(2,1)S(1)}, bf16[2,128,768]{2,1,0:T(8,128)(2,1)S(1)}, u32[]{:S(2)}, u32[]{:S(2)}) %collective-permute-start.14) | collective-permute-done | bytes 393248 | tf_op jit(solution)/shard_map/ppermute | solution.py:28
  80.8 3.1 %convolution_bitcast_fusion.4 = f32[1,128,3072]{2,1,0:T(8,128)S(1)} fusion(bf16[3072,1536]{1,0:T(8,128)(2,1)S(1)} %bitcast.115, bf16[2,128,1536]{2,1,0:T(8,128)(2,1)S(1)} %maximum_select_fusion.1), kind=kOutput, calls=%fused_computation.6 | convolution fusion | flops 1207959552 | bytes 11403264 | tf_op jit(solution)/shard_map/dot_general | solution.py:22
  86.5 2.4 collective-permute-start.11
  89.9 2.0 collective-permute-start.16
  94.4 3.1 %convolution_bitcast_fusion.2 = f32[1,128,3072]{2,1,0:T(8,128)S(1)} fusion(bf16[3072,1536]{1,0:T(8,128)(2,1)S(1)} %bitcast.115, bf16[2,128,1536]{2,1,0:T(8,128)(2,1)S(1)} %maximum_select_fusion.2), kind=kOutput, calls=%fused_computation.4 | convolution fusion | flops 1207959552 | bytes 11403264 | tf_op jit(solution)/shard_map/dot_general | solution.py:22
  101.3 2.3 fusion.59
  103.6 1.9 maximum_select_fusion.7
  109.4 2.2 collective-permute-start.18
  112.8 1.5 collective-permute-start.21
  114.3 2.4 fusion.60
  118.2 7.1 %convolution_bitcast_fusion.14 = f32[1,128,1536]{2,1,0:T(8,128)S(1)} fusion(bf16[1536,3072]{1,0:T(8,128)(2,1)} %copy-done.1, bf16[2,128,3072]{2,1,0:T(8,128)(2,1)S(1)} %pad_maximum_fusion.5), kind=kOutput, calls=%fused_computation.27 | convolution fusion | flops 1207959552 | bytes 11010048 | tf_op jit(solution)/shard_map/dot_general | solution.py:22
  125.4 1.6 convolution_bitcast_fusion.15
  129.4 3.1 %convolution_bitcast_fusion = f32[1,128,3072]{2,1,0:T(8,128)S(1)} fusion(bf16[3072,1536]{1,0:T(8,128)(2,1)S(1)} %bitcast.117, bf16[2,128,1536]{2,1,0:T(8,128)(2,1)S(1)} %maximum_select_fusion.3), kind=kOutput, calls=%fused_computation.2 | convolution fusion | flops 1207959552 | bytes 11403264 | tf_op jit(solution)/shard_map/dot_general | solution.py:22
  136.4 1.6 convert_add_fusion.2
  138.4 2.1 constant_dynamic-update-slice_fusion.14
  147.6 4.1 %convolution_bitcast_fusion.12 = f32[1,128,1536]{2,1,0:T(8,128)} fusion(bf16[1536,3072]{1,0:T(8,128)(2,1)S(1)} %bitcast.119, bf16[2,128,3072]{2,1,0:T(8,128)(2,1)S(1)} %pad_maximum_fusion.6), kind=kOutput, calls=%fused_computation.25 | convolution fusion | flops 1207959552 | bytes 11010048 | tf_op jit(solution)/shard_map/dot_general | solution.py:22
  154.6 1.6 convert_add_fusion.1
  162.2 6.2 %collective-permute-done.26 = bf16[2,32,768]{2,1,0:T(8,128)(2,1)S(1)} collective-permute-done((bf16[2,32,768]{2,1,0:T(8,128)(2,1)S(1)}, bf16[2,32,768]{2,1,0:T(8,128)(2,1)S(1)}, u32[]{:S(2)}, u32[]{:S(2)}) %collective-permute-start.26) | collective-permute-done | bytes 98336 | tf_op jit(solution)/shard_map/ppermute | solution.py:28
  169.1 2.0 collective-permute-done.30
  173.4 3.6 %convolution_bitcast_fusion.10 = f32[1,128,1536]{2,1,0:T(8,128)S(1)} fusion(bf16[1536,3072]{1,0:T(8,128)(2,1)S(1)} %bitcast.119, bf16[2,128,3072]{2,1,0:T(8,128)(2,1)S(1)} %pad_maximum_fusion.7), kind=kOutput, calls=%fused_computation.23 | convolution fusion | flops 1207959552 | bytes 11010048 | tf_op jit(solution)/shard_map/dot_general | solution.py:22
  180.3 1.4 convert_add_fusion
  185.8 2.2 collective-permute-start.34
  188.0 1.8 pad_maximum_fusion
  189.7 4.3 %collective-permute-start.28 = (bf16[2,32,768]{2,1,0:T(8,128)(2,1)}, bf16[2,32,768]{2,1,0:T(8,128)(2,1)S(1)}, u32[]{:S(2)}, u32[]{:S(2)}) collective-permute-start(bf16[2,32,768]{2,1,0:T(8,128)(2,1)} %fusion.55), channel_id=1, source_target_pairs={{0,0},{1,1},{2,8},{3,9},{4,16},{5,17},{6,24},{7,25},{8,2},{9,3},{1... | collective-permute-start | bytes 294920 | tf_op jit(solution)/shard_map/ppermute | solution.py:36
  195.8 4.0 %collective-permute-start.37 = (bf16[2,32,768]{2,1,0:T(8,128)(2,1)}, bf16[2,32,768]{2,1,0:T(8,128)(2,1)S(1)}, u32[]{:S(2)}, u32[]{:S(2)}) collective-permute-start(bf16[2,32,768]{2,1,0:T(8,128)(2,1)} %fusion.54), channel_id=1, source_target_pairs={{0,0},{1,1},{2,8},{3,9},{4,16},{5,17},{6,24},{7,25},{8,2},{9,3},{1... | collective-permute-start | bytes 294920 | tf_op jit(solution)/shard_map/ppermute | solution.py:36
  200.0 3.2 %convolution_bitcast_fusion.8 = f32[1,128,1536]{2,1,0:T(8,128)S(1)} fusion(bf16[1536,3072]{1,0:T(8,128)(2,1)S(1)} %bitcast.119, bf16[2,128,3072]{2,1,0:T(8,128)(2,1)S(1)} %pad_maximum_fusion.8), kind=kOutput, calls=%fused_computation.21 | convolution fusion | flops 1207959552 | bytes 11010048 | tf_op jit(solution)/shard_map/dot_general | solution.py:22
  207.8 3.4 %slice_bitcast_fusion = (bf16[512,3072]{1,0:T(8,128)(2,1)S(1)}, bf16[512,3072]{1,0:T(8,128)(2,1)S(1)}) fusion(bf16[2,512,3072]{2,1,0:T(8,128)(2,1)} %constant_dynamic-update-slice_fusion.8), kind=kLoop, calls=%fused_computation.10 | loop fusion | bytes 12582912 | tf_op jit(solution)/shard_map/squeeze | solution.py:200
  211.5 7.5 %convolution_convert_fusion.1 = bf16[1536,3072]{1,0:T(8,128)(2,1)} fusion(bf16[512,3072]{1,0:T(8,128)(2,1)S(1)} %get-tuple-element.97, bf16[2,512,1536]{2,1,0:T(8,128)(2,1)S(1)} %copy-done.31), kind=kOutput, calls=%fused_computation.1 | convolution fusion | flops 4836556800 | bytes 14155776 | tf_op jit(solution)/shard_map/dot_general | solution.py:22
  220.6 5.6 %collective-permute-done.40 = bf16[2,64,768]{2,1,0:T(8,128)(2,1)S(1)} collective-permute-done((bf16[2,64,768]{2,1,0:T(8,128)(2,1)S(1)}, bf16[2,64,768]{2,1,0:T(8,128)(2,1)S(1)}, u32[]{:S(2)}, u32[]{:S(2)}) %collective-permute-start.40) | collective-permute-done | bytes 196640 | tf_op jit(solution)/shard_map/ppermute | solution.py:28
  227.7 6.4 %collective-permute-start.41 = (bf16[2,32,768]{2,1,0:T(8,128)(2,1)S(1)}, bf16[2,32,768]{2,1,0:T(8,128)(2,1)S(1)}, u32[]{:S(2)}, u32[]{:S(2)}) collective-permute-start(bf16[2,32,768]{2,1,0:T(8,128)(2,1)S(1)} %fusion.53), channel_id=1, source_target_pairs={{0,0},{1,1},{2,8},{3,9},{4,16},{5,17},{6,24},{7,25},{8,2},{9,3},{1... | collective-permute-start | bytes 294920 | tf_op jit(solution)/shard_map/ppermute | solution.py:36
  234.2 3.0 %collective-permute-start.43 = (bf16[2,32,768]{2,1,0:T(8,128)(2,1)S(1)}, bf16[2,32,768]{2,1,0:T(8,128)(2,1)S(1)}, u32[]{:S(2)}, u32[]{:S(2)}) collective-permute-start(bf16[2,32,768]{2,1,0:T(8,128)(2,1)S(1)} %fusion.52), channel_id=1, source_target_pairs={{0,0},{1,1},{2,8},{3,9},{4,16},{5,17},{6,24},{7,25},{8,2},{9,3},{1... | collective-permute-start | bytes 294920 | tf_op jit(solution)/shard_map/ppermute | solution.py:36
  237.2 7.6 %convolution_convert_fusion = bf16[3072,1536]{1,0:T(8,128)(2,1)} fusion(bf16[512,3072]{1,0:T(8,128)(2,1)S(1)} %get-tuple-element.105, bf16[2,512,1536]{2,1,0:T(8,128)(2,1)S(1)} %copy-done.31), kind=kOutput, calls=%fused_computation | convolution fusion | flops 4836556800 | bytes 14155776 | tf_op jit(solution)/shard_map/dot_general | solution.py:22
  (242 shorter events, 71.0 us)
Async XLA Ops:
  1.6 23.8 %collective-permute-start = (bf16[2,32,768]{2,1,0:T(8,128)(2,1)S(1)}, bf16[2,32,768]{2,1,0:T(8,128)(2,1)S(1)}, u32[]{:S(2)}, u32[]{:S(2)}) collective-permute-start(bf16[2,32,768]{2,1,0:T(8,128)(2,1)S(1)} %get-tuple-element.129), channel_id=1, source_target_pairs={{0,0},{1,1},{2,8},{3,9},{4,16},{5,17},{6,24},{7,25},{8,2},{9,3},{1... | collective-permute-start | bytes 294920 | tf_op jit(solution)/shard_map/ppermute | solution.py:36
  22.9 8.8 %collective-permute-start.2 = (bf16[2,32,768]{2,1,0:T(8,128)(2,1)S(1)}, bf16[2,32,768]{2,1,0:T(8,128)(2,1)S(1)}, u32[]{:S(2)}, u32[]{:S(2)}) collective-permute-start(bf16[2,32,768]{2,1,0:T(8,128)(2,1)S(1)} %get-tuple-element.58), channel_id=1, source_target_pairs={{0,0},{1,1},{2,8},{3,9},{4,16},{5,17},{6,24},{7,25},{8,2},{9,3},{1... | collective-permute-start | bytes 294920 | tf_op jit(solution)/shard_map/ppermute | solution.py:36
  25.4 7.5 %collective-permute-start.1 = (bf16[2,32,768]{2,1,0:T(8,128)(2,1)S(1)}, bf16[2,32,768]{2,1,0:T(8,128)(2,1)S(1)}, u32[]{:S(2)}, u32[]{:S(2)}) collective-permute-start(bf16[2,32,768]{2,1,0:T(8,128)(2,1)S(1)} %collective-permute-done), channel_id=1, source_target_pairs={{0,4},{1,5},{2,6},{3,7},{4,0},{5,1},{6,2},{7,3},{8,12},{9,13},{10,... | collective-permute-start | bytes 294920 | tf_op jit(solution)/shard_map/ppermute | solution.py:28
  31.7 6.5 %collective-permute-start.4 = (bf16[2,32,768]{2,1,0:T(8,128)(2,1)S(1)}, bf16[2,32,768]{2,1,0:T(8,128)(2,1)S(1)}, u32[]{:S(2)}, u32[]{:S(2)}) collective-permute-start(bf16[2,32,768]{2,1,0:T(8,128)(2,1)S(1)} %collective-permute-done.2), channel_id=1, source_target_pairs={{0,4},{1,5},{2,6},{3,7},{4,0},{5,1},{6,2},{7,3},{8,12},{9,13},{10,... | collective-permute-start | bytes 294920 | tf_op jit(solution)/shard_map/ppermute | solution.py:28
  32.9 10.8 %collective-permute-start.3 = (bf16[2,64,768]{2,1,0:T(8,128)(2,1)S(1)}, bf16[2,64,768]{2,1,0:T(8,128)(2,1)S(1)}, u32[]{:S(2)}, u32[]{:S(2)}) collective-permute-start(bf16[2,64,768]{2,1,0:T(8,128)(2,1)S(1)} %constant_dynamic-update-slice_fusion), channel_id=1, source_target_pairs={{0,2},{1,3},{2,0},{3,1},{4,6},{5,7},{6,4},{7,5},{8,10},{9,11},{10,... | collective-permute-start | bytes 589832 | tf_op jit(solution)/shard_map/ppermute | solution.py:28
  38.2 12.4 %collective-permute-start.8 = (bf16[2,64,768]{2,1,0:T(8,128)(2,1)S(1)}, bf16[2,64,768]{2,1,0:T(8,128)(2,1)S(1)}, u32[]{:S(2)}, u32[]{:S(2)}) collective-permute-start(bf16[2,64,768]{2,1,0:T(8,128)(2,1)S(1)} %constant_dynamic-update-slice_fusion.2), channel_id=1, source_target_pairs={{0,2},{1,3},{2,0},{3,1},{4,6},{5,7},{6,4},{7,5},{8,10},{9,11},{10,... | collective-permute-start | bytes 589832 | tf_op jit(solution)/shard_map/ppermute | solution.py:28
  38.3 11.1 %collective-permute-start.6 = (bf16[2,32,768]{2,1,0:T(8,128)(2,1)S(1)}, bf16[2,32,768]{2,1,0:T(8,128)(2,1)S(1)}, u32[]{:S(2)}, u32[]{:S(2)}) collective-permute-start(bf16[2,32,768]{2,1,0:T(8,128)(2,1)S(1)} %get-tuple-element.62), channel_id=1, source_target_pairs={{0,0},{1,1},{2,8},{3,9},{4,16},{5,17},{6,24},{7,25},{8,2},{9,3},{1... | collective-permute-start | bytes 294920 | tf_op jit(solution)/shard_map/ppermute | solution.py:36
  43.8 11.1 %collective-permute-start.5 = (bf16[2,128,768]{2,1,0:T(8,128)(2,1)S(1)}, bf16[2,128,768]{2,1,0:T(8,128)(2,1)S(1)}, u32[]{:S(2)}, u32[]{:S(2)}) collective-permute-start(bf16[2,128,768]{2,1,0:T(8,128)(2,1)S(1)} %maximum_select_fusion.4), channel_id=1, source_target_pairs={{0,1},{1,0},{2,3},{3,2},{4,5},{5,4},{6,7},{7,6},{8,9},{9,8},{10,11... | collective-permute-start | bytes 1179656 | tf_op jit(solution)/shard_map/ppermute | solution.py:28
  49.4 5.4 %collective-permute-start.7 = (bf16[2,32,768]{2,1,0:T(8,128)(2,1)S(1)}, bf16[2,32,768]{2,1,0:T(8,128)(2,1)S(1)}, u32[]{:S(2)}, u32[]{:S(2)}) collective-permute-start(bf16[2,32,768]{2,1,0:T(8,128)(2,1)S(1)} %collective-permute-done.6), channel_id=1, source_target_pairs={{0,4},{1,5},{2,6},{3,7},{4,0},{5,1},{6,2},{7,3},{8,12},{9,13},{10,... | collective-permute-start | bytes 294920 | tf_op jit(solution)/shard_map/ppermute | solution.py:28
  62.0 18.8 %slice-start = ((s8[9437184]{0:T(1024)(128)(4,1)}), s8[4194304]{0:T(1024)(128)(4,1)S(1)}, s32[]{:S(2)}) async-start(s8[9437184]{0:T(1024)(128)(4,1)} %bitcast.114), calls=%async_computation | async-start | bytes 8388608
  62.0 18.8 %slice-start.1 = ((s8[9437184]{0:T(1024)(128)(4,1)}), s8[4194304]{0:T(1024)(128)(4,1)S(1)}, s32[]{:S(2)}) async-start(s8[9437184]{0:T(1024)(128)(4,1)} %bitcast.114), calls=%async_computation.1 | async-start | bytes 8388608
  63.4 17.4 %slice-start.2 = ((s8[9437184]{0:T(1024)(128)(4,1)}), s8[1048576]{0:T(1024)(128)(4,1)S(1)}, s32[]{:S(2)}) async-start(s8[9437184]{0:T(1024)(128)(4,1)} %bitcast.114), calls=%async_computation.2 | async-start | bytes 2097152
  63.6 11.6 %collective-permute-start.9 = (bf16[2,64,3072]{2,1,0:T(8,128)(2,1)S(1)}, bf16[2,64,3072]{2,1,0:T(8,128)(2,1)S(1)}, u32[]{:S(2)}, u32[]{:S(2)}) collective-permute-start(bf16[2,64,3072]{2,1,0:T(8,128)(2,1)S(1)} %fusion.11), channel_id=1, source_target_pairs={{0,8},{8,0},{16,24},{24,16},{1,9},{9,1},{17,25},{25,17},{2,10},{10... | collective-permute-start | bytes 2359304 | tf_op jit(solution)/shard_map/ppermute | solution.py:28
  67.3 6.5 %collective-permute-start.10 = (bf16[2,64,768]{2,1,0:T(8,128)(2,1)S(1)}, bf16[2,64,768]{2,1,0:T(8,128)(2,1)S(1)}, u32[]{:S(2)}, u32[]{:S(2)}) collective-permute-start(bf16[2,64,768]{2,1,0:T(8,128)(2,1)S(1)} %constant_dynamic-update-slice_fusion.4), channel_id=1, source_target_pairs={{0,2},{1,3},{2,0},{3,1},{4,6},{5,7},{6,4},{7,5},{8,10},{9,11},{10,... | collective-permute-start | bytes 589832 | tf_op jit(solution)/shard_map/ppermute | solution.py:28
  67.3 9.5 %collective-permute-start.12 = (bf16[2,32,768]{2,1,0:T(8,128)(2,1)S(1)}, bf16[2,32,768]{2,1,0:T(8,128)(2,1)S(1)}, u32[]{:S(2)}, u32[]{:S(2)}) collective-permute-start(bf16[2,32,768]{2,1,0:T(8,128)(2,1)S(1)} %get-tuple-element.66), channel_id=1, source_target_pairs={{0,0},{1,1},{2,8},{3,9},{4,16},{5,17},{6,24},{7,25},{8,2},{9,3},{1... | collective-permute-start | bytes 294920 | tf_op jit(solution)/shard_map/ppermute | solution.py:36
  70.5 10.1 %collective-permute-start.14 = (bf16[2,128,768]{2,1,0:T(8,128)(2,1)S(1)}, bf16[2,128,768]{2,1,0:T(8,128)(2,1)S(1)}, u32[]{:S(2)}, u32[]{:S(2)}) collective-permute-start(bf16[2,128,768]{2,1,0:T(8,128)(2,1)S(1)} %maximum_select_fusion.5), channel_id=1, source_target_pairs={{0,1},{1,0},{2,3},{3,2},{4,5},{5,4},{6,7},{7,6},{8,9},{9,8},{10,11... | collective-permute-start | bytes 1179656 | tf_op jit(solution)/shard_map/ppermute | solution.py:28
  73.8 20.3 %collective-permute-start.17 = (bf16[2,128,768]{2,1,0:T(8,128)(2,1)S(1)}, bf16[2,128,768]{2,1,0:T(8,128)(2,1)S(1)}, u32[]{:S(2)}, u32[]{:S(2)}) collective-permute-start(bf16[2,128,768]{2,1,0:T(8,128)(2,1)S(1)} %maximum_select_fusion.6), channel_id=1, source_target_pairs={{0,1},{1,0},{2,3},{3,2},{4,5},{5,4},{6,7},{7,6},{8,9},{9,8},{10,11... | collective-permute-start | bytes 1179656 | tf_op jit(solution)/shard_map/ppermute | solution.py:28
  83.9 17.4 %copy-start.4 = (f32[1,128,3072]{2,1,0:T(8,128)}, f32[1,128,3072]{2,1,0:T(8,128)S(1)}, u32[]{:S(2)}) copy-start(f32[1,128,3072]{2,1,0:T(8,128)S(1)} %convolution_bitcast_fusion.4) | copy-start | bytes 4718596
  85.3 7.3 %collective-permute-start.13 = (bf16[2,32,768]{2,1,0:T(8,128)(2,1)S(1)}, bf16[2,32,768]{2,1,0:T(8,128)(2,1)S(1)}, u32[]{:S(2)}, u32[]{:S(2)}) collective-permute-start(bf16[2,32,768]{2,1,0:T(8,128)(2,1)S(1)} %collective-permute-done.12), channel_id=1, source_target_pairs={{0,4},{1,5},{2,6},{3,7},{4,0},{5,1},{6,2},{7,3},{8,12},{9,13},{10,... | collective-permute-start | bytes 294920 | tf_op jit(solution)/shard_map/ppermute | solution.py:28
  86.5 19.0 %collective-permute-start.11 = (bf16[2,64,3072]{2,1,0:T(8,128)(2,1)}, bf16[2,64,3072]{2,1,0:T(8,128)(2,1)}, u32[]{:S(2)}, u32[]{:S(2)}) collective-permute-start(bf16[2,64,3072]{2,1,0:T(8,128)(2,1)} %fusion.62), channel_id=1, source_target_pairs={{0,16},{8,24},{16,0},{24,8},{1,17},{9,25},{17,1},{25,9},{2,18},{10... | collective-permute-start | bytes 2359304 | tf_op jit(solution)/shard_map/ppermute | solution.py:28
  89.9 11.4 %collective-permute-start.16 = (bf16[2,64,3072]{2,1,0:T(8,128)(2,1)}, bf16[2,64,3072]{2,1,0:T(8,128)(2,1)}, u32[]{:S(2)}, u32[]{:S(2)}) collective-permute-start(bf16[2,64,3072]{2,1,0:T(8,128)(2,1)} %fusion.5), channel_id=1, source_target_pairs={{0,8},{8,0},{16,24},{24,16},{1,9},{9,1},{17,25},{25,17},{2,10},{10... | collective-permute-start | bytes 2359304 | tf_op jit(solution)/shard_map/ppermute | solution.py:28
  93.3 10.3 %collective-permute-start.15 = (bf16[2,64,768]{2,1,0:T(8,128)(2,1)}, bf16[2,64,768]{2,1,0:T(8,128)(2,1)}, u32[]{:S(2)}, u32[]{:S(2)}) collective-permute-start(bf16[2,64,768]{2,1,0:T(8,128)(2,1)} %constant_dynamic-update-slice_fusion.6), channel_id=1, source_target_pairs={{0,2},{1,3},{2,0},{3,1},{4,6},{5,7},{6,4},{7,5},{8,10},{9,11},{10,... | collective-permute-start | bytes 589832 | tf_op jit(solution)/shard_map/ppermute | solution.py:28
  100.4 13.9 %collective-permute-start.19 = (bf16[2,64,3072]{2,1,0:T(8,128)(2,1)}, bf16[2,64,3072]{2,1,0:T(8,128)(2,1)}, u32[]{:S(2)}, u32[]{:S(2)}) collective-permute-start(bf16[2,64,3072]{2,1,0:T(8,128)(2,1)} %fusion.3), channel_id=1, source_target_pairs={{0,8},{8,0},{16,24},{24,16},{1,9},{9,1},{17,25},{25,17},{2,10},{10... | collective-permute-start | bytes 2359304 | tf_op jit(solution)/shard_map/ppermute | solution.py:28
  109.4 7.5 %collective-permute-start.18 = (bf16[2,64,3072]{2,1,0:T(8,128)(2,1)}, bf16[2,64,3072]{2,1,0:T(8,128)(2,1)}, u32[]{:S(2)}, u32[]{:S(2)}) collective-permute-start(bf16[2,64,3072]{2,1,0:T(8,128)(2,1)} %get-tuple-element.125), channel_id=1, source_target_pairs={{0,8},{8,0},{16,24},{24,16},{1,9},{9,1},{17,25},{25,17},{2,10},{10... | collective-permute-start | bytes 2359304 | tf_op jit(solution)/shard_map/ppermute | solution.py:28
  111.6 16.5 %collective-permute-start.22 = (bf16[2,128,768]{2,1,0:T(8,128)(2,1)}, bf16[2,128,768]{2,1,0:T(8,128)(2,1)S(1)}, u32[]{:S(2)}, u32[]{:S(2)}) collective-permute-start(bf16[2,128,768]{2,1,0:T(8,128)(2,1)} %maximum_select_fusion.7), channel_id=1, source_target_pairs={{0,1},{1,0},{2,3},{3,2},{4,5},{5,4},{6,7},{7,6},{8,9},{9,8},{10,11... | collective-permute-start | bytes 1179656 | tf_op jit(solution)/shard_map/ppermute | solution.py:28
  112.8 22.0 %collective-permute-start.21 = (bf16[2,64,3072]{2,1,0:T(8,128)(2,1)}, bf16[2,64,3072]{2,1,0:T(8,128)(2,1)}, u32[]{:S(2)}, u32[]{:S(2)}) collective-permute-start(bf16[2,64,3072]{2,1,0:T(8,128)(2,1)} %fusion.59), channel_id=1, source_target_pairs={{0,16},{8,24},{16,0},{24,8},{1,17},{9,25},{17,1},{25,9},{2,18},{10... | collective-permute-start | bytes 2359304 | tf_op jit(solution)/shard_map/ppermute | solution.py:28
  116.7 37.5 %collective-permute-start.27 = (bf16[2,64,3072]{2,1,0:T(8,128)(2,1)}, bf16[2,64,3072]{2,1,0:T(8,128)(2,1)}, u32[]{:S(2)}, u32[]{:S(2)}) collective-permute-start(bf16[2,64,3072]{2,1,0:T(8,128)(2,1)} %fusion.60), channel_id=1, source_target_pairs={{0,16},{8,24},{16,0},{24,8},{1,17},{9,25},{17,1},{25,9},{2,18},{10... | collective-permute-start | bytes 2359304 | tf_op jit(solution)/shard_map/ppermute | solution.py:28
  127.9 14.4 %collective-permute-start.20 = (bf16[2,128,768]{2,1,0:T(8,128)(2,1)}, bf16[2,128,768]{2,1,0:T(8,128)(2,1)}, u32[]{:S(2)}, u32[]{:S(2)}) collective-permute-start(bf16[2,128,768]{2,1,0:T(8,128)(2,1)} %fusion.49), channel_id=1, source_target_pairs={{0,1},{1,0},{2,3},{3,2},{4,5},{5,4},{6,7},{7,6},{8,9},{9,8},{10,11... | collective-permute-start | bytes 1179656 | tf_op jit(solution)/shard_map/ppermute | solution.py:28
  134.1 11.3 %collective-permute-start.25 = (bf16[2,64,3072]{2,1,0:T(8,128)(2,1)S(1)}, bf16[2,64,3072]{2,1,0:T(8,128)(2,1)S(1)}, u32[]{:S(2)}, u32[]{:S(2)}) collective-permute-start(bf16[2,64,3072]{2,1,0:T(8,128)(2,1)S(1)} %fusion.1), channel_id=1, source_target_pairs={{0,8},{8,0},{16,24},{24,16},{1,9},{9,1},{17,25},{25,17},{2,10},{10... | collective-permute-start | bytes 2359304 | tf_op jit(solution)/shard_map/ppermute | solution.py:28
  141.6 5.0 %collective-permute-start.24 = (bf16[2,64,3072]{2,1,0:T(8,128)(2,1)S(1)}, bf16[2,64,3072]{2,1,0:T(8,128)(2,1)S(1)}, u32[]{:S(2)}, u32[]{:S(2)}) collective-permute-start(bf16[2,64,3072]{2,1,0:T(8,128)(2,1)S(1)} %get-tuple-element.123), channel_id=1, source_target_pairs={{0,8},{8,0},{16,24},{24,16},{1,9},{9,1},{17,25},{25,17},{2,10},{10... | collective-permute-start | bytes 2359304 | tf_op jit(solution)/shard_map/ppermute | solution.py:28
  144.3 8.8 %collective-permute-start.23 = (bf16[2,64,768]{2,1,0:T(8,128)(2,1)}, bf16[2,64,768]{2,1,0:T(8,128)(2,1)}, u32[]{:S(2)}, u32[]{:S(2)}) collective-permute-start(bf16[2,64,768]{2,1,0:T(8,128)(2,1)} %dynamic-slice_convert_fusion.3), channel_id=1, source_target_pairs={{0,2},{1,3},{2,0},{3,1},{4,6},{5,7},{6,4},{7,5},{8,10},{9,11},{10,... | collective-permute-start | bytes 589832 | tf_op jit(solution)/shard_map/ppermute | solution.py:28
  159.3 13.0 %collective-permute-start.32 = (bf16[2,64,3072]{2,1,0:T(8,128)(2,1)S(1)}, bf16[2,64,3072]{2,1,0:T(8,128)(2,1)S(1)}, u32[]{:S(2)}, u32[]{:S(2)}) collective-permute-start(bf16[2,64,3072]{2,1,0:T(8,128)(2,1)S(1)} %get-tuple-element.121), channel_id=1, source_target_pairs={{0,8},{8,0},{16,24},{24,16},{1,9},{9,1},{17,25},{25,17},{2,10},{10... | collective-permute-start | bytes 2359304 | tf_op jit(solution)/shard_map/ppermute | solution.py:28
  160.2 10.9 %collective-permute-start.30 = (bf16[2,128,768]{2,1,0:T(8,128)(2,1)S(1)}, bf16[2,128,768]{2,1,0:T(8,128)(2,1)S(1)}, u32[]{:S(2)}, u32[]{:S(2)}) collective-permute-start(bf16[2,128,768]{2,1,0:T(8,128)(2,1)S(1)} %fusion.47), channel_id=1, source_target_pairs={{0,1},{1,0},{2,3},{3,2},{4,5},{5,4},{6,7},{7,6},{8,9},{9,8},{10,11... | collective-permute-start | bytes 1179656 | tf_op jit(solution)/shard_map/ppermute | solution.py:28
  160.8 7.5 %collective-permute-start.26 = (bf16[2,32,768]{2,1,0:T(8,128)(2,1)S(1)}, bf16[2,32,768]{2,1,0:T(8,128)(2,1)S(1)}, u32[]{:S(2)}, u32[]{:S(2)}) collective-permute-start(bf16[2,32,768]{2,1,0:T(8,128)(2,1)S(1)} %slice.409), channel_id=1, source_target_pairs={{0,4},{1,5},{2,6},{3,7},{4,0},{5,1},{6,2},{7,3},{8,12},{9,13},{10,... | collective-permute-start | bytes 294920 | tf_op jit(solution)/shard_map/ppermute | solution.py:28
  160.9 19.4 %collective-permute-start.29 = (bf16[2,64,3072]{2,1,0:T(8,128)(2,1)}, bf16[2,64,3072]{2,1,0:T(8,128)(2,1)}, u32[]{:S(2)}, u32[]{:S(2)}) collective-permute-start(bf16[2,64,3072]{2,1,0:T(8,128)(2,1)} %fusion.61), channel_id=1, source_target_pairs={{0,16},{8,24},{16,0},{24,8},{1,17},{9,25},{17,1},{25,9},{2,18},{10... | collective-permute-start | bytes 2359304 | tf_op jit(solution)/shard_map/ppermute | solution.py:28
  171.9 7.4 %collective-permute-start.31 = (bf16[2,64,768]{2,1,0:T(8,128)(2,1)}, bf16[2,64,768]{2,1,0:T(8,128)(2,1)}, u32[]{:S(2)}, u32[]{:S(2)}) collective-permute-start(bf16[2,64,768]{2,1,0:T(8,128)(2,1)} %dynamic-slice_convert_fusion.2), channel_id=1, source_target_pairs={{0,2},{1,3},{2,0},{3,1},{4,6},{5,7},{6,4},{7,5},{8,10},{9,11},{10,... | collective-permute-start | bytes 589832 | tf_op jit(solution)/shard_map/ppermute | solution.py:28
  184.8 15.0 %collective-permute-start.33 = (bf16[2,64,3072]{2,1,0:T(8,128)(2,1)S(1)}, bf16[2,64,3072]{2,1,0:T(8,128)(2,1)S(1)}, u32[]{:S(2)}, u32[]{:S(2)}) collective-permute-start(bf16[2,64,3072]{2,1,0:T(8,128)(2,1)S(1)} %get-tuple-element.119), channel_id=1, source_target_pairs={{0,8},{8,0},{16,24},{24,16},{1,9},{9,1},{17,25},{25,17},{2,10},{10... | collective-permute-start | bytes 2359304 | tf_op jit(solution)/shard_map/ppermute | solution.py:28
  185.8 9.4 %collective-permute-start.34 = (bf16[2,32,768]{2,1,0:T(8,128)(2,1)S(1)}, bf16[2,32,768]{2,1,0:T(8,128)(2,1)S(1)}, u32[]{:S(2)}, u32[]{:S(2)}) collective-permute-start(bf16[2,32,768]{2,1,0:T(8,128)(2,1)S(1)} %slice.408), channel_id=1, source_target_pairs={{0,4},{1,5},{2,6},{3,7},{4,0},{5,1},{6,2},{7,3},{8,12},{9,13},{10,... | collective-permute-start | bytes 294920 | tf_op jit(solution)/shard_map/ppermute | solution.py:28
  189.7 30.7 %collective-permute-start.28 = (bf16[2,32,768]{2,1,0:T(8,128)(2,1)}, bf16[2,32,768]{2,1,0:T(8,128)(2,1)S(1)}, u32[]{:S(2)}, u32[]{:S(2)}) collective-permute-start(bf16[2,32,768]{2,1,0:T(8,128)(2,1)} %fusion.55), channel_id=1, source_target_pairs={{0,0},{1,1},{2,8},{3,9},{4,16},{5,17},{6,24},{7,25},{8,2},{9,3},{1... | collective-permute-start | bytes 294920 | tf_op jit(solution)/shard_map/ppermute | solution.py:36
  194.1 11.6 %collective-permute-start.36 = (bf16[2,128,768]{2,1,0:T(8,128)(2,1)}, bf16[2,128,768]{2,1,0:T(8,128)(2,1)}, u32[]{:S(2)}, u32[]{:S(2)}) collective-permute-start(bf16[2,128,768]{2,1,0:T(8,128)(2,1)} %fusion.43), channel_id=1, source_target_pairs={{0,1},{1,0},{2,3},{3,2},{4,5},{5,4},{6,7},{7,6},{8,9},{9,8},{10,11... | collective-permute-start | bytes 1179656 | tf_op jit(solution)/shard_map/ppermute | solution.py:28
  195.8 38.3 %collective-permute-start.37 = (bf16[2,32,768]{2,1,0:T(8,128)(2,1)}, bf16[2,32,768]{2,1,0:T(8,128)(2,1)S(1)}, u32[]{:S(2)}, u32[]{:S(2)}) collective-permute-start(bf16[2,32,768]{2,1,0:T(8,128)(2,1)} %fusion.54), channel_id=1, source_target_pairs={{0,0},{1,1},{2,8},{3,9},{4,16},{5,17},{6,24},{7,25},{8,2},{9,3},{1... | collective-permute-start | bytes 294920 | tf_op jit(solution)/shard_map/ppermute | solution.py:36
  204.6 14.4 %collective-permute-start.35 = (bf16[2,128,768]{2,1,0:T(8,128)(2,1)S(1)}, bf16[2,128,768]{2,1,0:T(8,128)(2,1)S(1)}, u32[]{:S(2)}, u32[]{:S(2)}) collective-permute-start(bf16[2,128,768]{2,1,0:T(8,128)(2,1)S(1)} %fusion.37), channel_id=1, source_target_pairs={{0,1},{1,0},{2,3},{3,2},{4,5},{5,4},{6,7},{7,6},{8,9},{9,8},{10,11... | collective-permute-start | bytes 1179656 | tf_op jit(solution)/shard_map/ppermute | solution.py:28
  211.2 9.3 %collective-permute-start.38 = (bf16[2,64,768]{2,1,0:T(8,128)(2,1)S(1)}, bf16[2,64,768]{2,1,0:T(8,128)(2,1)S(1)}, u32[]{:S(2)}, u32[]{:S(2)}) collective-permute-start(bf16[2,64,768]{2,1,0:T(8,128)(2,1)S(1)} %dynamic-slice_convert_fusion.1), channel_id=1, source_target_pairs={{0,2},{1,3},{2,0},{3,1},{4,6},{5,7},{6,4},{7,5},{8,10},{9,11},{10,... | collective-permute-start | bytes 589832 | tf_op jit(solution)/shard_map/ppermute | solution.py:28
  219.2 7.1 %collective-permute-start.40 = (bf16[2,64,768]{2,1,0:T(8,128)(2,1)S(1)}, bf16[2,64,768]{2,1,0:T(8,128)(2,1)S(1)}, u32[]{:S(2)}, u32[]{:S(2)}) collective-permute-start(bf16[2,64,768]{2,1,0:T(8,128)(2,1)S(1)} %dynamic-slice_convert_fusion), channel_id=1, source_target_pairs={{0,2},{1,3},{2,0},{3,1},{4,6},{5,7},{6,4},{7,5},{8,10},{9,11},{10,... | collective-permute-start | bytes 589832 | tf_op jit(solution)/shard_map/ppermute | solution.py:28
  220.5 7.2 %collective-permute-start.39 = (bf16[2,32,768]{2,1,0:T(8,128)(2,1)S(1)}, bf16[2,32,768]{2,1,0:T(8,128)(2,1)S(1)}, u32[]{:S(2)}, u32[]{:S(2)}) collective-permute-start(bf16[2,32,768]{2,1,0:T(8,128)(2,1)S(1)} %slice.407), channel_id=1, source_target_pairs={{0,4},{1,5},{2,6},{3,7},{4,0},{5,1},{6,2},{7,3},{8,12},{9,13},{10,... | collective-permute-start | bytes 294920 | tf_op jit(solution)/shard_map/ppermute | solution.py:28
  226.3 7.9 %collective-permute-start.42 = (bf16[2,32,768]{2,1,0:T(8,128)(2,1)S(1)}, bf16[2,32,768]{2,1,0:T(8,128)(2,1)S(1)}, u32[]{:S(2)}, u32[]{:S(2)}) collective-permute-start(bf16[2,32,768]{2,1,0:T(8,128)(2,1)S(1)} %slice.406), channel_id=1, source_target_pairs={{0,4},{1,5},{2,6},{3,7},{4,0},{5,1},{6,2},{7,3},{8,12},{9,13},{10,... | collective-permute-start | bytes 294920 | tf_op jit(solution)/shard_map/ppermute | solution.py:28
  227.7 17.1 %collective-permute-start.41 = (bf16[2,32,768]{2,1,0:T(8,128)(2,1)S(1)}, bf16[2,32,768]{2,1,0:T(8,128)(2,1)S(1)}, u32[]{:S(2)}, u32[]{:S(2)}) collective-permute-start(bf16[2,32,768]{2,1,0:T(8,128)(2,1)S(1)} %fusion.53), channel_id=1, source_target_pairs={{0,0},{1,1},{2,8},{3,9},{4,16},{5,17},{6,24},{7,25},{8,2},{9,3},{1... | collective-permute-start | bytes 294920 | tf_op jit(solution)/shard_map/ppermute | solution.py:36
  234.2 10.6 %collective-permute-start.43 = (bf16[2,32,768]{2,1,0:T(8,128)(2,1)S(1)}, bf16[2,32,768]{2,1,0:T(8,128)(2,1)S(1)}, u32[]{:S(2)}, u32[]{:S(2)}) collective-permute-start(bf16[2,32,768]{2,1,0:T(8,128)(2,1)S(1)} %fusion.52), channel_id=1, source_target_pairs={{0,0},{1,1},{2,8},{3,9},{4,16},{5,17},{6,24},{7,25},{8,2},{9,3},{1... | collective-permute-start | bytes 294920 | tf_op jit(solution)/shard_map/ppermute | solution.py:36
  (48 other events, 177.8 us)

commit v3 on v2

v3 whole, which is shorter than its diff:
```python
import functools

import jax
import jax.numpy as jnp
from jax import lax
from jax.experimental import pallas as pl
from jax.experimental.pallas import tpu as pltpu
from jax.sharding import PartitionSpec as P

LIMIT = 8 << 20
SHARES = (2, 2, 2, 2)
ORDER = (
    0, 1, 0, 1, 0, 2, 1, 0, 2, 3, 1, 2, 0, 2, 0, 3, 1, 3, 2, 1, 3, 0, 2, 0, 3, 1, 0, 3, 1, 0, 2, 0, 1, 2, 1, 3, 1, 3,
    2, -1, 3, 0, 2, 3, 2, 1, 3, -1, 3, 2,
)


VMEM = pl.BlockSpec(memory_space=pltpu.VMEM)
SMEM = pl.BlockSpec(memory_space=pltpu.SMEM)


def cdf_of(value):
    return 0.5 * (1.0 + lax.erf(value * 0.7071067811865476))


def contract(left, right, left_dim, right_dim):
    return lax.dot_general(
        left, right, (((left_dim,), (right_dim,)), ((), ())), preferred_element_type=jnp.float32
    )


def activations(sums):
    hidden_pre, grad_act = sums[0], sums[1]
    cumul = cdf_of(hidden_pre)
    density = jnp.exp(-0.5 * hidden_pre * hidden_pre) * 0.3989422804014327
    act = (hidden_pre * cumul).astype(jnp.bfloat16)
    return act, (grad_act * (cumul + hidden_pre * density)).astype(jnp.bfloat16)


def swap(value, axis, size, mask):
    return lax.ppermute(value, axis, [(i, i ^ mask) for i in range(size)])


def transposed(value, rows, cols):
    per = cols // rows
    pairs = [
        (r * cols + c, (c // per) * cols + r * per + c % per) for r in range(rows) for c in range(cols)
    ]
    return lax.ppermute(value, ("row", "col"), pairs)


def fetch_kernel(*refs):
    count = len(refs) // 2
    copies = [pltpu.make_async_copy(refs[i], refs[count + i], refs[-1].at[i]) for i in range(count)]
    for copy in copies:
        copy.start()
    for copy in copies:
        copy.wait()


def fetched(*arrays):
    return pl.pallas_call(
        fetch_kernel,
        out_shape=[jax.ShapeDtypeStruct(a.shape, a.dtype) for a in arrays],
        in_specs=[pl.BlockSpec(memory_space=pltpu.HBM)] * len(arrays),
        out_specs=[VMEM] * len(arrays),
        scratch_shapes=[pltpu.SemaphoreType.DMA((len(arrays),))],
        compiler_params=pltpu.CompilerParams(vmem_limit_bytes=34 << 20),
    )(*arrays)


def at_part(side, size):
    return pl.multiple_of(side * size, size)


def in_kernel(y_ref, mine, other, weight_in, weight_out, away, keep):
    half, f = mine.shape[1] // 2, mine.shape[2]
    blocks = ((mine, at_part(y_ref[0], f)), (other, at_part(1 - y_ref[0], f)))
    tile = 512

    @pl.loop(0, weight_in.shape[1] // tile)
    def _(step):
        cols = pl.ds(pl.multiple_of(step * tile, tile), tile)
        hidden = [contract(b[0], weight_in[pl.ds(at, f), cols], 1, 0) for b, at in blocks]
        hidden = hidden[0] + hidden[1]
        keep[0, :, cols] = hidden[:half]
        away[0, :, cols] = hidden[half:].astype(away.dtype)
        grad = [contract(b[1], weight_out[cols, pl.ds(at, f)], 1, 1) for b, at in blocks]
        grad = grad[0] + grad[1]
        keep[1, :, cols] = grad[:half]
        away[1, :, cols] = grad[half:].astype(away.dtype)


def out_kernel(y_ref, own, got, weight_in, weight_out, away, keep, full):
    half, f = own.shape[1], keep.shape[2]
    full[:, :half] = own[...]
    full[:, half:] = got[...]
    tile = 256

    @pl.loop(0, f // tile)
    def _(step):
        cols = pl.ds(pl.multiple_of(step * tile, tile), tile)
        for out, side in ((away, 1 - y_ref[0]), (keep, y_ref[0])):
            at = pl.ds(pl.multiple_of(at_part(side, f) + step * tile, tile), tile)
            out[0, :, cols] = contract(full[0], weight_out[:, at], 1, 0).astype(out.dtype)
            out[1, :, cols] = contract(full[1], weight_in[at, :], 1, 1).astype(out.dtype)


def in_terms(y, mine, other, weight_in, weight_out):
    shape = (2, mine.shape[1] // 2, weight_in.shape[1])
    return pl.pallas_call(
        in_kernel,
        out_shape=[jax.ShapeDtypeStruct(shape, jnp.bfloat16), jax.ShapeDtypeStruct(shape, jnp.float32)],
        in_specs=[SMEM, VMEM, VMEM, VMEM, VMEM],
        out_specs=[VMEM, VMEM],
        compiler_params=pltpu.CompilerParams(vmem_limit_bytes=LIMIT),
    )(y, mine, other, weight_in, weight_out)


def out_terms(y, own, got, weight_in, weight_out):
    shape = (2, own.shape[1] * 2, weight_in.shape[0] // 2)
    return pl.pallas_call(
        out_kernel,
        out_shape=[jax.ShapeDtypeStruct(shape, jnp.bfloat16), jax.ShapeDtypeStruct(shape, jnp.float32)],
        in_specs=[SMEM, VMEM, VMEM, VMEM, VMEM],
        out_specs=[VMEM, VMEM],
        scratch_shapes=[pltpu.VMEM((2, own.shape[1] * 2, own.shape[2]), jnp.bfloat16)],
        compiler_params=pltpu.CompilerParams(vmem_limit_bytes=LIMIT),
    )(y, own, got, weight_in, weight_out)


def gradient_kernel(which, parts, y_ref, *refs):
    pieces, (out, tokens, hidden, turned, sems) = refs[: 4 * parts], refs[4 * parts :]
    f = pieces[0].shape[2]
    copies, at = [], 0
    for part in range(parts):
        mine, other, own, got = pieces[4 * part : 4 * part + 4]
        n = mine.shape[1]
        for block, side in ((mine, y_ref[0]), (other, 1 - y_ref[0])):
            copies.append((block.at[1 - which], tokens.at[pl.ds(at, n), pl.ds(at_part(side, f), f)]))
        for block in (own, got):
            copies.append((block.at[which], hidden.at[pl.ds(at, n // 2)]))
            at += n // 2

    @pl.when(pl.program_id(0) == 0)
    def _():
        started = [pltpu.make_async_copy(*copy, sems.at[i]) for i, copy in enumerate(copies)]
        for copy in started:
            copy.start()
        for copy in started:
            copy.wait()

    left, right = (tokens, hidden) if which else (hidden, tokens)
    rows = out.shape[0]
    cols = pl.ds(pl.multiple_of(pl.program_id(0) * rows, rows), rows)
    turned[...] = left[:, cols].T
    tile = 512

    @pl.loop(0, out.shape[1] // tile)
    def _(step):
        at = pl.ds(pl.multiple_of(step * tile, tile), tile)
        out[:, at] = contract(turned[...], right[:, at], 1, 0).astype(out.dtype)


def weight_gradient(which, y, made):
    pieces = [piece for part in made for piece in part["pieces"]]
    rows = sum(part["pieces"][0].shape[1] for part in made)
    width, ff = 2 * pieces[0].shape[2], pieces[2].shape[2]
    shape = (width, ff) if which else (ff, width)
    tile = 256 if which else 512
    return pl.pallas_call(
        functools.partial(gradient_kernel, which, len(made)),
        out_shape=jax.ShapeDtypeStruct(shape, jnp.bfloat16),
        grid=(shape[0] // tile,),
        in_specs=[SMEM] + [pl.BlockSpec(memory_space=pl.ANY)] * len(pieces),
        out_specs=pl.BlockSpec((tile, shape[1]), lambda i: (i, 0)),
        scratch_shapes=[
            pltpu.VMEM((rows, width), jnp.bfloat16),
            pltpu.VMEM((rows, ff), jnp.bfloat16),
            pltpu.VMEM((tile, rows), jnp.bfloat16),
            pltpu.SemaphoreType.DMA((len(pieces),)),
        ],
        compiler_params=pltpu.CompilerParams(vmem_limit_bytes=24 << 20),
    )(y, *pieces)


class Clock:
    def __init__(self):
        self.last = None

    def start(self, value):
        if self.last is None:
            return value
        return lax.optimization_barrier((value, self.last))[0]

    def end(self, value):
        self.last = value
        return value


class Grid:
    def __init__(self, rows, cols, clock):
        self.rows, self.cols, self.clock = rows, cols, clock
        self.core = lax.axis_index("row") % 2
        self.side = jnp.reshape(lax.axis_index("col") % 2, (1,)).astype(jnp.int32)

    def gather(self, block):
        clock = self.clock
        block = clock.end(clock.start(block))
        block = transposed(block, self.rows, self.cols)
        yield
        block = clock.end(clock.start(block))
        far = swap(block, "col", self.cols, 4)
        yield
        near = clock.end(jnp.concatenate([block, clock.start(far)], axis=1))
        far = swap(near, "col", self.cols, 2)
        yield
        far = clock.start(far)
        mine = jnp.where(
            self.core == 0,
            jnp.concatenate([near, far], axis=1),
            jnp.concatenate([far, near], axis=1),
        )
        mine = clock.end(mine)
        other = swap(mine, "col", self.cols, 1)
        yield
        return mine, clock.start(other)

    def scatter(self, away, keep):
        clock, n = self.clock, keep.shape[1] // 4
        clock.end(away)
        got = swap(away, "col", self.cols, 1)
        yield
        total = keep + clock.start(got)
        away = lax.dynamic_slice_in_dim(total, (1 - self.core) * 2 * n, 2 * n, axis=1)
        away = clock.end(away.astype(jnp.bfloat16))
        keep = lax.dynamic_slice_in_dim(total, self.core * 2 * n, 2 * n, axis=1)
        got = swap(away, "col", self.cols, 2)
        yield
        total = keep + clock.start(got)
        away = clock.end(total[:, n:].astype(jnp.bfloat16))
        got = swap(away, "col", self.cols, 4)
        yield
        out = clock.end((total[:, :n] + clock.start(got)).astype(jnp.bfloat16))
        out = transposed(out, self.rows, self.cols)
        yield
        return clock.end(clock.start(out))


def part_steps(grid, clock, weights, block, made):
    rows = grid.rows
    mine, other = yield from grid.gather(block)
    away, keep = in_terms(grid.side, mine, other, *weights)
    got = swap(clock.end(away), "row", rows, 1)
    yield
    sums = keep + clock.start(got)
    got = swap(clock.end(sums.astype(jnp.bfloat16)), "row", rows, 2)
    yield
    act, grad_pre = activations(sums + clock.start(got))
    own = clock.end(jnp.stack([act, grad_pre]))
    got = swap(own, "row", rows, 1)
    yield
    got = clock.start(got)
    made["pieces"] = mine, other, own, got
    made["out"] = yield from grid.scatter(*out_terms(grid.side, own, got, *weights))


def body(rows, cols, tokens, weight_in, weight_out, out_grad):
    clock = Clock()
    grid = Grid(rows, cols, clock)
    both = jnp.stack([tokens, out_grad])
    weights = [weight_in, weight_out]
    parts, made = [], []
    first = 0
    for share in SHARES:
        n = tokens.shape[0] * share // sum(SHARES)
        made.append({})
        parts.append(part_steps(grid, clock, weights, both[:, first : first + n], made[-1]))
        first += n
    grads = []
    for count, part in enumerate(ORDER):
        if count == 1:
            weights[:] = fetched(clock.start(weight_in), weight_out)
            clock.end(weights[1])
        if part < 0:
            made[0]["pieces"] = (clock.start(made[0]["pieces"][0]), *made[0]["pieces"][1:])
            grads.append(clock.end(weight_gradient(1 - len(grads), grid.side, made)))
        else:
            next(parts[part], None)
    out = jnp.concatenate([m["out"] for m in made], axis=1)
    return out[0], out[1], grads[0], grads[1]


def plain_body(rows, cols, tokens, weight_in, weight_out, out_grad):
    per = cols // rows
    both = jnp.stack([tokens, out_grad])
    two, n, f = both.shape
    panel = lax.all_gather(transposed(both, rows, cols), "col", axis=0)
    panel = panel.reshape(rows, per, two, n, f).transpose(2, 0, 3, 1, 4).reshape(two, rows * n, per * f)
    terms = jnp.stack([contract(panel[0], weight_in, 1, 0), contract(panel[1], weight_out, 1, 1)])
    act, grad_pre = activations(lax.psum_scatter(terms, "row", scatter_dimension=1, tiled=True))
    full = lax.all_gather(jnp.stack([act, grad_pre]), "row", axis=1, tiled=True)
    terms = jnp.stack([contract(full[0], weight_out, 1, 0), contract(full[1], weight_in, 1, 1)])
    terms = terms.reshape(two, rows, n, per, f).transpose(1, 3, 0, 2, 4).reshape(cols, two, n, f)
    out = lax.psum_scatter(terms, "col", scatter_dimension=0).astype(jnp.bfloat16)
    out = transposed(out, rows, cols)
    grad_in = contract(panel[0], full[1], 0, 0).astype(jnp.bfloat16)
    grad_out = contract(full[0], panel[1], 0, 0).astype(jnp.bfloat16)
    return out[0], out[1], grad_in, grad_out


def solution(mesh):
    shape = (mesh.shape["row"], mesh.shape["col"])
    return jax.shard_map(
        functools.partial(body if shape == (4, 8) else plain_body, *shape),
        mesh=mesh,
        in_specs=(P("row", "col"), P("row", "col"), P("col", "row"), P("row", "col")),
        out_specs=(P("row", "col"), P("row", "col"), P("row", "col"), P("col", "row")),
        check_vma=False,
    )
```

time: 251 us -> 237 us (0.944)
  the two profiles are of different devices: /device:TPU:3 before, /device:TPU:2 now
where the time goes in v3:
time: 237 us; the launch traced here: 236 us
  Pallas kernels  74.4 us (31%)
  waiting for transfers between devices  65.5 us (28%)
  starting transfers between devices  60.5 us (26%)
  local copies, waits for them, and re-layouts  23.5 us (10%)
  other arithmetic  10.6 us (4%)
    ppermute x36, waiting for transfers between devices, swap(): return lax.ppermute(value, axis, [(i, i ^ mask) for i in range(size)])  46.2 us
    ppermute x8, starting transfers between devices, transposed(): return lax.ppermute(value, ('row', 'col'), pairs)  30.3 us
    ppermute x36, starting transfers between devices, swap(): return lax.ppermute(value, axis, [(i, i ^ mask) for i in range(size)])  30.2 us
    pallas_call x2, Pallas kernels, weight_gradient(): pl.pallas_call(functools.partial(gradient_kernel, which, len(made)), out_...  27.2 us
    unnamed x67, local copies, waits for them, and re-layouts  22.5 us
    pallas_call x4, Pallas kernels, in_terms(): pl.pallas_call(in_kernel, out_shape=[jax.ShapeDtypeStruct(shape, jnp.bflo...  21.9 us
    ppermute x8, waiting for transfers between devices, transposed(): return lax.ppermute(value, ('row', 'col'), pairs)  19.3 us
    pallas_call x4, Pallas kernels, out_terms(): pl.pallas_call(out_kernel, out_shape=[jax.ShapeDtypeStruct(shape, jnp.bfl...  19 us
  transfers between devices with their start and end apart: 44, of which 20 were waited for; matrix products, arithmetic and copies ran while one was open for 4% of the time, Pallas kernels for 27%

profile of v3, /device:TPU:2, one launch (start us, length us, event | category | flops | bytes accessed | tf_op | source)
XLA Modules:
  0.0 236.2 jit_solution(16537195245428290226)
XLA Ops:
  1.6 4.5 %collective-permute-start = (bf16[2,32,768]{2,1,0:T(8,128)(2,1)S(1)}, bf16[2,32,768]{2,1,0:T(8,128)(2,1)S(1)}, u32[]{:S(2)}, u32[]{:S(2)}) collective-permute-start(bf16[2,32,768]{2,1,0:T(8,128)(2,1)S(1)} %get-tuple-element.151), channel_id=1, source_target_pairs={{0,0},{1,1},{2,8},{3,9},{4,16},{5,17},{6,24},{7,25},{8,2},{9,3},{1... | collective-permute-start | bytes 294920 | tf_op jit(solution)/shard_map/ppermute | solution.py:49
  6.1 6.4 %shard_map.75 = (bf16[1536,3072]{1,0:T(8,128)(2,1)S(1)}, bf16[3072,1536]{1,0:T(8,128)(2,1)S(1)}) custom-call(bf16[1536,3072]{1,0:T(8,128)(2,1)} %refs_0_, bf16[3072,1536]{1,0:T(8,128)(2,1)} %refs_1_.1), custom_call_target="tpu_custom_call" | custom-call | tf_op jit(solution)/shard_map/pallas_call | solution.py:62
  12.5 3.7 %copy-done = bf16[1536,3072]{1,0:T(8,128)(2,1)} copy-done((bf16[1536,3072]{1,0:T(8,128)(2,1)}, bf16[1536,3072]{1,0:T(8,128)(2,1)S(1)}, u32[]{:S(2)}) %copy-start) | copy-done | bytes 9437208
  16.2 3.7 %copy-done.3 = bf16[3072,1536]{1,0:T(8,128)(2,1)} copy-done((bf16[3072,1536]{1,0:T(8,128)(2,1)}, bf16[3072,1536]{1,0:T(8,128)(2,1)S(1)}, u32[]{:S(2)}) %copy-start.3) | copy-done | bytes 9437208
  20.0 3.2 %collective-permute-start.2 = (bf16[2,32,768]{2,1,0:T(8,128)(2,1)S(1)}, bf16[2,32,768]{2,1,0:T(8,128)(2,1)S(1)}, u32[]{:S(2)}, u32[]{:S(2)}) collective-permute-start(bf16[2,32,768]{2,1,0:T(8,128)(2,1)S(1)} %get-tuple-element.74), channel_id=1, source_target_pairs={{0,0},{1,1},{2,8},{3,9},{4,16},{5,17},{6,24},{7,25},{8,2},{9,3},{1... | collective-permute-start | bytes 294920 | tf_op jit(solution)/shard_map/ppermute | solution.py:49
  23.2 9.3 %collective-permute-done.2 = bf16[2,32,768]{2,1,0:T(8,128)(2,1)S(1)} collective-permute-done((bf16[2,32,768]{2,1,0:T(8,128)(2,1)S(1)}, bf16[2,32,768]{2,1,0:T(8,128)(2,1)S(1)}, u32[]{:S(2)}, u32[]{:S(2)}) %collective-permute-start.2) | collective-permute-done | bytes 98336 | tf_op jit(solution)/shard_map/ppermute | solution.py:49
  34.1 4.0 %collective-permute-done.4 = bf16[2,32,768]{2,1,0:T(8,128)(2,1)S(1)} collective-permute-done((bf16[2,32,768]{2,1,0:T(8,128)(2,1)S(1)}, bf16[2,32,768]{2,1,0:T(8,128)(2,1)S(1)}, u32[]{:S(2)}, u32[]{:S(2)}) %collective-permute-start.4) | collective-permute-done | bytes 98336 | tf_op jit(solution)/shard_map/ppermute | solution.py:41
  38.2 2.1 collective-permute-start.6
  42.0 1.6 collective-permute-start.5
  43.6 6.0 %collective-permute-done.6 = bf16[2,32,768]{2,1,0:T(8,128)(2,1)S(1)} collective-permute-done((bf16[2,32,768]{2,1,0:T(8,128)(2,1)S(1)}, bf16[2,32,768]{2,1,0:T(8,128)(2,1)S(1)}, u32[]{:S(2)}, u32[]{:S(2)}) %collective-permute-start.6) | collective-permute-done | bytes 98336 | tf_op jit(solution)/shard_map/ppermute | solution.py:49
  49.8 6.4 %collective-permute-done.7 = bf16[2,32,768]{2,1,0:T(8,128)(2,1)S(1)} collective-permute-done((bf16[2,32,768]{2,1,0:T(8,128)(2,1)S(1)}, bf16[2,32,768]{2,1,0:T(8,128)(2,1)S(1)}, u32[]{:S(2)}, u32[]{:S(2)}) %collective-permute-start.7) | collective-permute-done | bytes 98336 | tf_op jit(solution)/shard_map/ppermute | solution.py:41
  56.2 3.8 %copy-done.1 = bf16[1536,3072]{1,0:T(8,128)(2,1)S(1)} copy-done((bf16[1536,3072]{1,0:T(8,128)(2,1)S(1)}, bf16[1536,3072]{1,0:T(8,128)(2,1)}, u32[]{:S(2)}) %copy-start.1) | copy-done | bytes 9437208
  60.0 3.7 %copy-done.4 = bf16[3072,1536]{1,0:T(8,128)(2,1)S(1)} copy-done((bf16[3072,1536]{1,0:T(8,128)(2,1)S(1)}, bf16[3072,1536]{1,0:T(8,128)(2,1)}, u32[]{:S(2)}) %copy-start.4) | copy-done | bytes 9437208
  63.7 5.2 %shard_map.76 = (bf16[2,64,3072]{2,1,0:T(8,128)(2,1)S(1)}, f32[2,64,3072]{2,1,0:T(8,128)S(1)}) custom-call(s32[1]{0:T(128)} %bitcast.y_ref, bf16[2,128,768]{2,1,0:T(8,128)(2,1)S(1)} %maximum_select_fusion.mine.refs_0_, bf16[2,128,768]{2,1,0:T(8,128)(2,1)S(1)} %collective-permute-done.5.other.refs_1_, bf16[1536,3072]{1,0:T(8,128)(2,1)S(1)} %copy-done.1, ...), custom_call_target="tpu_custom_call" | custom-call | tf_op jit(solution)/shard_map/pallas_call | solution.py:111
  69.1 3.6 %collective-permute-start.12 = (bf16[2,32,768]{2,1,0:T(8,128)(2,1)S(1)}, bf16[2,32,768]{2,1,0:T(8,128)(2,1)S(1)}, u32[]{:S(2)}, u32[]{:S(2)}) collective-permute-start(bf16[2,32,768]{2,1,0:T(8,128)(2,1)S(1)} %get-tuple-element.82), channel_id=1, source_target_pairs={{0,0},{1,1},{2,8},{3,9},{4,16},{5,17},{6,24},{7,25},{8,2},{9,3},{1... | collective-permute-start | bytes 294920 | tf_op jit(solution)/shard_map/ppermute | solution.py:49
  72.8 1.6 collective-permute-start.14
  74.3 2.0 collective-permute-done.10
  76.6 3.9 %collective-permute-done.12 = bf16[2,32,768]{2,1,0:T(8,128)(2,1)S(1)} collective-permute-done((bf16[2,32,768]{2,1,0:T(8,128)(2,1)S(1)}, bf16[2,32,768]{2,1,0:T(8,128)(2,1)S(1)}, u32[]{:S(2)}, u32[]{:S(2)}) %collective-permute-start.12) | collective-permute-done | bytes 98336 | tf_op jit(solution)/shard_map/ppermute | solution.py:49
  80.6 2.9 %collective-permute-done.14.other.refs_5_ = bf16[2,128,768]{2,1,0:T(8,128)(2,1)S(1)} collective-permute-done((bf16[2,128,768]{2,1,0:T(8,128)(2,1)S(1)}, bf16[2,128,768]{2,1,0:T(8,128)(2,1)S(1)}, u32[]{:S(2)}, u32[]{:S(2)}) %collective-permute-start.14) | collective-permute-done | bytes 393248 | tf_op jit(solution)/shard_map/ppermute | solution.py:41
  83.5 5.2 %shard_map.77 = (bf16[2,64,3072]{2,1,0:T(8,128)(2,1)S(1)}, f32[2,64,3072]{2,1,0:T(8,128)S(1)}) custom-call(s32[1]{0:T(128)} %bitcast.y_ref, bf16[2,128,768]{2,1,0:T(8,128)(2,1)S(1)} %maximum_select_fusion.1.mine.refs_4_, bf16[2,128,768]{2,1,0:T(8,128)(2,1)S(1)} %collective-permute-done.14.other.refs_5_, bf16[1536,3072]{1,0:T(8,128)(2,1)S(1)} %bitcast.8, ...), custom_call_target="tpu_custom_call" | custom-call | tf_op jit(solution)/shard_map/pallas_call | solution.py:111
  90.4 3.7 %collective-permute-start.13 = (bf16[2,32,768]{2,1,0:T(8,128)(2,1)S(1)}, bf16[2,32,768]{2,1,0:T(8,128)(2,1)S(1)}, u32[]{:S(2)}, u32[]{:S(2)}) collective-permute-start(bf16[2,32,768]{2,1,0:T(8,128)(2,1)S(1)} %collective-permute-done.12), channel_id=1, source_target_pairs={{0,4},{1,5},{2,6},{3,7},{4,0},{5,1},{6,2},{7,3},{8,12},{9,13},{10,... | collective-permute-start | bytes 294920 | tf_op jit(solution)/shard_map/ppermute | solution.py:41
  94.1 4.9 %collective-permute-done.13 = bf16[2,32,768]{2,1,0:T(8,128)(2,1)S(1)} collective-permute-done((bf16[2,32,768]{2,1,0:T(8,128)(2,1)S(1)}, bf16[2,32,768]{2,1,0:T(8,128)(2,1)S(1)}, u32[]{:S(2)}, u32[]{:S(2)}) %collective-permute-start.13) | collective-permute-done | bytes 98336 | tf_op jit(solution)/shard_map/ppermute | solution.py:41
  100.4 6.2 %shard_map.78 = (bf16[2,64,3072]{2,1,0:T(8,128)(2,1)}, f32[2,64,3072]{2,1,0:T(8,128)S(1)}) custom-call(s32[1]{0:T(128)} %bitcast.y_ref, bf16[2,128,768]{2,1,0:T(8,128)(2,1)S(1)} %maximum_select_fusion.2.mine.refs_8_, bf16[2,128,768]{2,1,0:T(8,128)(2,1)S(1)} %collective-permute-done.17.other.refs_9_, bf16[1536,3072]{1,0:T(8,128)(2,1)S(1)} %bitcast.8, ...), custom_call_target="tpu_custom_call" | custom-call | tf_op jit(solution)/shard_map/pallas_call | solution.py:111
  113.0 1.8 collective-permute-start.27
  114.8 3.7 %copy-done.2 = bf16[1536,3072]{1,0:T(8,128)(2,1)S(1)} copy-done((bf16[1536,3072]{1,0:T(8,128)(2,1)S(1)}, bf16[1536,3072]{1,0:T(8,128)(2,1)}, u32[]{:S(2)}) %copy-start.2) | copy-done | bytes 9437208
  118.5 3.7 %copy-done.5 = bf16[3072,1536]{1,0:T(8,128)(2,1)S(1)} copy-done((bf16[3072,1536]{1,0:T(8,128)(2,1)S(1)}, bf16[3072,1536]{1,0:T(8,128)(2,1)}, u32[]{:S(2)}) %copy-start.5) | copy-done | bytes 9437208
  122.2 4.7 %shard_map.79 = (bf16[2,128,768]{2,1,0:T(8,128)(2,1)S(1)}, f32[2,128,768]{2,1,0:T(8,128)S(1)}) custom-call(s32[1]{0:T(128)} %bitcast.y_ref, bf16[2,64,3072]{2,1,0:T(8,128)(2,1)S(1)} %pad_maximum_fusion.own.refs_2_, bf16[2,64,3072]{2,1,0:T(8,128)(2,1)S(1)} %collective-permute-done.18.got.refs_3_, bf16[1536,3072]{1,0:T(8,128)(2,1)S(1)} %copy-done.2, ...), custom_call_target="tpu_custom_call" | custom-call | tf_op jit(solution)/shard_map/pallas_call | solution.py:122
  126.9 1.6 collective-permute-start.20
  128.5 5.2 %shard_map.80 = (bf16[2,64,3072]{2,1,0:T(8,128)(2,1)S(1)}, f32[2,64,3072]{2,1,0:T(8,128)S(1)}) custom-call(s32[1]{0:T(128)} %bitcast.y_ref, bf16[2,128,768]{2,1,0:T(8,128)(2,1)S(1)} %copy-done.12, bf16[2,128,768]{2,1,0:T(8,128)(2,1)S(1)} %collective-permute-done.22.other.refs_13_, bf16[1536,3072]{1,0:T(8,128)(2,1)S(1)} %copy-done.2, ...), custom_call_target="tpu_custom_call" | custom-call | tf_op jit(solution)/shard_map/pallas_call | solution.py:111
  133.9 1.6 convert_add_fusion.3
  139.2 4.7 %shard_map.81 = (bf16[2,128,768]{2,1,0:T(8,128)(2,1)S(1)}, f32[2,128,768]{2,1,0:T(8,128)S(1)}) custom-call(s32[1]{0:T(128)} %bitcast.y_ref, bf16[2,64,3072]{2,1,0:T(8,128)(2,1)S(1)} %pad_maximum_fusion.1.own.refs_6_, bf16[2,64,3072]{2,1,0:T(8,128)(2,1)S(1)} %collective-permute-done.24.got.refs_7_, bf16[1536,3072]{1,0:T(8,128)(2,1)S(1)} %bitcast.10, ...), custom_call_target="tpu_custom_call" | custom-call | tf_op jit(solution)/shard_map/pallas_call | solution.py:122
  144.0 1.6 collective-permute-start.30
  145.7 3.9 %collective-permute-start.26 = (bf16[2,32,768]{2,1,0:T(8,128)(2,1)S(1)}, bf16[2,32,768]{2,1,0:T(8,128)(2,1)S(1)}, u32[]{:S(2)}, u32[]{:S(2)}) collective-permute-start(bf16[2,32,768]{2,1,0:T(8,128)(2,1)S(1)} %slice.187), channel_id=1, source_target_pairs={{0,4},{1,5},{2,6},{3,7},{4,0},{5,1},{6,2},{7,3},{8,12},{9,13},{10,... | collective-permute-start | bytes 294920 | tf_op jit(solution)/shard_map/ppermute | solution.py:41
  151.5 1.7 collective-permute-done.26
  155.8 4.7 %shard_map.82 = (bf16[2,128,768]{2,1,0:T(8,128)(2,1)S(1)}, f32[2,128,768]{2,1,0:T(8,128)S(1)}) custom-call(s32[1]{0:T(128)} %bitcast.y_ref, bf16[2,64,3072]{2,1,0:T(8,128)(2,1)S(1)} %pad_maximum_fusion.2.own.refs_10_, bf16[2,64,3072]{2,1,0:T(8,128)(2,1)S(1)} %collective-permute-done.32.got.refs_11_, bf16[1536,3072]{1,0:T(8,128)(2,1)S(1)} %bitcast.10, ...), custom_call_target="tpu_custom_call" | custom-call | tf_op jit(solution)/shard_map/pallas_call | solution.py:122
  160.7 4.0 %collective-permute-done.29 = bf16[2,64,3072]{2,1,0:T(8,128)(2,1)S(1)} collective-permute-done((bf16[2,64,3072]{2,1,0:T(8,128)(2,1)S(1)}, bf16[2,64,3072]{2,1,0:T(8,128)(2,1)S(1)}, u32[]{:S(2)}, u32[]{:S(2)}) %collective-permute-start.29) | collective-permute-done | bytes 786464 | tf_op jit(solution)/shard_map/ppermute | solution.py:41
  166.1 2.0 collective-permute-start.34
  168.0 5.9 %collective-permute-done.34 = bf16[2,32,768]{2,1,0:T(8,128)(2,1)S(1)} collective-permute-done((bf16[2,32,768]{2,1,0:T(8,128)(2,1)S(1)}, bf16[2,32,768]{2,1,0:T(8,128)(2,1)S(1)}, u32[]{:S(2)}, u32[]{:S(2)}) %collective-permute-start.34) | collective-permute-done | bytes 98336 | tf_op jit(solution)/shard_map/ppermute | solution.py:41
  174.0 4.9 %shard_map.83 = (bf16[2,128,768]{2,1,0:T(8,128)(2,1)S(1)}, f32[2,128,768]{2,1,0:T(8,128)S(1)}) custom-call(s32[1]{0:T(128)} %bitcast.y_ref, bf16[2,64,3072]{2,1,0:T(8,128)(2,1)S(1)} %pad_maximum_fusion.3.own.refs_14_, bf16[2,64,3072]{2,1,0:T(8,128)(2,1)S(1)} %collective-permute-done.33.got.refs_15_, bf16[1536,3072]{1,0:T(8,128)(2,1)S(1)} %bitcast.10, ...), custom_call_target="tpu_custom_call" | custom-call | tf_op jit(solution)/shard_map/pallas_call | solution.py:122
  178.9 1.6 collective-permute-start.35
  180.5 3.1 %collective-permute-start.28 = (bf16[2,32,768]{2,1,0:T(8,128)(2,1)S(1)}, bf16[2,32,768]{2,1,0:T(8,128)(2,1)S(1)}, u32[]{:S(2)}, u32[]{:S(2)}) collective-permute-start(bf16[2,32,768]{2,1,0:T(8,128)(2,1)S(1)} %fusion.31), channel_id=1, source_target_pairs={{0,0},{1,1},{2,8},{3,9},{4,16},{5,17},{6,24},{7,25},{8,2},{9,3},{1... | collective-permute-start | bytes 294920 | tf_op jit(solution)/shard_map/ppermute | solution.py:49
  183.6 4.5 %collective-permute-start.37 = (bf16[2,32,768]{2,1,0:T(8,128)(2,1)S(1)}, bf16[2,32,768]{2,1,0:T(8,128)(2,1)S(1)}, u32[]{:S(2)}, u32[]{:S(2)}) collective-permute-start(bf16[2,32,768]{2,1,0:T(8,128)(2,1)S(1)} %fusion.30), channel_id=1, source_target_pairs={{0,0},{1,1},{2,8},{3,9},{4,16},{5,17},{6,24},{7,25},{8,2},{9,3},{1... | collective-permute-start | bytes 294920 | tf_op jit(solution)/shard_map/ppermute | solution.py:49
  188.4 14.9 %shard_map.84 = bf16[1536,3072]{1,0:T(8,128)(2,1)} custom-call(s32[1]{0:T(128)} %bitcast.y_ref, bf16[2,128,768]{2,1,0:T(8,128)(2,1)S(1)} %maximum_select_fusion.mine.refs_0_, bf16[2,128,768]{2,1,0:T(8,128)(2,1)S(1)} %copy-done.14, bf16[2,64,3072]{2,1,0:T(8,128)(2,1)S(1)} %pad_maximum_fusion.own.refs_2_, ...), custom_call_target="tpu_custom_call" | custom-call | tf_op jit(solution)/shard_map/pallas_call | solution.py:171
  203.4 2.1 collective-permute-start.40
  205.6 6.1 %collective-permute-done.40 = bf16[2,64,768]{2,1,0:T(8,128)(2,1)S(1)} collective-permute-done((bf16[2,64,768]{2,1,0:T(8,128)(2,1)S(1)}, bf16[2,64,768]{2,1,0:T(8,128)(2,1)S(1)}, u32[]{:S(2)}, u32[]{:S(2)}) %collective-permute-start.40) | collective-permute-done | bytes 196640 | tf_op jit(solution)/shard_map/ppermute | solution.py:41
  212.8 4.8 %collective-permute-start.41 = (bf16[2,32,768]{2,1,0:T(8,128)(2,1)S(1)}, bf16[2,32,768]{2,1,0:T(8,128)(2,1)S(1)}, u32[]{:S(2)}, u32[]{:S(2)}) collective-permute-start(bf16[2,32,768]{2,1,0:T(8,128)(2,1)S(1)} %fusion.29), channel_id=1, source_target_pairs={{0,0},{1,1},{2,8},{3,9},{4,16},{5,17},{6,24},{7,25},{8,2},{9,3},{1... | collective-permute-start | bytes 294920 | tf_op jit(solution)/shard_map/ppermute | solution.py:49
  218.5 4.6 %collective-permute-start.43 = (bf16[2,32,768]{2,1,0:T(8,128)(2,1)S(1)}, bf16[2,32,768]{2,1,0:T(8,128)(2,1)S(1)}, u32[]{:S(2)}, u32[]{:S(2)}) collective-permute-start(bf16[2,32,768]{2,1,0:T(8,128)(2,1)S(1)} %fusion.28), channel_id=1, source_target_pairs={{0,0},{1,1},{2,8},{3,9},{4,16},{5,17},{6,24},{7,25},{8,2},{9,3},{1... | collective-permute-start | bytes 294920 | tf_op jit(solution)/shard_map/ppermute | solution.py:49
  223.1 12.2 %shard_map.85 = bf16[3072,1536]{1,0:T(8,128)(2,1)} custom-call(s32[1]{0:T(128)} %bitcast.y_ref, bf16[2,128,768]{2,1,0:T(8,128)(2,1)S(1)} %maximum_select_fusion.mine.refs_0_, bf16[2,128,768]{2,1,0:T(8,128)(2,1)S(1)} %copy-done.14, bf16[2,64,3072]{2,1,0:T(8,128)(2,1)S(1)} %pad_maximum_fusion.own.refs_2_, ...), custom_call_target="tpu_custom_call" | custom-call | tf_op jit(solution)/shard_map/pallas_call | solution.py:171
  (168 shorter events, 27.3 us)
Async XLA Ops:
  1.6 21.5 %collective-permute-start = (bf16[2,32,768]{2,1,0:T(8,128)(2,1)S(1)}, bf16[2,32,768]{2,1,0:T(8,128)(2,1)S(1)}, u32[]{:S(2)}, u32[]{:S(2)}) collective-permute-start(bf16[2,32,768]{2,1,0:T(8,128)(2,1)S(1)} %get-tuple-element.151), channel_id=1, source_target_pairs={{0,0},{1,1},{2,8},{3,9},{4,16},{5,17},{6,24},{7,25},{8,2},{9,3},{1... | collective-permute-start | bytes 294920 | tf_op jit(solution)/shard_map/ppermute | solution.py:49
  20.0 12.6 %collective-permute-start.2 = (bf16[2,32,768]{2,1,0:T(8,128)(2,1)S(1)}, bf16[2,32,768]{2,1,0:T(8,128)(2,1)S(1)}, u32[]{:S(2)}, u32[]{:S(2)}) collective-permute-start(bf16[2,32,768]{2,1,0:T(8,128)(2,1)S(1)} %get-tuple-element.74), channel_id=1, source_target_pairs={{0,0},{1,1},{2,8},{3,9},{4,16},{5,17},{6,24},{7,25},{8,2},{9,3},{1... | collective-permute-start | bytes 294920 | tf_op jit(solution)/shard_map/ppermute | solution.py:49
  23.2 9.4 %collective-permute-start.1 = (bf16[2,32,768]{2,1,0:T(8,128)(2,1)S(1)}, bf16[2,32,768]{2,1,0:T(8,128)(2,1)S(1)}, u32[]{:S(2)}, u32[]{:S(2)}) collective-permute-start(bf16[2,32,768]{2,1,0:T(8,128)(2,1)S(1)} %collective-permute-done), channel_id=1, source_target_pairs={{0,4},{1,5},{2,6},{3,7},{4,0},{5,1},{6,2},{7,3},{8,12},{9,13},{10,... | collective-permute-start | bytes 294920 | tf_op jit(solution)/shard_map/ppermute | solution.py:41
  32.6 5.6 %collective-permute-start.4 = (bf16[2,32,768]{2,1,0:T(8,128)(2,1)S(1)}, bf16[2,32,768]{2,1,0:T(8,128)(2,1)S(1)}, u32[]{:S(2)}, u32[]{:S(2)}) collective-permute-start(bf16[2,32,768]{2,1,0:T(8,128)(2,1)S(1)} %collective-permute-done.2), channel_id=1, source_target_pairs={{0,4},{1,5},{2,6},{3,7},{4,0},{5,1},{6,2},{7,3},{8,12},{9,13},{10,... | collective-permute-start | bytes 294920 | tf_op jit(solution)/shard_map/ppermute | solution.py:41
  32.6 9.3 %collective-permute-start.3 = (bf16[2,64,768]{2,1,0:T(8,128)(2,1)S(1)}, bf16[2,64,768]{2,1,0:T(8,128)(2,1)S(1)}, u32[]{:S(2)}, u32[]{:S(2)}) collective-permute-start(bf16[2,64,768]{2,1,0:T(8,128)(2,1)S(1)} %constant_dynamic-update-slice_fusion), channel_id=1, source_target_pairs={{0,2},{1,3},{2,0},{3,1},{4,6},{5,7},{6,4},{7,5},{8,10},{9,11},{10,... | collective-permute-start | bytes 589832 | tf_op jit(solution)/shard_map/ppermute | solution.py:41
  38.2 11.5 %collective-permute-start.8 = (bf16[2,64,768]{2,1,0:T(8,128)(2,1)S(1)}, bf16[2,64,768]{2,1,0:T(8,128)(2,1)S(1)}, u32[]{:S(2)}, u32[]{:S(2)}) collective-permute-start(bf16[2,64,768]{2,1,0:T(8,128)(2,1)S(1)} %constant_dynamic-update-slice_fusion.2), channel_id=1, source_target_pairs={{0,2},{1,3},{2,0},{3,1},{4,6},{5,7},{6,4},{7,5},{8,10},{9,11},{10,... | collective-permute-start | bytes 589832 | tf_op jit(solution)/shard_map/ppermute | solution.py:41
  38.2 11.4 %collective-permute-start.6 = (bf16[2,32,768]{2,1,0:T(8,128)(2,1)S(1)}, bf16[2,32,768]{2,1,0:T(8,128)(2,1)S(1)}, u32[]{:S(2)}, u32[]{:S(2)}) collective-permute-start(bf16[2,32,768]{2,1,0:T(8,128)(2,1)S(1)} %get-tuple-element.78), channel_id=1, source_target_pairs={{0,0},{1,1},{2,8},{3,9},{4,16},{5,17},{6,24},{7,25},{8,2},{9,3},{1... | collective-permute-start | bytes 294920 | tf_op jit(solution)/shard_map/ppermute | solution.py:49
  41.9 41.5 %slice-start = ((s8[9437184]{0:T(1024)(128)(4,1)}), s8[1048576]{0:T(1024)(128)(4,1)S(1)}, s32[]{:S(2)}) async-start(s8[9437184]{0:T(1024)(128)(4,1)} %bitcast.7), calls=%async_computation | async-start | bytes 2097152
  42.0 14.2 %collective-permute-start.5 = (bf16[2,128,768]{2,1,0:T(8,128)(2,1)S(1)}, bf16[2,128,768]{2,1,0:T(8,128)(2,1)S(1)}, u32[]{:S(2)}, u32[]{:S(2)}) collective-permute-start(bf16[2,128,768]{2,1,0:T(8,128)(2,1)S(1)} %maximum_select_fusion.mine.refs_0_), channel_id=1, source_target_pairs={{0,1},{1,0},{2,3},{3,2},{4,5},{5,4},{6,7},{7,6},{8,9},{9,8},{10,11... | collective-permute-start | bytes 1179656 | tf_op jit(solution)/shard_map/ppermute | solution.py:41
  49.7 6.5 %collective-permute-start.7 = (bf16[2,32,768]{2,1,0:T(8,128)(2,1)S(1)}, bf16[2,32,768]{2,1,0:T(8,128)(2,1)S(1)}, u32[]{:S(2)}, u32[]{:S(2)}) collective-permute-start(bf16[2,32,768]{2,1,0:T(8,128)(2,1)S(1)} %collective-permute-done.6), channel_id=1, source_target_pairs={{0,4},{1,5},{2,6},{3,7},{4,0},{5,1},{6,2},{7,3},{8,12},{9,13},{10,... | collective-permute-start | bytes 294920 | tf_op jit(solution)/shard_map/ppermute | solution.py:41
  49.8 33.7 %copy-start.8 = (bf16[2,128,768]{2,1,0:T(8,128)(2,1)}, bf16[2,128,768]{2,1,0:T(8,128)(2,1)S(1)}, u32[]{:S(2)}) copy-start(bf16[2,128,768]{2,1,0:T(8,128)(2,1)S(1)} %maximum_select_fusion.1.mine.refs_4_) | copy-start | bytes 1179652
  63.7 19.7 %slice-start.2 = ((s8[9437184]{0:T(1024)(128)(4,1)}), s8[4194304]{0:T(1024)(128)(4,1)S(1)}, s32[]{:S(2)}) async-start(s8[9437184]{0:T(1024)(128)(4,1)} %bitcast.7), calls=%async_computation.2 | async-start | bytes 8388608
  69.0 7.5 %collective-permute-start.9 = (bf16[2,64,3072]{2,1,0:T(8,128)(2,1)S(1)}, bf16[2,64,3072]{2,1,0:T(8,128)(2,1)S(1)}, u32[]{:S(2)}, u32[]{:S(2)}) collective-permute-start(bf16[2,64,3072]{2,1,0:T(8,128)(2,1)S(1)} %get-tuple-element.88), channel_id=1, source_target_pairs={{0,8},{8,0},{16,24},{24,16},{1,9},{9,1},{17,25},{25,17},{2,10},{10... | collective-permute-start | bytes 2359304 | tf_op jit(solution)/shard_map/ppermute | solution.py:41
  69.0 7.3 %collective-permute-start.10 = (bf16[2,64,768]{2,1,0:T(8,128)(2,1)S(1)}, bf16[2,64,768]{2,1,0:T(8,128)(2,1)S(1)}, u32[]{:S(2)}, u32[]{:S(2)}) collective-permute-start(bf16[2,64,768]{2,1,0:T(8,128)(2,1)S(1)} %constant_dynamic-update-slice_fusion.4), channel_id=1, source_target_pairs={{0,2},{1,3},{2,0},{3,1},{4,6},{5,7},{6,4},{7,5},{8,10},{9,11},{10,... | collective-permute-start | bytes 589832 | tf_op jit(solution)/shard_map/ppermute | solution.py:41
  69.1 11.4 %collective-permute-start.12 = (bf16[2,32,768]{2,1,0:T(8,128)(2,1)S(1)}, bf16[2,32,768]{2,1,0:T(8,128)(2,1)S(1)}, u32[]{:S(2)}, u32[]{:S(2)}) collective-permute-start(bf16[2,32,768]{2,1,0:T(8,128)(2,1)S(1)} %get-tuple-element.82), channel_id=1, source_target_pairs={{0,0},{1,1},{2,8},{3,9},{4,16},{5,17},{6,24},{7,25},{8,2},{9,3},{1... | collective-permute-start | bytes 294920 | tf_op jit(solution)/shard_map/ppermute | solution.py:49
  72.8 10.7 %collective-permute-start.14 = (bf16[2,128,768]{2,1,0:T(8,128)(2,1)S(1)}, bf16[2,128,768]{2,1,0:T(8,128)(2,1)S(1)}, u32[]{:S(2)}, u32[]{:S(2)}) collective-permute-start(bf16[2,128,768]{2,1,0:T(8,128)(2,1)S(1)} %maximum_select_fusion.1.mine.refs_4_), channel_id=1, source_target_pairs={{0,1},{1,0},{2,3},{3,2},{4,5},{5,4},{6,7},{7,6},{8,9},{9,8},{10,11... | collective-permute-start | bytes 1179656 | tf_op jit(solution)/shard_map/ppermute | solution.py:41
  76.4 23.9 %copy-start.10 = (bf16[2,128,768]{2,1,0:T(8,128)(2,1)}, bf16[2,128,768]{2,1,0:T(8,128)(2,1)S(1)}, u32[]{:S(2)}) copy-start(bf16[2,128,768]{2,1,0:T(8,128)(2,1)S(1)} %maximum_select_fusion.2.mine.refs_8_) | copy-start | bytes 1179652
  88.7 17.8 %collective-permute-start.16 = (bf16[2,64,3072]{2,1,0:T(8,128)(2,1)S(1)}, bf16[2,64,3072]{2,1,0:T(8,128)(2,1)S(1)}, u32[]{:S(2)}, u32[]{:S(2)}) collective-permute-start(bf16[2,64,3072]{2,1,0:T(8,128)(2,1)S(1)} %get-tuple-element.93), channel_id=1, source_target_pairs={{0,8},{8,0},{16,24},{24,16},{1,9},{9,1},{17,25},{25,17},{2,10},{10... | collective-permute-start | bytes 2359304 | tf_op jit(solution)/shard_map/ppermute | solution.py:41
  88.8 11.5 %collective-permute-start.17 = (bf16[2,128,768]{2,1,0:T(8,128)(2,1)S(1)}, bf16[2,128,768]{2,1,0:T(8,128)(2,1)S(1)}, u32[]{:S(2)}, u32[]{:S(2)}) collective-permute-start(bf16[2,128,768]{2,1,0:T(8,128)(2,1)S(1)} %maximum_select_fusion.2.mine.refs_8_), channel_id=1, source_target_pairs={{0,1},{1,0},{2,3},{3,2},{4,5},{5,4},{6,7},{7,6},{8,9},{9,8},{10,11... | collective-permute-start | bytes 1179656 | tf_op jit(solution)/shard_map/ppermute | solution.py:41
  90.4 19.6 %collective-permute-start.11 = (bf16[2,64,3072]{2,1,0:T(8,128)(2,1)S(1)}, bf16[2,64,3072]{2,1,0:T(8,128)(2,1)S(1)}, u32[]{:S(2)}, u32[]{:S(2)}) collective-permute-start(bf16[2,64,3072]{2,1,0:T(8,128)(2,1)S(1)} %fusion), channel_id=1, source_target_pairs={{0,16},{8,24},{16,0},{24,8},{1,17},{9,25},{17,1},{25,9},{2,18},{10... | collective-permute-start | bytes 2359304 | tf_op jit(solution)/shard_map/ppermute | solution.py:41
  90.4 8.7 %collective-permute-start.13 = (bf16[2,32,768]{2,1,0:T(8,128)(2,1)S(1)}, bf16[2,32,768]{2,1,0:T(8,128)(2,1)S(1)}, u32[]{:S(2)}, u32[]{:S(2)}) collective-permute-start(bf16[2,32,768]{2,1,0:T(8,128)(2,1)S(1)} %collective-permute-done.12), channel_id=1, source_target_pairs={{0,4},{1,5},{2,6},{3,7},{4,0},{5,1},{6,2},{7,3},{8,12},{9,13},{10,... | collective-permute-start | bytes 294920 | tf_op jit(solution)/shard_map/ppermute | solution.py:41
  99.1 8.6 %collective-permute-start.15 = (bf16[2,64,768]{2,1,0:T(8,128)(2,1)S(1)}, bf16[2,64,768]{2,1,0:T(8,128)(2,1)S(1)}, u32[]{:S(2)}, u32[]{:S(2)}) collective-permute-start(bf16[2,64,768]{2,1,0:T(8,128)(2,1)S(1)} %constant_dynamic-update-slice_fusion.6), channel_id=1, source_target_pairs={{0,2},{1,3},{2,0},{3,1},{4,6},{5,7},{6,4},{7,5},{8,10},{9,11},{10,... | collective-permute-start | bytes 589832 | tf_op jit(solution)/shard_map/ppermute | solution.py:41
  106.5 5.1 %collective-permute-start.19 = (bf16[2,64,3072]{2,1,0:T(8,128)(2,1)}, bf16[2,64,3072]{2,1,0:T(8,128)(2,1)}, u32[]{:S(2)}, u32[]{:S(2)}) collective-permute-start(bf16[2,64,3072]{2,1,0:T(8,128)(2,1)} %get-tuple-element.97), channel_id=1, source_target_pairs={{0,8},{8,0},{16,24},{24,16},{1,9},{9,1},{17,25},{25,17},{2,10},{10... | collective-permute-start | bytes 2359304 | tf_op jit(solution)/shard_map/ppermute | solution.py:41
  110.7 4.1 %collective-permute-start.18 = (bf16[2,64,3072]{2,1,0:T(8,128)(2,1)S(1)}, bf16[2,64,3072]{2,1,0:T(8,128)(2,1)S(1)}, u32[]{:S(2)}, u32[]{:S(2)}) collective-permute-start(bf16[2,64,3072]{2,1,0:T(8,128)(2,1)S(1)} %pad_maximum_fusion.own.refs_2_), channel_id=1, source_target_pairs={{0,8},{8,0},{16,24},{24,16},{1,9},{9,1},{17,25},{25,17},{2,10},{10... | collective-permute-start | bytes 2359304 | tf_op jit(solution)/shard_map/ppermute | solution.py:41
  110.8 23.1 %collective-permute-start.21 = (bf16[2,64,3072]{2,1,0:T(8,128)(2,1)}, bf16[2,64,3072]{2,1,0:T(8,128)(2,1)}, u32[]{:S(2)}, u32[]{:S(2)}) collective-permute-start(bf16[2,64,3072]{2,1,0:T(8,128)(2,1)} %fusion.1), channel_id=1, source_target_pairs={{0,16},{8,24},{16,0},{24,8},{1,17},{9,25},{17,1},{25,9},{2,18},{10... | collective-permute-start | bytes 2359304 | tf_op jit(solution)/shard_map/ppermute | solution.py:41
  111.1 17.4 %collective-permute-start.22 = (bf16[2,128,768]{2,1,0:T(8,128)(2,1)}, bf16[2,128,768]{2,1,0:T(8,128)(2,1)S(1)}, u32[]{:S(2)}, u32[]{:S(2)}) collective-permute-start(bf16[2,128,768]{2,1,0:T(8,128)(2,1)} %maximum_select_fusion.3.mine.refs_12_), channel_id=1, source_target_pairs={{0,1},{1,0},{2,3},{3,2},{4,5},{5,4},{6,7},{7,6},{8,9},{9,8},{10,11... | collective-permute-start | bytes 1179656 | tf_op jit(solution)/shard_map/ppermute | solution.py:41
  113.0 36.5 %collective-permute-start.27 = (bf16[2,64,3072]{2,1,0:T(8,128)(2,1)S(1)}, bf16[2,64,3072]{2,1,0:T(8,128)(2,1)S(1)}, u32[]{:S(2)}, u32[]{:S(2)}) collective-permute-start(bf16[2,64,3072]{2,1,0:T(8,128)(2,1)S(1)} %fusion.2), channel_id=1, source_target_pairs={{0,16},{8,24},{16,0},{24,8},{1,17},{9,25},{17,1},{25,9},{2,18},{10... | collective-permute-start | bytes 2359304 | tf_op jit(solution)/shard_map/ppermute | solution.py:41
  126.9 10.7 %collective-permute-start.20 = (bf16[2,128,768]{2,1,0:T(8,128)(2,1)S(1)}, bf16[2,128,768]{2,1,0:T(8,128)(2,1)S(1)}, u32[]{:S(2)}, u32[]{:S(2)}) collective-permute-start(bf16[2,128,768]{2,1,0:T(8,128)(2,1)S(1)} %get-tuple-element.105), channel_id=1, source_target_pairs={{0,1},{1,0},{2,3},{3,2},{4,5},{5,4},{6,7},{7,6},{8,9},{9,8},{10,11... | collective-permute-start | bytes 1179656 | tf_op jit(solution)/shard_map/ppermute | solution.py:41
  133.8 4.8 %collective-permute-start.25 = (bf16[2,64,3072]{2,1,0:T(8,128)(2,1)S(1)}, bf16[2,64,3072]{2,1,0:T(8,128)(2,1)S(1)}, u32[]{:S(2)}, u32[]{:S(2)}) collective-permute-start(bf16[2,64,3072]{2,1,0:T(8,128)(2,1)S(1)} %get-tuple-element.107), channel_id=1, source_target_pairs={{0,8},{8,0},{16,24},{24,16},{1,9},{9,1},{17,25},{25,17},{2,10},{10... | collective-permute-start | bytes 2359304 | tf_op jit(solution)/shard_map/ppermute | solution.py:41
  135.9 3.2 %collective-permute-start.24 = (bf16[2,64,3072]{2,1,0:T(8,128)(2,1)S(1)}, bf16[2,64,3072]{2,1,0:T(8,128)(2,1)S(1)}, u32[]{:S(2)}, u32[]{:S(2)}) collective-permute-start(bf16[2,64,3072]{2,1,0:T(8,128)(2,1)S(1)} %pad_maximum_fusion.1.own.refs_6_), channel_id=1, source_target_pairs={{0,8},{8,0},{16,24},{24,16},{1,9},{9,1},{17,25},{25,17},{2,10},{10... | collective-permute-start | bytes 2359304 | tf_op jit(solution)/shard_map/ppermute | solution.py:41
  137.7 7.9 %collective-permute-start.23 = (bf16[2,64,768]{2,1,0:T(8,128)(2,1)S(1)}, bf16[2,64,768]{2,1,0:T(8,128)(2,1)S(1)}, u32[]{:S(2)}, u32[]{:S(2)}) collective-permute-start(bf16[2,64,768]{2,1,0:T(8,128)(2,1)S(1)} %dynamic-slice_convert_fusion.3), channel_id=1, source_target_pairs={{0,2},{1,3},{2,0},{3,1},{4,6},{5,7},{6,4},{7,5},{8,10},{9,11},{10,... | collective-permute-start | bytes 589832 | tf_op jit(solution)/shard_map/ppermute | solution.py:41
  138.8 25.9 %collective-permute-start.29 = (bf16[2,64,3072]{2,1,0:T(8,128)(2,1)S(1)}, bf16[2,64,3072]{2,1,0:T(8,128)(2,1)S(1)}, u32[]{:S(2)}, u32[]{:S(2)}) collective-permute-start(bf16[2,64,3072]{2,1,0:T(8,128)(2,1)S(1)} %fusion.3), channel_id=1, source_target_pairs={{0,16},{8,24},{16,0},{24,8},{1,17},{9,25},{17,1},{25,9},{2,18},{10... | collective-permute-start | bytes 2359304 | tf_op jit(solution)/shard_map/ppermute | solution.py:41
  144.0 10.8 %collective-permute-start.30 = (bf16[2,128,768]{2,1,0:T(8,128)(2,1)S(1)}, bf16[2,128,768]{2,1,0:T(8,128)(2,1)S(1)}, u32[]{:S(2)}, u32[]{:S(2)}) collective-permute-start(bf16[2,128,768]{2,1,0:T(8,128)(2,1)S(1)} %get-tuple-element.113), channel_id=1, source_target_pairs={{0,1},{1,0},{2,3},{3,2},{4,5},{5,4},{6,7},{7,6},{8,9},{9,8},{10,11... | collective-permute-start | bytes 1179656 | tf_op jit(solution)/shard_map/ppermute | solution.py:41
  145.7 7.5 %collective-permute-start.26 = (bf16[2,32,768]{2,1,0:T(8,128)(2,1)S(1)}, bf16[2,32,768]{2,1,0:T(8,128)(2,1)S(1)}, u32[]{:S(2)}, u32[]{:S(2)}) collective-permute-start(bf16[2,32,768]{2,1,0:T(8,128)(2,1)S(1)} %slice.187), channel_id=1, source_target_pairs={{0,4},{1,5},{2,6},{3,7},{4,0},{5,1},{6,2},{7,3},{8,12},{9,13},{10,... | collective-permute-start | bytes 294920 | tf_op jit(solution)/shard_map/ppermute | solution.py:41
  151.4 4.4 %collective-permute-start.32 = (bf16[2,64,3072]{2,1,0:T(8,128)(2,1)S(1)}, bf16[2,64,3072]{2,1,0:T(8,128)(2,1)S(1)}, u32[]{:S(2)}, u32[]{:S(2)}) collective-permute-start(bf16[2,64,3072]{2,1,0:T(8,128)(2,1)S(1)} %pad_maximum_fusion.2.own.refs_10_), channel_id=1, source_target_pairs={{0,8},{8,0},{16,24},{24,16},{1,9},{9,1},{17,25},{25,17},{2,10},{10... | collective-permute-start | bytes 2359304 | tf_op jit(solution)/shard_map/ppermute | solution.py:41
  154.9 5.7 %collective-permute-start.31 = (bf16[2,64,768]{2,1,0:T(8,128)(2,1)S(1)}, bf16[2,64,768]{2,1,0:T(8,128)(2,1)S(1)}, u32[]{:S(2)}, u32[]{:S(2)}) collective-permute-start(bf16[2,64,768]{2,1,0:T(8,128)(2,1)S(1)} %dynamic-slice_convert_fusion.2), channel_id=1, source_target_pairs={{0,2},{1,3},{2,0},{3,1},{4,6},{5,7},{6,4},{7,5},{8,10},{9,11},{10,... | collective-permute-start | bytes 589832 | tf_op jit(solution)/shard_map/ppermute | solution.py:41
  165.4 8.6 %collective-permute-start.33 = (bf16[2,64,3072]{2,1,0:T(8,128)(2,1)S(1)}, bf16[2,64,3072]{2,1,0:T(8,128)(2,1)S(1)}, u32[]{:S(2)}, u32[]{:S(2)}) collective-permute-start(bf16[2,64,3072]{2,1,0:T(8,128)(2,1)S(1)} %pad_maximum_fusion.3.own.refs_14_), channel_id=1, source_target_pairs={{0,8},{8,0},{16,24},{24,16},{1,9},{9,1},{17,25},{25,17},{2,10},{10... | collective-permute-start | bytes 2359304 | tf_op jit(solution)/shard_map/ppermute | solution.py:41
  165.5 22.7 %collective-permute-start.36 = (bf16[2,128,768]{2,1,0:T(8,128)(2,1)S(1)}, bf16[2,128,768]{2,1,0:T(8,128)(2,1)S(1)}, u32[]{:S(2)}, u32[]{:S(2)}) collective-permute-start(bf16[2,128,768]{2,1,0:T(8,128)(2,1)S(1)} %get-tuple-element.120), channel_id=1, source_target_pairs={{0,1},{1,0},{2,3},{3,2},{4,5},{5,4},{6,7},{7,6},{8,9},{9,8},{10,11... | collective-permute-start | bytes 1179656 | tf_op jit(solution)/shard_map/ppermute | solution.py:41
  166.1 7.9 %collective-permute-start.34 = (bf16[2,32,768]{2,1,0:T(8,128)(2,1)S(1)}, bf16[2,32,768]{2,1,0:T(8,128)(2,1)S(1)}, u32[]{:S(2)}, u32[]{:S(2)}) collective-permute-start(bf16[2,32,768]{2,1,0:T(8,128)(2,1)S(1)} %slice.186), channel_id=1, source_target_pairs={{0,4},{1,5},{2,6},{3,7},{4,0},{5,1},{6,2},{7,3},{8,12},{9,13},{10,... | collective-permute-start | bytes 294920 | tf_op jit(solution)/shard_map/ppermute | solution.py:41
  178.9 24.4 %collective-permute-start.35 = (bf16[2,128,768]{2,1,0:T(8,128)(2,1)S(1)}, bf16[2,128,768]{2,1,0:T(8,128)(2,1)S(1)}, u32[]{:S(2)}, u32[]{:S(2)}) collective-permute-start(bf16[2,128,768]{2,1,0:T(8,128)(2,1)S(1)} %get-tuple-element.126), channel_id=1, source_target_pairs={{0,1},{1,0},{2,3},{3,2},{4,5},{5,4},{6,7},{7,6},{8,9},{9,8},{10,11... | collective-permute-start | bytes 1179656 | tf_op jit(solution)/shard_map/ppermute | solution.py:41
  180.5 25.0 %collective-permute-start.28 = (bf16[2,32,768]{2,1,0:T(8,128)(2,1)S(1)}, bf16[2,32,768]{2,1,0:T(8,128)(2,1)S(1)}, u32[]{:S(2)}, u32[]{:S(2)}) collective-permute-start(bf16[2,32,768]{2,1,0:T(8,128)(2,1)S(1)} %fusion.31), channel_id=1, source_target_pairs={{0,0},{1,1},{2,8},{3,9},{4,16},{5,17},{6,24},{7,25},{8,2},{9,3},{1... | collective-permute-start | bytes 294920 | tf_op jit(solution)/shard_map/ppermute | solution.py:49
  183.6 34.0 %collective-permute-start.37 = (bf16[2,32,768]{2,1,0:T(8,128)(2,1)S(1)}, bf16[2,32,768]{2,1,0:T(8,128)(2,1)S(1)}, u32[]{:S(2)}, u32[]{:S(2)}) collective-permute-start(bf16[2,32,768]{2,1,0:T(8,128)(2,1)S(1)} %fusion.30), channel_id=1, source_target_pairs={{0,0},{1,1},{2,8},{3,9},{4,16},{5,17},{6,24},{7,25},{8,2},{9,3},{1... | collective-permute-start | bytes 294920 | tf_op jit(solution)/shard_map/ppermute | solution.py:49
  188.3 17.2 %collective-permute-start.38 = (bf16[2,64,768]{2,1,0:T(8,128)(2,1)S(1)}, bf16[2,64,768]{2,1,0:T(8,128)(2,1)S(1)}, u32[]{:S(2)}, u32[]{:S(2)}) collective-permute-start(bf16[2,64,768]{2,1,0:T(8,128)(2,1)S(1)} %dynamic-slice_convert_fusion.1), channel_id=1, source_target_pairs={{0,2},{1,3},{2,0},{3,1},{4,6},{5,7},{6,4},{7,5},{8,10},{9,11},{10,... | collective-permute-start | bytes 589832 | tf_op jit(solution)/shard_map/ppermute | solution.py:41
  203.4 8.3 %collective-permute-start.40 = (bf16[2,64,768]{2,1,0:T(8,128)(2,1)S(1)}, bf16[2,64,768]{2,1,0:T(8,128)(2,1)S(1)}, u32[]{:S(2)}, u32[]{:S(2)}) collective-permute-start(bf16[2,64,768]{2,1,0:T(8,128)(2,1)S(1)} %dynamic-slice_convert_fusion), channel_id=1, source_target_pairs={{0,2},{1,3},{2,0},{3,1},{4,6},{5,7},{6,4},{7,5},{8,10},{9,11},{10,... | collective-permute-start | bytes 589832 | tf_op jit(solution)/shard_map/ppermute | solution.py:41
  205.5 7.3 %collective-permute-start.39 = (bf16[2,32,768]{2,1,0:T(8,128)(2,1)S(1)}, bf16[2,32,768]{2,1,0:T(8,128)(2,1)S(1)}, u32[]{:S(2)}, u32[]{:S(2)}) collective-permute-start(bf16[2,32,768]{2,1,0:T(8,128)(2,1)S(1)} %slice.185), channel_id=1, source_target_pairs={{0,4},{1,5},{2,6},{3,7},{4,0},{5,1},{6,2},{7,3},{8,12},{9,13},{10,... | collective-permute-start | bytes 294920 | tf_op jit(solution)/shard_map/ppermute | solution.py:41
  211.8 6.7 %collective-permute-start.42 = (bf16[2,32,768]{2,1,0:T(8,128)(2,1)S(1)}, bf16[2,32,768]{2,1,0:T(8,128)(2,1)S(1)}, u32[]{:S(2)}, u32[]{:S(2)}) collective-permute-start(bf16[2,32,768]{2,1,0:T(8,128)(2,1)S(1)} %slice.184), channel_id=1, source_target_pairs={{0,4},{1,5},{2,6},{3,7},{4,0},{5,1},{6,2},{7,3},{8,12},{9,13},{10,... | collective-permute-start | bytes 294920 | tf_op jit(solution)/shard_map/ppermute | solution.py:41
  212.8 22.5 %collective-permute-start.41 = (bf16[2,32,768]{2,1,0:T(8,128)(2,1)S(1)}, bf16[2,32,768]{2,1,0:T(8,128)(2,1)S(1)}, u32[]{:S(2)}, u32[]{:S(2)}) collective-permute-start(bf16[2,32,768]{2,1,0:T(8,128)(2,1)S(1)} %fusion.29), channel_id=1, source_target_pairs={{0,0},{1,1},{2,8},{3,9},{4,16},{5,17},{6,24},{7,25},{8,2},{9,3},{1... | collective-permute-start | bytes 294920 | tf_op jit(solution)/shard_map/ppermute | solution.py:49
  218.5 16.8 %collective-permute-start.43 = (bf16[2,32,768]{2,1,0:T(8,128)(2,1)S(1)}, bf16[2,32,768]{2,1,0:T(8,128)(2,1)S(1)}, u32[]{:S(2)}, u32[]{:S(2)}) collective-permute-start(bf16[2,32,768]{2,1,0:T(8,128)(2,1)S(1)} %fusion.28), channel_id=1, source_target_pairs={{0,0},{1,1},{2,8},{3,9},{4,16},{5,17},{6,24},{7,25},{8,2},{9,3},{1... | collective-permute-start | bytes 294920 | tf_op jit(solution)/shard_map/ppermute | solution.py:49
  (26 other events, 217.0 us)

commit v4 on v2

v4 whole, which is shorter than its diff:
```python
import functools

import jax
import jax.numpy as jnp
from jax import lax
from jax.experimental import pallas as pl
from jax.experimental.pallas import tpu as pltpu
from jax.sharding import PartitionSpec as P

SHARES = (3, 3, 2)
ORDER = (
    0, 0, 1, 0, 1, 0, 1, 2, 0, 1, 0, 2, 2, 1, 0, 2, 1, 2, 0, 2, 3, 1, 0, 1, 4, 0, 2, 1, 0, 2,
    5, 1, -1, 2, 1, 2, -1, 2, 0, 1, 2,
)


HBM = pl.BlockSpec(memory_space=pltpu.HBM)


def cdf_of(value):
    return 0.5 * (1.0 + lax.erf(value * 0.7071067811865476))


def contract(left, right, left_dim, right_dim):
    return lax.dot_general(
        left, right, (((left_dim,), (right_dim,)), ((), ())), preferred_element_type=jnp.float32
    )


def activations(sums):
    hidden_pre, grad_act = sums[0], sums[1]
    cumul = cdf_of(hidden_pre)
    density = jnp.exp(-0.5 * hidden_pre * hidden_pre) * 0.3989422804014327
    act = (hidden_pre * cumul).astype(jnp.bfloat16)
    return act, (grad_act * (cumul + hidden_pre * density)).astype(jnp.bfloat16)


def swap(value, axis, size, mask):
    return lax.ppermute(value, axis, [(i, i ^ mask) for i in range(size)])


def transposed(value, rows, cols):
    per = cols // rows
    pairs = [
        (r * cols + c, (c // per) * cols + r * per + c % per) for r in range(rows) for c in range(cols)
    ]
    return lax.ppermute(value, ("row", "col"), pairs)


def store_kernel(first, full, panel, *refs):
    arrays, sems = refs[-5:-1], refs[-1]
    rows = pl.ds(first, full.shape[1])
    sources = (panel.at[0], panel.at[1], full.at[0], full.at[1])
    copies = [
        pltpu.make_async_copy(source, array.at[rows], sems.at[i])
        for i, (source, array) in enumerate(zip(sources, arrays))
    ]
    for copy in copies:
        copy.start()
    for copy in copies:
        copy.wait()


def stored(full, panel, arrays, first, total):
    inputs = [full, panel, *(arrays or ())]
    shapes = [jax.ShapeDtypeStruct((total, a.shape[2]), jnp.bfloat16) for a in (panel, panel, full, full)]
    return pl.pallas_call(
        functools.partial(store_kernel, first),
        out_shape=shapes,
        in_specs=[pl.BlockSpec(memory_space=pl.ANY)] * len(inputs),
        out_specs=[HBM] * 4,
        scratch_shapes=[pltpu.SemaphoreType.DMA((4,))],
        input_output_aliases={2 + i: i for i in range(4)} if arrays else {},
        cost_estimate=pl.CostEstimate(flops=0, bytes_accessed=4 * full.size, transcendentals=0),
    )(*inputs)


class Clock:
    def __init__(self):
        self.last = None

    def start(self, value):
        if self.last is None:
            return value
        return lax.optimization_barrier((value, self.last))[0]

    def end(self, value):
        self.last = value
        return value


class Grid:
    def __init__(self, rows, cols, clock):
        self.rows, self.cols, self.clock = rows, cols, clock
        self.core = lax.axis_index("row") % 2
        self.y = lax.axis_index("col") % 2

    def gather(self, block):
        clock = self.clock
        block = transposed(clock.end(clock.start(block)), self.rows, self.cols)
        yield
        block = clock.end(clock.start(block))
        far = swap(block, "col", self.cols, 4)
        yield
        near = clock.end(jnp.concatenate([block, clock.start(far)], axis=1))
        far = swap(near, "col", self.cols, 2)
        yield
        far = clock.start(far)
        mine = jnp.where(
            self.core == 0,
            jnp.concatenate([near, far], axis=1),
            jnp.concatenate([far, near], axis=1),
        )
        mine = clock.end(mine)
        other = swap(mine, "col", self.cols, 1)
        yield
        other = clock.start(other)
        return jnp.where(
            self.y == 0,
            jnp.concatenate([mine, other], axis=2),
            jnp.concatenate([other, mine], axis=2),
        )

    def scatter(self, terms):
        clock = self.clock
        f, n = terms.shape[2] // 2, terms.shape[1] // 4
        away = lax.dynamic_slice_in_dim(terms, (1 - self.y) * f, f, axis=2).astype(jnp.bfloat16)
        away = clock.end(away)
        keep = lax.dynamic_slice_in_dim(terms, self.y * f, f, axis=2)
        got = swap(away, "col", self.cols, 1)
        yield
        total = keep + clock.start(got)
        away = lax.dynamic_slice_in_dim(total, (1 - self.core) * 2 * n, 2 * n, axis=1)
        away = clock.end(away.astype(jnp.bfloat16))
        keep = lax.dynamic_slice_in_dim(total, self.core * 2 * n, 2 * n, axis=1)
        got = swap(away, "col", self.cols, 2)
        yield
        total = keep + clock.start(got)
        away = clock.end(total[:, n:].astype(jnp.bfloat16))
        got = swap(away, "col", self.cols, 4)
        yield
        out = clock.end((total[:, :n] + clock.start(got)).astype(jnp.bfloat16))
        out = transposed(out, self.rows, self.cols)
        yield
        return clock.end(clock.start(out))


def part_steps(grid, block, weights, made):
    clock, rows = grid.clock, grid.rows
    weight_in, weight_out = weights
    panel = yield from grid.gather(block)
    half = panel.shape[1] // 2
    terms = jnp.stack([contract(panel[0], weight_in, 1, 0), contract(panel[1], weight_out, 1, 1)])
    away = clock.end(terms[:, half:].astype(jnp.bfloat16))
    got = swap(away, "row", rows, 1)
    yield
    sums = terms[:, :half] + clock.start(got)
    got = swap(clock.end(sums.astype(jnp.bfloat16)), "row", rows, 2)
    yield
    act, grad_pre = activations(sums + clock.start(got))
    own = clock.end(jnp.stack([act, grad_pre]))
    got = swap(own, "row", rows, 1)
    yield
    full = jnp.concatenate([own, clock.start(got)], axis=1)
    made["operands"] = full, panel
    terms = jnp.stack([contract(full[0], weight_out, 1, 0), contract(full[1], weight_in, 1, 1)])
    made["out"] = yield from grid.scatter(terms)


def body(rows, cols, tokens, weight_in, weight_out, out_grad):
    clock = Clock()
    grid = Grid(rows, cols, clock)
    both = jnp.stack([tokens, out_grad])
    count = tokens.shape[0]
    size = [count * share // sum(SHARES) for share in SHARES]
    start = [sum(size[:part]) for part in range(len(size))]
    made = [{} for _ in size]
    parts = [
        part_steps(grid, both[:, at : at + n], (weight_in, weight_out), out)
        for at, n, out in zip(start, size, made)
    ]
    arrays, grads = None, []
    for part in ORDER:
        if part < 0:
            panel, full = arrays[len(grads)], clock.start(arrays[3 - len(grads)])
            grad = contract(full, panel, 0, 0) if grads else contract(panel, full, 0, 0)
            grads.append(clock.end(grad.astype(jnp.bfloat16)))
        elif part >= len(parts):
            full, panel = made[part - len(parts)]["operands"]
            arrays = stored(clock.start(full), panel, arrays, rows * start[part - len(parts)], rows * count)
            clock.end(arrays[3])
        else:
            next(parts[part], None)
    out = jnp.concatenate([m["out"] for m in made], axis=1)
    return out[0], out[1], grads[0], grads[1]


def plain_body(rows, cols, tokens, weight_in, weight_out, out_grad):
    per = cols // rows
    both = jnp.stack([tokens, out_grad])
    two, n, f = both.shape
    panel = lax.all_gather(transposed(both, rows, cols), "col", axis=0)
    panel = panel.reshape(rows, per, two, n, f).transpose(2, 0, 3, 1, 4).reshape(two, rows * n, per * f)
    terms = jnp.stack([contract(panel[0], weight_in, 1, 0), contract(panel[1], weight_out, 1, 1)])
    act, grad_pre = activations(lax.psum_scatter(terms, "row", scatter_dimension=1, tiled=True))
    full = lax.all_gather(jnp.stack([act, grad_pre]), "row", axis=1, tiled=True)
    terms = jnp.stack([contract(full[0], weight_out, 1, 0), contract(full[1], weight_in, 1, 1)])
    terms = terms.reshape(two, rows, n, per, f).transpose(1, 3, 0, 2, 4).reshape(cols, two, n, f)
    out = lax.psum_scatter(terms, "col", scatter_dimension=0).astype(jnp.bfloat16)
    out = transposed(out, rows, cols)
    grad_in = contract(panel[0], full[1], 0, 0).astype(jnp.bfloat16)
    grad_out = contract(full[0], panel[1], 0, 0).astype(jnp.bfloat16)
    return out[0], out[1], grad_in, grad_out


def solution(mesh):
    shape = (mesh.shape["row"], mesh.shape["col"])
    return jax.shard_map(
        functools.partial(body if shape == (4, 8) else plain_body, *shape),
        mesh=mesh,
        in_specs=(P("row", "col"), P("row", "col"), P("col", "row"), P("row", "col")),
        out_specs=(P("row", "col"), P("row", "col"), P("row", "col"), P("col", "row")),
        check_vma=False,
    )
```

time: 251 us -> 539 us (2.15)
  the two profiles are of different devices: /device:TPU:3 before, /device:TPU:2 now
where the time goes in v4:
time: 539 us; the launch traced here: 538 us
  Pallas kernels  289 us (54%)
  waiting for transfers between devices  81.8 us (15%)
  matrix products  67.7 us (13%)
  starting transfers between devices  51.7 us (10%)
  other arithmetic  36.9 us (7%)
  local copies, waits for them, and re-layouts  9.37 us (2%)
    pallas_call x3, Pallas kernels, stored(): pl.pallas_call(functools.partial(store_kernel, first), out_shape=shapes,...  289 us
    dot_general x14, matrix products, contract(): lax.dot_general(left, right, (((left_dim,), (right_dim,)), ((), ())), pre...  67.7 us
    ppermute x27, waiting for transfers between devices, swap(): return lax.ppermute(value, axis, [(i, i ^ mask) for i in range(size)])  63.7 us
    ppermute x6, starting transfers between devices, transposed(): return lax.ppermute(value, ('row', 'col'), pairs)  26.7 us
    ppermute x27, starting transfers between devices, swap(): return lax.ppermute(value, axis, [(i, i ^ mask) for i in range(size)])  25 us
    ppermute x6, waiting for transfers between devices, transposed(): return lax.ppermute(value, ('row', 'col'), pairs)  18.1 us
  transfers between devices with their start and end apart: 33, of which 14 were waited for; matrix products, arithmetic and copies ran while one was open for 17% of the time, Pallas kernels for 54%

profile of v4, /device:TPU:2, one launch (start us, length us, event | category | flops | bytes accessed | tf_op | source)
XLA Modules:
  0.0 538.4 jit_solution(6309307206844869883)
XLA Ops:
  1.7 4.5 collective-permute-start
  6.2 8.6 %collective-permute-done = bf16[2,48,768]{2,1,0:T(8,128)(2,1)S(1)} collective-permute-done((bf16[2,48,768]{2,1,0:T(8,128)(2,1)S(1)}, bf16[2,48,768]{2,1,0:T(8,128)(2,1)S(1)}, u32[]{:S(2)}, u32[]{:S(2)}) %collective-permute-start) | collective-permute-done | bytes 147488 | tf_op jit(solution)/shard_map/ppermute | solution.py:47
  14.9 7.3 %collective-permute-done.1 = bf16[2,48,768]{2,1,0:T(8,128)(2,1)S(1)} collective-permute-done((bf16[2,48,768]{2,1,0:T(8,128)(2,1)S(1)}, bf16[2,48,768]{2,1,0:T(8,128)(2,1)S(1)}, u32[]{:S(2)}, u32[]{:S(2)}) %collective-permute-start.1) | collective-permute-done | bytes 147488 | tf_op jit(solution)/shard_map/ppermute | solution.py:39
  22.3 6.3 %collective-permute-start.3 = (bf16[2,48,768]{2,1,0:T(8,128)(2,1)S(1)}, bf16[2,48,768]{2,1,0:T(8,128)(2,1)S(1)}, u32[]{:S(2)}, u32[]{:S(2)}) collective-permute-start(bf16[2,48,768]{2,1,0:T(8,128)(2,1)S(1)} %get-tuple-element.57), channel_id=1, source_target_pairs={{0,0},{1,1},{2,8},{3,9},{4,16},{5,17},{6,24},{7,25},{8,2},{9,3},{1... | collective-permute-start | bytes 442376 | tf_op jit(solution)/shard_map/ppermute | solution.py:47
  28.6 4.1 collective-permute-done.3
  32.9 1.6 collective-permute-start.4
  36.6 3.9 collective-permute-done.5
  41.3 5.1 collective-permute-done.4
  46.7 7.4 %convolution_bitcast_fusion.2 = f32[1,192,3072]{2,1,0:T(8,128)S(1)} fusion(bf16[3072,1536]{1,0:T(8,128)(2,1)} %param.6, bf16[2,192,1536]{2,1,0:T(8,128)(2,1)S(1)} %maximum_select_fusion.panel), kind=kOutput, calls=%fused_computation.8 | convolution fusion | flops 1811939328 | bytes 12386304 | tf_op jit(solution)/shard_map/dot_general | solution.py:25
  54.1 2.0 convolution_bitcast_fusion.3
  57.9 2.6 collective-permute-start.6
  60.5 2.5 collective-permute-start.7
  63.0 3.6 collective-permute-start.10
  66.6 4.2 collective-permute-done.7
  72.3 1.6 collective-permute-start.9
  75.5 3.8 collective-permute-start.11
  80.0 3.0 collective-permute-done.11
  84.2 3.2 collective-permute-done.9
  87.7 7.3 %convolution_bitcast_fusion = f32[1,192,3072]{2,1,0:T(8,128)S(1)} fusion(bf16[3072,1536]{1,0:T(8,128)(2,1)} %param.6, bf16[2,192,1536]{2,1,0:T(8,128)(2,1)S(1)} %maximum_select_fusion.1.panel), kind=kOutput, calls=%fused_computation.6 | convolution fusion | flops 1811939328 | bytes 12386304 | tf_op jit(solution)/shard_map/dot_general | solution.py:25
  95.1 2.0 convolution_bitcast_fusion.1
  97.4 5.6 %collective-permute-done.8 = bf16[2,96,3072]{2,1,0:T(8,128)(2,1)} collective-permute-done((bf16[2,96,3072]{2,1,0:T(8,128)(2,1)S(1)}, bf16[2,96,3072]{2,1,0:T(8,128)(2,1)}, u32[]{:S(2)}, u32[]{:S(2)}) %collective-permute-start.8) | collective-permute-done | bytes 1179680 | tf_op jit(solution)/shard_map/ppermute | solution.py:39
  103.0 1.9 convert_add_fusion.1
  109.2 9.1 %collective-permute-done.14 = bf16[2,128,768]{2,1,0:T(8,128)(2,1)S(1)} collective-permute-done((bf16[2,128,768]{2,1,0:T(8,128)(2,1)S(1)}, bf16[2,128,768]{2,1,0:T(8,128)(2,1)S(1)}, u32[]{:S(2)}, u32[]{:S(2)}) %collective-permute-start.14) | collective-permute-done | bytes 393248 | tf_op jit(solution)/shard_map/ppermute | solution.py:39
  118.5 3.2 convolution_bitcast_fusion.4
  121.7 1.6 convolution_bitcast_fusion.5
  124.8 2.8 pad_maximum_fusion.2.full
  127.6 4.8 convolution_bitcast_fusion.8
  132.4 3.8 convolution_bitcast_fusion.9
  138.3 2.2 fusion.45
  140.5 108.3 %shard_map.75 = (bf16[512,1536]{1,0:T(8,128)(2,1)}, bf16[512,1536]{1,0:T(8,128)(2,1)}, bf16[512,3072]{1,0:T(8,128)(2,1)}, bf16[512,3072]{1,0:T(8,128)(2,1)}) custom-call(bf16[2,192,3072]{2,1,0:T(8,128)(2,1)} %pad_maximum_fusion.2.full, bf16[2,192,1536]{2,1,0:T(8,128)(2,1)} %copy-done.16), custom_call_target="tpu_custom_call" | custom-call | bytes 4718592 | tf_op jit(solution)/shard_map/pallas_call | solution.py:67
  248.9 2.1 convert_add_fusion
  254.1 14.6 %collective-permute-done.16 = bf16[2,192,768]{2,1,0:T(8,128)(2,1)} collective-permute-done((bf16[2,192,768]{2,1,0:T(8,128)(2,1)}, bf16[2,192,768]{2,1,0:T(8,128)(2,1)}, u32[]{:S(2)}, u32[]{:S(2)}) %collective-permute-start.16) | collective-permute-done | bytes 589856 | tf_op jit(solution)/shard_map/ppermute | solution.py:39
  271.2 1.6 collective-permute-start.19
  274.2 7.8 %convolution_bitcast_fusion.6 = f32[1,192,1536]{2,1,0:T(8,128)S(1)} fusion(bf16[1536,3072]{1,0:T(8,128)(2,1)} %param.5, bf16[2,192,3072]{2,1,0:T(8,128)(2,1)S(1)} %pad_maximum_fusion.3.full), kind=kOutput, calls=%fused_computation.22 | convolution fusion | flops 1811939328 | bytes 11796480 | tf_op jit(solution)/shard_map/dot_general | solution.py:25
  282.0 2.0 convolution_bitcast_fusion.7
  285.8 108.3 %shard_map.76 = (bf16[512,1536]{1,0:T(8,128)(2,1)}, bf16[512,1536]{1,0:T(8,128)(2,1)}, bf16[512,3072]{1,0:T(8,128)(2,1)}, bf16[512,3072]{1,0:T(8,128)(2,1)}) custom-call(bf16[2,192,3072]{2,1,0:T(8,128)(2,1)} %copy-done.13, bf16[2,192,1536]{2,1,0:T(8,128)(2,1)} %copy-done.15, ...), custom_call_target="tpu_custom_call", output_to_operand_aliasing={{0}: (2, {}), {1}: (3, {}), {2}: (4, {}), {3}: (5, {})} | custom-call | bytes 4718592 | tf_op jit(solution)/shard_map/pallas_call | solution.py:67
  396.4 1.6 convert_add_fusion.2
  402.9 6.9 %collective-permute-done.21 = bf16[2,48,768]{2,1,0:T(8,128)(2,1)S(1)} collective-permute-done((bf16[2,48,768]{2,1,0:T(8,128)(2,1)S(1)}, bf16[2,48,768]{2,1,0:T(8,128)(2,1)S(1)}, u32[]{:S(2)}, u32[]{:S(2)}) %collective-permute-start.21) | collective-permute-done | bytes 147488 | tf_op jit(solution)/shard_map/ppermute | solution.py:39
  409.8 1.6 fusion.40
  411.4 2.2 collective-permute-start.24
  414.9 7.5 %convolution_bitcast_fusion.10 = f32[1,128,1536]{2,1,0:T(8,128)S(1)} fusion(bf16[1536,3072]{1,0:T(8,128)(2,1)} %param.5, bf16[2,128,3072]{2,1,0:T(8,128)(2,1)S(1)} %pad_maximum_fusion.5.full), kind=kOutput, calls=%fused_computation.26 | convolution fusion | flops 1207959552 | bytes 11010048 | tf_op jit(solution)/shard_map/dot_general | solution.py:25
  425.3 72.6 %shard_map.77 = (bf16[512,1536]{1,0:T(8,128)(2,1)}, bf16[512,1536]{1,0:T(8,128)(2,1)}, bf16[512,3072]{1,0:T(8,128)(2,1)}, bf16[512,3072]{1,0:T(8,128)(2,1)}) custom-call(bf16[2,128,3072]{2,1,0:T(8,128)(2,1)} %copy-done.11, bf16[2,128,1536]{2,1,0:T(8,128)(2,1)} %copy-done.14, ...), custom_call_target="tpu_custom_call", output_to_operand_aliasing={{0}: (2, {}), {1}: (3, {}), {2}: (4, {}), {3}: (5, {})} | custom-call | bytes 3145728 | tf_op jit(solution)/shard_map/pallas_call | solution.py:67
  499.4 9.5 %convolution_convert_fusion.1 = bf16[1536,3072]{1,0:T(8,128)(2,1)} fusion(bf16[512,1536]{1,0:T(8,128)(2,1)S(1)} %copy-done.19, bf16[512,3072]{1,0:T(8,128)(2,1)} %get-tuple-element.97), kind=kOutput, calls=%fused_computation.1 | convolution fusion | flops 4836556800 | bytes 14155776 | tf_op jit(solution)/shard_map/dot_general | solution.py:25
  510.0 5.8 %collective-permute-start.31 = (bf16[2,48,768]{2,1,0:T(8,128)(2,1)S(1)}, bf16[2,48,768]{2,1,0:T(8,128)(2,1)S(1)}, u32[]{:S(2)}, u32[]{:S(2)}) collective-permute-start(bf16[2,48,768]{2,1,0:T(8,128)(2,1)S(1)} %fusion.39), channel_id=1, source_target_pairs={{0,0},{1,1},{2,8},{3,9},{4,16},{5,17},{6,24},{7,25},{8,2},{9,3},{1... | collective-permute-start | bytes 442376 | tf_op jit(solution)/shard_map/ppermute | solution.py:47
  516.5 3.0 collective-permute-start.30
  519.5 7.5 %convolution_convert_fusion = bf16[3072,1536]{1,0:T(8,128)(2,1)} fusion(bf16[512,3072]{1,0:T(8,128)(2,1)S(1)} %copy-done.12, bf16[512,1536]{1,0:T(8,128)(2,1)S(1)} %copy-done.20), kind=kOutput, calls=%fused_computation | convolution fusion | flops 4836556800 | bytes 14155776 | tf_op jit(solution)/shard_map/dot_general | solution.py:25
  527.0 4.2 collective-permute-start.32
  532.3 5.4 collective-permute-done.32
  (191 shorter events, 44.4 us)
Async XLA Ops:
  0.6 34.7 %copy-start.32 = (bf16[128,768]{1,0:T(8,128)(2,1)S(1)}, bf16[128,768]{1,0:T(8,128)(2,1)}, u32[]{:S(2)}) copy-start(bf16[128,768]{1,0:T(8,128)(2,1)} %param.4) | copy-start | bytes 589828
  0.6 34.7 %copy-start.33 = (bf16[128,768]{1,0:T(8,128)(2,1)S(1)}, bf16[128,768]{1,0:T(8,128)(2,1)}, u32[]{:S(2)}) copy-start(bf16[128,768]{1,0:T(8,128)(2,1)} %param.7) | copy-start | bytes 589828
  1.7 13.1 %collective-permute-start = (bf16[2,48,768]{2,1,0:T(8,128)(2,1)S(1)}, bf16[2,48,768]{2,1,0:T(8,128)(2,1)S(1)}, u32[]{:S(2)}, u32[]{:S(2)}) collective-permute-start(bf16[2,48,768]{2,1,0:T(8,128)(2,1)S(1)} %get-tuple-element.117), channel_id=1, source_target_pairs={{0,0},{1,1},{2,8},{3,9},{4,16},{5,17},{6,24},{7,25},{8,2},{9,3},{1... | collective-permute-start | bytes 442376 | tf_op jit(solution)/shard_map/ppermute | solution.py:47
  14.8 7.4 %collective-permute-start.1 = (bf16[2,48,768]{2,1,0:T(8,128)(2,1)S(1)}, bf16[2,48,768]{2,1,0:T(8,128)(2,1)S(1)}, u32[]{:S(2)}, u32[]{:S(2)}) collective-permute-start(bf16[2,48,768]{2,1,0:T(8,128)(2,1)S(1)} %collective-permute-done), channel_id=1, source_target_pairs={{0,4},{1,5},{2,6},{3,7},{4,0},{5,1},{6,2},{7,3},{8,12},{9,13},{10,... | collective-permute-start | bytes 442376 | tf_op jit(solution)/shard_map/ppermute | solution.py:39
  22.2 10.5 %collective-permute-start.2 = (bf16[2,96,768]{2,1,0:T(8,128)(2,1)S(1)}, bf16[2,96,768]{2,1,0:T(8,128)(2,1)S(1)}, u32[]{:S(2)}, u32[]{:S(2)}) collective-permute-start(bf16[2,96,768]{2,1,0:T(8,128)(2,1)S(1)} %constant_dynamic-update-slice_fusion), channel_id=1, source_target_pairs={{0,2},{1,3},{2,0},{3,1},{4,6},{5,7},{6,4},{7,5},{8,10},{9,11},{10,... | collective-permute-start | bytes 884744 | tf_op jit(solution)/shard_map/ppermute | solution.py:39
  22.3 10.4 %collective-permute-start.3 = (bf16[2,48,768]{2,1,0:T(8,128)(2,1)S(1)}, bf16[2,48,768]{2,1,0:T(8,128)(2,1)S(1)}, u32[]{:S(2)}, u32[]{:S(2)}) collective-permute-start(bf16[2,48,768]{2,1,0:T(8,128)(2,1)S(1)} %get-tuple-element.57), channel_id=1, source_target_pairs={{0,0},{1,1},{2,8},{3,9},{4,16},{5,17},{6,24},{7,25},{8,2},{9,3},{1... | collective-permute-start | bytes 442376 | tf_op jit(solution)/shard_map/ppermute | solution.py:47
  32.9 13.5 %collective-permute-start.4 = (bf16[2,192,768]{2,1,0:T(8,128)(2,1)S(1)}, bf16[2,192,768]{2,1,0:T(8,128)(2,1)S(1)}, u32[]{:S(2)}, u32[]{:S(2)}) collective-permute-start(bf16[2,192,768]{2,1,0:T(8,128)(2,1)S(1)} %maximum_select_fusion.3), channel_id=1, source_target_pairs={{0,1},{1,0},{2,3},{3,2},{4,5},{5,4},{6,7},{7,6},{8,9},{9,8},{10,11... | collective-permute-start | bytes 1769480 | tf_op jit(solution)/shard_map/ppermute | solution.py:39
  34.5 6.0 %collective-permute-start.5 = (bf16[2,48,768]{2,1,0:T(8,128)(2,1)S(1)}, bf16[2,48,768]{2,1,0:T(8,128)(2,1)S(1)}, u32[]{:S(2)}, u32[]{:S(2)}) collective-permute-start(bf16[2,48,768]{2,1,0:T(8,128)(2,1)S(1)} %collective-permute-done.3), channel_id=1, source_target_pairs={{0,4},{1,5},{2,6},{3,7},{4,0},{5,1},{6,2},{7,3},{8,12},{9,13},{10,... | collective-permute-start | bytes 442376 | tf_op jit(solution)/shard_map/ppermute | solution.py:39
  54.1 19.9 %copy-start.1 = (f32[1,192,3072]{2,1,0:T(8,128)}, f32[1,192,3072]{2,1,0:T(8,128)S(1)}, u32[]{:S(2)}) copy-start(f32[1,192,3072]{2,1,0:T(8,128)S(1)} %convolution_bitcast_fusion.2) | copy-start | bytes 7077892
  57.9 16.0 %collective-permute-start.6 = (bf16[2,96,3072]{2,1,0:T(8,128)(2,1)}, bf16[2,96,3072]{2,1,0:T(8,128)(2,1)S(1)}, u32[]{:S(2)}, u32[]{:S(2)}) collective-permute-start(bf16[2,96,3072]{2,1,0:T(8,128)(2,1)} %fusion.5), channel_id=1, source_target_pairs={{0,8},{8,0},{16,24},{24,16},{1,9},{9,1},{17,25},{25,17},{2,10},{10... | collective-permute-start | bytes 3538952 | tf_op jit(solution)/shard_map/ppermute | solution.py:39
  60.5 10.3 %collective-permute-start.7 = (bf16[2,96,768]{2,1,0:T(8,128)(2,1)}, bf16[2,96,768]{2,1,0:T(8,128)(2,1)}, u32[]{:S(2)}, u32[]{:S(2)}) collective-permute-start(bf16[2,96,768]{2,1,0:T(8,128)(2,1)} %constant_dynamic-update-slice_fusion.2), channel_id=1, source_target_pairs={{0,2},{1,3},{2,0},{3,1},{4,6},{5,7},{6,4},{7,5},{8,10},{9,11},{10,... | collective-permute-start | bytes 884744 | tf_op jit(solution)/shard_map/ppermute | solution.py:39
  63.0 12.6 %collective-permute-start.10 = (bf16[2,32,768]{2,1,0:T(8,128)(2,1)}, bf16[2,32,768]{2,1,0:T(8,128)(2,1)S(1)}, u32[]{:S(2)}, u32[]{:S(2)}) collective-permute-start(bf16[2,32,768]{2,1,0:T(8,128)(2,1)} %pad_maximum_fusion.9), channel_id=1, source_target_pairs={{0,0},{1,1},{2,8},{3,9},{4,16},{5,17},{6,24},{7,25},{8,2},{9,3},{1... | collective-permute-start | bytes 294920 | tf_op jit(solution)/shard_map/ppermute | solution.py:47
  70.8 24.3 %slice-start.9 = ((s8[9437184]{0:T(1024)(128)(4,1)}), s8[4194304]{0:T(1024)(128)(4,1)S(1)}, s32[]{:S(2)}) async-start(s8[9437184]{0:T(1024)(128)(4,1)} %bitcast.88), calls=%async_computation.9 | async-start | bytes 8388608
  72.3 22.8 %slice-start.10 = ((s8[9437184]{0:T(1024)(128)(4,1)}), s8[4194304]{0:T(1024)(128)(4,1)S(1)}, s32[]{:S(2)}) async-start(s8[9437184]{0:T(1024)(128)(4,1)} %bitcast.88), calls=%async_computation.10 | async-start | bytes 8388608
  72.3 15.1 %collective-permute-start.9 = (bf16[2,192,768]{2,1,0:T(8,128)(2,1)S(1)}, bf16[2,192,768]{2,1,0:T(8,128)(2,1)S(1)}, u32[]{:S(2)}, u32[]{:S(2)}) collective-permute-start(bf16[2,192,768]{2,1,0:T(8,128)(2,1)S(1)} %maximum_select_fusion.4), channel_id=1, source_target_pairs={{0,1},{1,0},{2,3},{3,2},{4,5},{5,4},{6,7},{7,6},{8,9},{9,8},{10,11... | collective-permute-start | bytes 1769480 | tf_op jit(solution)/shard_map/ppermute | solution.py:39
  75.5 27.6 %collective-permute-start.8 = (bf16[2,96,3072]{2,1,0:T(8,128)(2,1)S(1)}, bf16[2,96,3072]{2,1,0:T(8,128)(2,1)}, u32[]{:S(2)}, u32[]{:S(2)}) collective-permute-start(bf16[2,96,3072]{2,1,0:T(8,128)(2,1)S(1)} %fusion.46), channel_id=1, source_target_pairs={{0,16},{8,24},{16,0},{24,8},{1,17},{9,25},{17,1},{25,9},{2,18},{10... | collective-permute-start | bytes 3538952 | tf_op jit(solution)/shard_map/ppermute | solution.py:39
  75.5 7.5 %collective-permute-start.11 = (bf16[2,32,768]{2,1,0:T(8,128)(2,1)S(1)}, bf16[2,32,768]{2,1,0:T(8,128)(2,1)S(1)}, u32[]{:S(2)}, u32[]{:S(2)}) collective-permute-start(bf16[2,32,768]{2,1,0:T(8,128)(2,1)S(1)} %collective-permute-done.10), channel_id=1, source_target_pairs={{0,4},{1,5},{2,6},{3,7},{4,0},{5,1},{6,2},{7,3},{8,12},{9,13},{10,... | collective-permute-start | bytes 294920 | tf_op jit(solution)/shard_map/ppermute | solution.py:39
  83.7 22.9 %collective-permute-start.13 = (bf16[2,64,768]{2,1,0:T(8,128)(2,1)}, bf16[2,64,768]{2,1,0:T(8,128)(2,1)S(1)}, u32[]{:S(2)}, u32[]{:S(2)}) collective-permute-start(bf16[2,64,768]{2,1,0:T(8,128)(2,1)} %constant_dynamic-update-slice_fusion.4), channel_id=1, source_target_pairs={{0,2},{1,3},{2,0},{3,1},{4,6},{5,7},{6,4},{7,5},{8,10},{9,11},{10,... | collective-permute-start | bytes 589832 | tf_op jit(solution)/shard_map/ppermute | solution.py:39
  97.3 10.1 %collective-permute-start.15 = (bf16[2,96,3072]{2,1,0:T(8,128)(2,1)S(1)}, bf16[2,96,3072]{2,1,0:T(8,128)(2,1)S(1)}, u32[]{:S(2)}, u32[]{:S(2)}) collective-permute-start(bf16[2,96,3072]{2,1,0:T(8,128)(2,1)S(1)} %fusion.1), channel_id=1, source_target_pairs={{0,8},{8,0},{16,24},{24,16},{1,9},{9,1},{17,25},{25,17},{2,10},{10... | collective-permute-start | bytes 3538952 | tf_op jit(solution)/shard_map/ppermute | solution.py:39
  103.0 15.5 %slice-start = ((s8[9437184]{0:T(1024)(128)(4,1)}), s8[4194304]{0:T(1024)(128)(4,1)S(1)}, s32[]{:S(2)}) async-start(s8[9437184]{0:T(1024)(128)(4,1)} %bitcast.82), calls=%async_computation | async-start | bytes 8388608
  103.0 15.5 %slice-start.1 = ((s8[9437184]{0:T(1024)(128)(4,1)}), s8[4194304]{0:T(1024)(128)(4,1)S(1)}, s32[]{:S(2)}) async-start(s8[9437184]{0:T(1024)(128)(4,1)} %bitcast.82), calls=%async_computation.1 | async-start | bytes 8388608
  106.6 18.2 %collective-permute-start.12 = (bf16[2,96,3072]{2,1,0:T(8,128)(2,1)}, bf16[2,96,3072]{2,1,0:T(8,128)(2,1)}, u32[]{:S(2)}, u32[]{:S(2)}) collective-permute-start(bf16[2,96,3072]{2,1,0:T(8,128)(2,1)} %pad_maximum_fusion.6), channel_id=1, source_target_pairs={{0,8},{8,0},{16,24},{24,16},{1,9},{9,1},{17,25},{25,17},{2,10},{10... | collective-permute-start | bytes 3538952 | tf_op jit(solution)/shard_map/ppermute | solution.py:39
  106.7 11.6 %collective-permute-start.14 = (bf16[2,128,768]{2,1,0:T(8,128)(2,1)S(1)}, bf16[2,128,768]{2,1,0:T(8,128)(2,1)S(1)}, u32[]{:S(2)}, u32[]{:S(2)}) collective-permute-start(bf16[2,128,768]{2,1,0:T(8,128)(2,1)S(1)} %maximum_select_fusion.5), channel_id=1, source_target_pairs={{0,1},{1,0},{2,3},{3,2},{4,5},{5,4},{6,7},{7,6},{8,9},{9,8},{10,11... | collective-permute-start | bytes 1179656 | tf_op jit(solution)/shard_map/ppermute | solution.py:39
  108.9 140.0 %collective-permute-start.17 = (bf16[2,96,3072]{2,1,0:T(8,128)(2,1)}, bf16[2,96,3072]{2,1,0:T(8,128)(2,1)}, u32[]{:S(2)}, u32[]{:S(2)}) collective-permute-start(bf16[2,96,3072]{2,1,0:T(8,128)(2,1)} %fusion.44), channel_id=1, source_target_pairs={{0,16},{8,24},{16,0},{24,8},{1,17},{9,25},{17,1},{25,9},{2,18},{10... | collective-permute-start | bytes 3538952 | tf_op jit(solution)/shard_map/ppermute | solution.py:39
  121.7 15.5 %copy-start.3 = (f32[1,128,3072]{2,1,0:T(8,128)}, f32[1,128,3072]{2,1,0:T(8,128)S(1)}, u32[]{:S(2)}) copy-start(f32[1,128,3072]{2,1,0:T(8,128)S(1)} %convolution_bitcast_fusion.4) | copy-start | bytes 4718596
  124.8 12.4 %collective-permute-start.18 = (bf16[2,64,3072]{2,1,0:T(8,128)(2,1)}, bf16[2,64,3072]{2,1,0:T(8,128)(2,1)}, u32[]{:S(2)}, u32[]{:S(2)}) collective-permute-start(bf16[2,64,3072]{2,1,0:T(8,128)(2,1)} %fusion.7), channel_id=1, source_target_pairs={{0,8},{8,0},{16,24},{24,16},{1,9},{9,1},{17,25},{25,17},{2,10},{10... | collective-permute-start | bytes 2359304 | tf_op jit(solution)/shard_map/ppermute | solution.py:39
  140.5 108.4 %copy-start.22 = (bf16[2,96,3072]{2,1,0:T(8,128)(2,1)S(1)}, bf16[2,96,3072]{2,1,0:T(8,128)(2,1)}, u32[]{:S(2)}) copy-start(bf16[2,96,3072]{2,1,0:T(8,128)(2,1)} %copy-done.21) | copy-start | bytes 3538948
  251.5 17.2 %copy-start.24 = (f32[1,192,1536]{2,1,0:T(8,128)S(1)}, f32[1,192,1536]{2,1,0:T(8,128)}, u32[]{:S(2)}) copy-start(f32[1,192,1536]{2,1,0:T(8,128)} %copy-done.23) | copy-start | bytes 3538948
  251.5 17.2 %copy-start.26 = (f32[1,192,1536]{2,1,0:T(8,128)S(1)}, f32[1,192,1536]{2,1,0:T(8,128)}, u32[]{:S(2)}) copy-start(f32[1,192,1536]{2,1,0:T(8,128)} %copy-done.25) | copy-start | bytes 3538948
  252.6 20.1 %collective-permute-start.20 = (bf16[2,96,3072]{2,1,0:T(8,128)(2,1)}, bf16[2,96,3072]{2,1,0:T(8,128)(2,1)}, u32[]{:S(2)}, u32[]{:S(2)}) collective-permute-start(bf16[2,96,3072]{2,1,0:T(8,128)(2,1)} %pad_maximum_fusion.7), channel_id=1, source_target_pairs={{0,8},{8,0},{16,24},{24,16},{1,9},{9,1},{17,25},{25,17},{2,10},{10... | collective-permute-start | bytes 3538952 | tf_op jit(solution)/shard_map/ppermute | solution.py:39
  253.2 15.6 %collective-permute-start.16 = (bf16[2,192,768]{2,1,0:T(8,128)(2,1)}, bf16[2,192,768]{2,1,0:T(8,128)(2,1)}, u32[]{:S(2)}, u32[]{:S(2)}) collective-permute-start(bf16[2,192,768]{2,1,0:T(8,128)(2,1)} %fusion.26), channel_id=1, source_target_pairs={{0,1},{1,0},{2,3},{3,2},{4,5},{5,4},{6,7},{7,6},{8,9},{9,8},{10,11... | collective-permute-start | bytes 1769480 | tf_op jit(solution)/shard_map/ppermute | solution.py:39
  253.9 142.5 %collective-permute-start.23 = (bf16[2,64,3072]{2,1,0:T(8,128)(2,1)}, bf16[2,64,3072]{2,1,0:T(8,128)(2,1)}, u32[]{:S(2)}, u32[]{:S(2)}) collective-permute-start(bf16[2,64,3072]{2,1,0:T(8,128)(2,1)} %fusion.45), channel_id=1, source_target_pairs={{0,16},{8,24},{16,0},{24,8},{1,17},{9,25},{17,1},{25,9},{2,18},{10... | collective-permute-start | bytes 2359304 | tf_op jit(solution)/shard_map/ppermute | solution.py:39
  271.2 123.0 %collective-permute-start.19 = (bf16[2,96,768]{2,1,0:T(8,128)(2,1)S(1)}, bf16[2,96,768]{2,1,0:T(8,128)(2,1)S(1)}, u32[]{:S(2)}, u32[]{:S(2)}) collective-permute-start(bf16[2,96,768]{2,1,0:T(8,128)(2,1)S(1)} %dynamic-slice_convert_fusion.1), channel_id=1, source_target_pairs={{0,2},{1,3},{2,0},{3,1},{4,6},{5,7},{6,4},{7,5},{8,10},{9,11},{10,... | collective-permute-start | bytes 884744 | tf_op jit(solution)/shard_map/ppermute | solution.py:39
  285.1 114.3 %collective-permute-start.22 = (bf16[2,192,768]{2,1,0:T(8,128)(2,1)}, bf16[2,192,768]{2,1,0:T(8,128)(2,1)}, u32[]{:S(2)}, u32[]{:S(2)}) collective-permute-start(bf16[2,192,768]{2,1,0:T(8,128)(2,1)} %fusion.24), channel_id=1, source_target_pairs={{0,1},{1,0},{2,3},{3,2},{4,5},{5,4},{6,7},{7,6},{8,9},{9,8},{10,11... | collective-permute-start | bytes 1769480 | tf_op jit(solution)/shard_map/ppermute | solution.py:39
  285.8 110.5 %copy-start.7 = (f32[1,128,3072]{2,1,0:T(8,128)S(1)}, f32[1,128,3072]{2,1,0:T(8,128)}, u32[]{:S(2)}) copy-start(f32[1,128,3072]{2,1,0:T(8,128)} %copy-done.5) | copy-start | bytes 4718596
  398.0 24.4 %slice-start.6 = ((s8[9437184]{0:T(1024)(128)(4,1)}), s8[1048576]{0:T(1024)(128)(4,1)S(1)}, s32[]{:S(2)}) async-start(s8[9437184]{0:T(1024)(128)(4,1)} %bitcast.86), calls=%async_computation.6 | async-start | bytes 2097152
  399.4 14.3 %collective-permute-start.25 = (bf16[2,64,3072]{2,1,0:T(8,128)(2,1)}, bf16[2,64,3072]{2,1,0:T(8,128)(2,1)}, u32[]{:S(2)}, u32[]{:S(2)}) collective-permute-start(bf16[2,64,3072]{2,1,0:T(8,128)(2,1)} %pad_maximum_fusion.8), channel_id=1, source_target_pairs={{0,8},{8,0},{16,24},{24,16},{1,9},{9,1},{17,25},{25,17},{2,10},{10... | collective-permute-start | bytes 2359304 | tf_op jit(solution)/shard_map/ppermute | solution.py:39
  399.4 23.1 %slice-start.7 = ((s8[9437184]{0:T(1024)(128)(4,1)}), s8[4194304]{0:T(1024)(128)(4,1)S(1)}, s32[]{:S(2)}) async-start(s8[9437184]{0:T(1024)(128)(4,1)} %bitcast.86), calls=%async_computation.7 | async-start | bytes 8388608
  399.4 10.4 %collective-permute-start.21 = (bf16[2,48,768]{2,1,0:T(8,128)(2,1)S(1)}, bf16[2,48,768]{2,1,0:T(8,128)(2,1)S(1)}, u32[]{:S(2)}, u32[]{:S(2)}) collective-permute-start(bf16[2,48,768]{2,1,0:T(8,128)(2,1)S(1)} %copy-done.36), channel_id=1, source_target_pairs={{0,4},{1,5},{2,6},{3,7},{4,0},{5,1},{6,2},{7,3},{8,12},{9,13},{10,... | collective-permute-start | bytes 442376 | tf_op jit(solution)/shard_map/ppermute | solution.py:39
  401.8 96.2 %collective-permute-start.27 = (bf16[2,96,768]{2,1,0:T(8,128)(2,1)}, bf16[2,96,768]{2,1,0:T(8,128)(2,1)}, u32[]{:S(2)}, u32[]{:S(2)}) collective-permute-start(bf16[2,96,768]{2,1,0:T(8,128)(2,1)} %dynamic-slice_convert_fusion), channel_id=1, source_target_pairs={{0,2},{1,3},{2,0},{3,1},{4,6},{5,7},{6,4},{7,5},{8,10},{9,11},{10,... | collective-permute-start | bytes 884744 | tf_op jit(solution)/shard_map/ppermute | solution.py:39
  411.4 119.8 %collective-permute-start.24 = (bf16[2,48,768]{2,1,0:T(8,128)(2,1)}, bf16[2,48,768]{2,1,0:T(8,128)(2,1)}, u32[]{:S(2)}, u32[]{:S(2)}) collective-permute-start(bf16[2,48,768]{2,1,0:T(8,128)(2,1)} %fusion.40), channel_id=1, source_target_pairs={{0,0},{1,1},{2,8},{3,9},{4,16},{5,17},{6,24},{7,25},{8,2},{9,3},{1... | collective-permute-start | bytes 442376 | tf_op jit(solution)/shard_map/ppermute | solution.py:47
  424.0 84.9 %collective-permute-start.26 = (bf16[2,128,768]{2,1,0:T(8,128)(2,1)S(1)}, bf16[2,128,768]{2,1,0:T(8,128)(2,1)S(1)}, u32[]{:S(2)}, u32[]{:S(2)}) collective-permute-start(bf16[2,128,768]{2,1,0:T(8,128)(2,1)S(1)} %fusion.36), channel_id=1, source_target_pairs={{0,1},{1,0},{2,3},{3,2},{4,5},{5,4},{6,7},{7,6},{8,9},{9,8},{10,11... | collective-permute-start | bytes 1179656 | tf_op jit(solution)/shard_map/ppermute | solution.py:39
  425.3 72.6 %copy-start.29 = (f32[2,192,768]{2,1,0:T(8,128)S(1)}, f32[2,192,768]{2,1,0:T(8,128)}, u32[]{:S(2)}) copy-start(f32[2,192,768]{2,1,0:T(8,128)} %copy-done.28) | copy-start | bytes 3538948
  499.1 10.8 %collective-permute-start.29 = (bf16[2,48,768]{2,1,0:T(8,128)(2,1)S(1)}, bf16[2,48,768]{2,1,0:T(8,128)(2,1)S(1)}, u32[]{:S(2)}, u32[]{:S(2)}) collective-permute-start(bf16[2,48,768]{2,1,0:T(8,128)(2,1)S(1)} %slice.288), channel_id=1, source_target_pairs={{0,4},{1,5},{2,6},{3,7},{4,0},{5,1},{6,2},{7,3},{8,12},{9,13},{10,... | collective-permute-start | bytes 442376 | tf_op jit(solution)/shard_map/ppermute | solution.py:39
  509.1 7.4 %collective-permute-start.28 = (bf16[2,64,768]{2,1,0:T(8,128)(2,1)S(1)}, bf16[2,64,768]{2,1,0:T(8,128)(2,1)S(1)}, u32[]{:S(2)}, u32[]{:S(2)}) collective-permute-start(bf16[2,64,768]{2,1,0:T(8,128)(2,1)S(1)} %dynamic-slice_convert_fusion.2), channel_id=1, source_target_pairs={{0,2},{1,3},{2,0},{3,1},{4,6},{5,7},{6,4},{7,5},{8,10},{9,11},{10,... | collective-permute-start | bytes 589832 | tf_op jit(solution)/shard_map/ppermute | solution.py:39
  510.0 22.2 %collective-permute-start.31 = (bf16[2,48,768]{2,1,0:T(8,128)(2,1)S(1)}, bf16[2,48,768]{2,1,0:T(8,128)(2,1)S(1)}, u32[]{:S(2)}, u32[]{:S(2)}) collective-permute-start(bf16[2,48,768]{2,1,0:T(8,128)(2,1)S(1)} %fusion.39), channel_id=1, source_target_pairs={{0,0},{1,1},{2,8},{3,9},{4,16},{5,17},{6,24},{7,25},{8,2},{9,3},{1... | collective-permute-start | bytes 442376 | tf_op jit(solution)/shard_map/ppermute | solution.py:47
  516.5 10.5 %collective-permute-start.30 = (bf16[2,32,768]{2,1,0:T(8,128)(2,1)S(1)}, bf16[2,32,768]{2,1,0:T(8,128)(2,1)S(1)}, u32[]{:S(2)}, u32[]{:S(2)}) collective-permute-start(bf16[2,32,768]{2,1,0:T(8,128)(2,1)S(1)} %slice.290), channel_id=1, source_target_pairs={{0,4},{1,5},{2,6},{3,7},{4,0},{5,1},{6,2},{7,3},{8,12},{9,13},{10,... | collective-permute-start | bytes 294920 | tf_op jit(solution)/shard_map/ppermute | solution.py:39
  527.0 10.6 %collective-permute-start.32 = (bf16[2,32,768]{2,1,0:T(8,128)(2,1)S(1)}, bf16[2,32,768]{2,1,0:T(8,128)(2,1)S(1)}, u32[]{:S(2)}, u32[]{:S(2)}) collective-permute-start(bf16[2,32,768]{2,1,0:T(8,128)(2,1)S(1)} %fusion.41), channel_id=1, source_target_pairs={{0,0},{1,1},{2,8},{3,9},{4,16},{5,17},{6,24},{7,25},{8,2},{9,3},{1... | collective-permute-start | bytes 294920 | tf_op jit(solution)/shard_map/ppermute | solution.py:47
  (34 other events, 206.2 us)
